TPU v7x, 32 devices: a whole 2x2x4 slice. The times are simulated.
32 devices in a mesh: parts: 2 (over y), dp: 4 (over z), mp: 4 (over x, core).
Axes of the slice: x: 2, y: 2, z: 4, core: 2. Of those that a mesh axis runs over, the one named last changes fastest.
Arguments:
- tokens: bfloat16 [192, 4096], P(('parts', 'dp'), 'mp'), parts along dimension 0, may hold values from -6 to 6
- curvature: float32 [192], P('parts'), parts along dimension 0, may hold values from 0.02 to 0.2
- gate_weight: bfloat16 [4096, 16384], P('mp', 'dp'), may hold values from -0.09375 to 0.09375
- up_weight: bfloat16 [4096, 16384], P('mp', 'dp'), may hold values from -0.09375 to 0.09375
- down_weight: bfloat16 [16384, 4096], P('dp', 'mp'), may hold values from -0.046875 to 0.046875
- gate_vector: bfloat16 [8192, 16384], P(('parts', 'mp'), 'dp'), parts along dimension 0, may hold values from -0.09375 to 0.09375
- up_vector: bfloat16 [8192, 16384], P(('parts', 'mp'), 'dp'), parts along dimension 0, may hold values from -0.09375 to 0.09375
- down_vector: bfloat16 [32768, 4096], P(('parts', 'dp'), 'mp'), parts along dimension 0, may hold values from -0.046875 to 0.046875
Outputs:
- fisher_gate: bfloat16 [8192, 16384], P(('parts', 'mp'), 'dp'), parts along dimension 0
- fisher_up: bfloat16 [8192, 16384], P(('parts', 'mp'), 'dp'), parts along dimension 0
- fisher_down: bfloat16 [32768, 4096], P(('parts', 'dp'), 'mp'), parts along dimension 0
There are 2 independent parts, one for each index of `parts`. A program takes and returns all parts, laid end to end along the dimension named above; an argument that names none is the same for every part. Nothing has to cross between parts.
All inputs are finite; a program needn't handle non-finite values.
Results may differ from a plain program's by a relative error of at most 0.025.
Values may be sent and summed in bfloat16 or wider, within the bound.
No kernel may reach another device: no remote copies, remote signals or barrier semaphores. Data moves between devices by JAX's collectives and lax.ppermute only.
A program may use at most 192 MiB of HBM per device.

v0:
```python
import jax
import jax.numpy as jnp
from jax import lax
from jax.sharding import PartitionSpec as P


def forward_terms(gate, up, gate_tan, up_tan):
    logistic = jax.nn.sigmoid(gate)
    swish = gate * logistic
    slope = logistic * (1.0 + gate * (1.0 - logistic))
    hidden = (swish * up).astype(jnp.bfloat16)
    hidden_tan = (slope * gate_tan * up + swish * up_tan).astype(jnp.bfloat16)
    return (swish, slope, hidden, hidden_tan)


def backward_terms(back, up, slope, swish):
    gate_back = (back * up * slope).astype(jnp.bfloat16)
    up_back = (back * swish).astype(jnp.bfloat16)
    return (gate_back, up_back)


def split_four(summed, slab):
    return (
        summed[:, :slab],
        summed[:, slab : 2 * slab],
        summed[:, 2 * slab : 3 * slab],
        summed[:, 3 * slab :],
    )


def per_device(
    tokens, curvature, gate_weight, up_weight, down_weight, gate_vector, up_vector, down_vector
):
    slab = gate_weight.shape[1]
    gathered = lax.all_gather(tokens, "dp", axis=0, tiled=True)
    stacked = jnp.concatenate((gate_weight, up_weight, gate_vector, up_vector), axis=1)
    partials = jnp.dot(gathered, stacked, preferred_element_type=jnp.float32)
    summed = lax.psum(partials.astype(jnp.bfloat16), "mp").astype(jnp.float32)
    gate, up, gate_tan, up_tan = split_four(summed, slab)
    swish, slope, hidden, hidden_tan = forward_terms(gate, up, gate_tan, up_tan)
    out_part = jnp.dot(hidden_tan, down_weight, preferred_element_type=jnp.float32) + jnp.dot(
        hidden, down_vector, preferred_element_type=jnp.float32
    )
    out_tan = lax.psum(out_part.astype(jnp.bfloat16), "dp").astype(jnp.float32)
    weighted = (curvature[:, None] * out_tan).astype(jnp.bfloat16)
    back_part = lax.dot_general(
        weighted, down_weight, (((1,), (1,)), ((), ())), preferred_element_type=jnp.float32
    )
    back = lax.psum(back_part.astype(jnp.bfloat16), "mp").astype(jnp.float32)
    gate_back, up_back = backward_terms(back, up, slope, swish)
    fisher_gate = lax.dot_general(
        gathered, gate_back, (((0,), (0,)), ((), ())), preferred_element_type=jnp.float32
    ).astype(jnp.bfloat16)
    fisher_up = lax.dot_general(
        gathered, up_back, (((0,), (0,)), ((), ())), preferred_element_type=jnp.float32
    ).astype(jnp.bfloat16)
    fisher_down = lax.dot_general(
        hidden, weighted, (((0,), (0,)), ((), ())), preferred_element_type=jnp.float32
    ).astype(jnp.bfloat16)
    return (fisher_gate, fisher_up, fisher_down)


def solution(mesh):
    placed = (
        P(("parts", "dp"), "mp"),
        P("parts"),
        P("mp", "dp"),
        P("mp", "dp"),
        P("dp", "mp"),
        P(("parts", "mp"), "dp"),
        P(("parts", "mp"), "dp"),
        P(("parts", "dp"), "mp"),
    )
    return jax.shard_map(
        per_device,
        mesh=mesh,
        in_specs=placed,
        out_specs=(P(("parts", "mp"), "dp"), P(("parts", "mp"), "dp"), P(("parts", "dp"), "mp")),
        check_vma=False,
    )
```

profile of v0, /device:TPU:0, one launch (start us, length us, event | category | flops | bytes accessed | tf_op | source)
XLA Modules:
  0.0 245.1 jit_solution(16893585439060831138)
XLA Ops:
  7.2 0.0 all-reduce.4.cloned.1.call-start
  7.2 15.7 %all_gather.3 = bf16[96,1024]{1,0:T(8,128)(2,1)S(1)} all-gather(bf16[24,1024]{1,0:T(8,128)(2,1)} %param.8), channel_id=1, replica_groups=mesh['parts'=2,'dp'=4,'mp'=4] {'dp'}, dimensions={0}, use_global_device_ids=true | all-gather | bytes 245760 | tf_op jit(solution)/shard_map/all_gather | solution.py:35
  22.9 17.1 %fusion.11 = bf16[96,16384]{1,0:T(8,128)(2,1)} fusion(bf16[96,1024]{1,0:T(8,128)(2,1)S(1)} %all_gather.3, bf16[1024,4096]{1,0:T(8,128)(2,1)} %param.14, bf16[1024,4096]{1,0:T(8,128)(2,1)} %param.13, bf16[1024,4096]{1,0:T(8,128)(2,1)} %param.11, bf16[1024,4096]{1,0:T(8,128)(2,1)} %param.10), kind=kOutput, calls=%fused_computation.9 | convolution fusion | flops 3357016064 | bytes 36896768 | tf_op jit(solution)/shard_map/dot_general | solution.py:37
  40.0 0.0 all-reduce.4.cloned.1.call-update
  40.0 0.0 all-reduce.6.cloned.1.call-start
  40.1 69.8 %all-reduce.4.cloned.1.call-done = bf16[96,16384]{1,0:T(8,128)(2,1)} async-done(((bf16[96,16384]{1,0:T(8,128)(2,1)}), bf16[96,16384]{1,0:T(8,128)(2,1)}) %all-reduce.4.cloned.1.call-update) | async-done | bytes 3145744 | tf_op jit(solution)/shard_map/psum | solution.py:38
  109.9 2.4 convert_element_type.53
  112.3 0.0 copy-start
  112.3 0.0 slice-start
  112.4 0.4 multiply_convert_fusion
  112.8 0.0 slice-start.1
  112.8 8.0 %fusion.22 = f32[96,1024]{1,0:T(8,128)S(1)} fusion(bf16[4096,1024]{1,0:T(8,128)(2,1)} %param.12, f32[96,16384]{1,0:T(8,128)S(1)} %convert_element_type.53), kind=kOutput, calls=%fused_computation.30 | convolution fusion | flops 810418176 | bytes 15073280 | tf_op jit(solution)/shard_map/dot_general | solution.py:41
  120.8 0.0 copy-done
  120.8 0.0 slice-done
  120.8 0.0 slice-done.1
  120.8 0.0 copy-start.3
  120.8 2.1 fusion.21
  123.0 0.0 all-reduce.6.cloned.1.call-update
  123.0 0.2 all-reduce.8.cloned.1.call-start
  123.2 34.8 %all-reduce.6.cloned.1.call-done = bf16[96,1024]{1,0:T(8,128)(2,1)} async-done(((bf16[96,1024]{1,0:T(8,128)(2,1)}), bf16[96,1024]{1,0:T(8,128)(2,1)}) %all-reduce.6.cloned.1.call-update) | async-done | bytes 196624 | tf_op jit(solution)/shard_map/psum | solution.py:44
  158.1 0.0 copy-done.3
  158.1 0.0 copy-start.2
  158.1 7.1 %convolution_convert_fusion.1 = bf16[96,4096]{1,0:T(8,128)(2,1)} fusion(bf16[4096,1024]{1,0:T(8,128)(2,1)} %param.12, bf16[96,1024]{1,0:T(8,128)(2,1)} %all-reduce.6.cloned.1.call-done, f32[96]{0:T(128)S(1)} %copy-done.3), kind=kOutput, calls=%fused_computation.13 | convolution fusion | flops 805994496 | bytes 9372032 | tf_op jit(solution)/shard_map/dot_general | solution.py:46
  165.2 0.0 all-reduce.8.cloned.1.call-update
  165.2 0.0 copy-done.2
  165.2 5.8 %convolution_convert_fusion = bf16[4096,1024]{1,0:T(8,128)(2,1)} fusion(bf16[96,4096]{1,0:T(8,128)(2,1)S(1)} %multiply_convert_fusion, bf16[96,1024]{1,0:T(8,128)(2,1)S(1)} %copy-done.2, f32[96]{0:T(128)S(1)} %copy-done.3), kind=kOutput, calls=%fused_computation.12 | convolution fusion | flops 809795584 | bytes 9372032 | tf_op jit(solution)/shard_map/dot_general | solution.py:57
  171.0 28.7 %all-reduce.8.cloned.1.call-done = bf16[96,4096]{1,0:T(8,128)(2,1)} async-done(((bf16[96,4096]{1,0:T(8,128)(2,1)}), bf16[96,4096]{1,0:T(8,128)(2,1)}) %all-reduce.8.cloned.1.call-update) | async-done | bytes 786448 | tf_op jit(solution)/shard_map/psum | solution.py:49
  199.7 7.5 %convert_bitcast_fusion = bf16[1024,4096]{0,1:T(8,128)(2,1)} fusion(bf16[96,1024]{1,0:T(8,128)(2,1)S(1)} %all_gather.3, bf16[96,4096]{1,0:T(8,128)(2,1)} %all-reduce.8.cloned.1.call-done, f32[96,16384]{1,0:T(8,128)} %copy-done), kind=kOutput, calls=%fused_computation.10 | convolution fusion | flops 812253184 | bytes 10944512 | tf_op jit(solution)/shard_map/dot_general | solution.py:54
  207.2 12.0 %copy.12 = bf16[1024,4096]{1,0:T(8,128)(2,1)} copy(bf16[1024,4096]{0,1:T(8,128)(2,1)} %convert_bitcast_fusion) | data formatting | bytes 16777216
  219.2 0.0 copy-done.1
  219.2 7.5 %convert_bitcast_fusion.1 = bf16[1024,4096]{0,1:T(8,128)(2,1)} fusion(bf16[96,1024]{1,0:T(8,128)(2,1)S(1)} %all_gather.3, bf16[96,4096]{1,0:T(8,128)(2,1)S(1)} %copy-done.1, f32[96,16384]{1,0:T(8,128)} %copy-done), kind=kOutput, calls=%fused_computation.11 | convolution fusion | flops 813826048 | bytes 12517376 | tf_op jit(solution)/shard_map/dot_general | solution.py:51
  226.7 11.9 %copy.11 = bf16[1024,4096]{1,0:T(8,128)(2,1)} copy(bf16[1024,4096]{0,1:T(8,128)(2,1)} %convert_bitcast_fusion.1) | data formatting | bytes 16777216
  (2 shorter events, 0.0 us)
Async XLA Ops:
  7.2 102.7 %all-reduce.4.cloned.1.call-start = ((), (), s32[]{:S(2)}) async-start(), calls=%async_computation | async-start | bytes 6291456 | tf_op jit(solution)/shard_map/psum | solution.py:38
  40.0 118.0 %all-reduce.6.cloned.1.call-start = ((), (), s32[]{:S(2)}) async-start(), calls=%async_computation.1 | async-start | bytes 393216 | tf_op jit(solution)/shard_map/psum | solution.py:44
  112.3 8.4 %copy-start = (f32[96,16384]{1,0:T(8,128)}, f32[96,16384]{1,0:T(8,128)S(1)}, u32[]{:S(2)}) copy-start(f32[96,16384]{1,0:T(8,128)S(1)} %convert_element_type.53) | copy-start | bytes 18874372
  112.3 8.4 %slice-start = ((s8[8388608]{0:T(1024)(128)(4,1)}), s8[4194304]{0:T(1024)(128)(4,1)S(1)}, s32[]{:S(2)}) async-start(s8[8388608]{0:T(1024)(128)(4,1)} %bitcast.14), calls=%async_computation.3 | async-start | bytes 8388608
  112.8 8.0 %slice-start.1 = ((s8[8388608]{0:T(1024)(128)(4,1)}), s8[4194304]{0:T(1024)(128)(4,1)S(1)}, s32[]{:S(2)}) async-start(s8[8388608]{0:T(1024)(128)(4,1)} %bitcast.14), calls=%async_computation.4 | async-start | bytes 8388608
  120.8 37.3 %copy-start.3 = (f32[96]{0:T(128)S(1)}, f32[96]{0:T(128)}, u32[]{:S(2)}) copy-start(f32[96]{0:T(128)} %param.9) | copy-start | bytes 1156
  123.0 76.7 %all-reduce.8.cloned.1.call-start = ((), (), s32[]{:S(2)}) async-start(), calls=%async_computation.2 | async-start | bytes 1572864 | tf_op jit(solution)/shard_map/psum | solution.py:49
  158.1 7.2 %copy-start.2 = (bf16[96,1024]{1,0:T(8,128)(2,1)S(1)}, bf16[96,1024]{1,0:T(8,128)(2,1)}, u32[]{:S(2)}) copy-start(bf16[96,1024]{1,0:T(8,128)(2,1)} %all-reduce.6.cloned.1.call-done) | copy-start | bytes 589828
  207.2 12.0 %copy-start.1 = (bf16[96,4096]{1,0:T(8,128)(2,1)S(1)}, bf16[96,4096]{1,0:T(8,128)(2,1)}, u32[]{:S(2)}) copy-start(bf16[96,4096]{1,0:T(8,128)(2,1)} %all-reduce.8.cloned.1.call-done) | copy-start | bytes 2359300
Sparse Core Ops, SparseCore 0:
  40.1 69.6 all-reduce.3
  123.1 34.9 all-reduce.5
  165.4 34.3 all-reduce.7
where the time goes:
time: 246 us; the launch traced here: 245 us
  waiting for transfers between devices  133 us (54%)
  matrix products  55.1 us (22%)
  local copies, waits for them, and re-layouts  23.9 us (10%)
  blocking collectives  15.7 us (6%)
  between operations  13.8 us (6%)
  other arithmetic  2.87 us (1%)
    psum x1, waiting for transfers between devices, per_device(): summed = lax.psum(partials.astype(jnp.bfloat16), 'mp').astype(jnp.float32)  69.8 us
    psum x1, waiting for transfers between devices, per_device(): out_tan = lax.psum(out_part.astype(jnp.bfloat16), 'dp').astype(jnp.float32)  34.8 us
    psum x1, waiting for transfers between devices, per_device(): back = lax.psum(back_part.astype(jnp.bfloat16), 'mp').astype(jnp.float32)  28.7 us
    unnamed x14, local copies, waits for them, and re-layouts  23.9 us
    dot_general x1, matrix products, per_device(): partials = jnp.dot(gathered, stacked, preferred_element_type=jnp.float32)  17.1 us
    all_gather x1, blocking collectives, per_device(): gathered = lax.all_gather(tokens, 'dp', axis=0, tiled=True)  15.7 us
    dot_general x1, matrix products, per_device(): jnp.dot(hidden_tan, down_weight, preferred_element_type=jnp.float32)  7.96 us
    dot_general x1, matrix products, per_device(): lax.dot_general(gathered, gate_back, (((0,), (0,)), ((), ())), preferred_...  7.53 us
  transfers between devices with their start and end apart: 3, of which 3 were waited for; matrix products, arithmetic and copies ran while one was open for 2% of the time, Pallas kernels for 0%

commit v1 on v0

v1 whole, which is shorter than its diff:
```python
import functools

import jax
import jax.numpy as jnp
from jax import lax
from jax.experimental import pallas as pl
from jax.experimental.pallas import tpu as pltpu
from jax.sharding import PartitionSpec as P

F32, BF16 = jnp.float32, jnp.bfloat16
CHUNKS = 2
PARAMS = pltpu.CompilerParams(vmem_limit_bytes=24 * 1024 * 1024)


def partner(index, step, count):
    if count & (count - 1) == 0:
        return index ^ step
    return (index + step) % count


def giver(index, step, count):
    if count & (count - 1) == 0:
        return index ^ step
    return (index - step) % count


def cost(flops, *arrays):
    return pl.CostEstimate(
        flops=int(flops), bytes_accessed=int(sum(arrays)), transcendentals=0
    )


def call(body, grid, in_specs, out_specs, out_shape, estimate, scratch=(), aliases=None):
    return pl.pallas_call(
        body,
        grid_spec=pltpu.PrefetchScalarGridSpec(
            num_scalar_prefetch=1,
            grid=grid,
            in_specs=in_specs,
            out_specs=out_specs,
            scratch_shapes=scratch,
        ),
        out_shape=out_shape,
        compiler_params=PARAMS,
        cost_estimate=estimate,
        input_output_aliases=aliases or {},
    )


def project(core, rows, weights, side, first, count, added, dtype):
    tokens, depth = rows.shape
    chunk = weights[0].shape[1] // 2 // CHUNKS
    width = min(256, chunk)
    blocks = chunk // width
    kinds = len(weights)

    def body(core_ref, x_ref, *refs):
        for k in range(kinds):
            total = jnp.dot(x_ref[...], refs[k][...], preferred_element_type=F32)
            if added is not None:
                total += refs[kinds][k].astype(F32)
            refs[-1][k] = total.astype(dtype)

    w_spec = pl.BlockSpec(
        (depth, width), lambda j, c: (0, ((c[0] ^ side) * CHUNKS + first) * blocks + j)
    )
    o_spec = pl.BlockSpec((kinds, tokens, width), lambda j, c: (0, 0, j))
    return call(
        body,
        (count * blocks,),
        [pl.BlockSpec((tokens, depth), lambda j, c: (0, 0))]
        + [w_spec] * kinds
        + ([o_spec] if added is not None else []),
        o_spec,
        jax.ShapeDtypeStruct((kinds, tokens, count * chunk), dtype),
        cost(2 * kinds * tokens * depth * chunk * count, 2 * kinds * depth * chunk * count),
    )(core, rows, *weights, *([added] if added is not None else []))


def activate(core, own, others, tangents, index):
    _, tokens, chunk = own.shape
    width = min(512, chunk)
    blocks = chunk // width

    def body(core_ref, own_ref, *refs):
        arrived, t_ref = refs[: len(others)], refs[len(others)]
        hidden_ref, tan_ref, swish_ref, slope_up_ref = refs[len(others) + 1 :]
        gate, up = own_ref[0].astype(F32), own_ref[1].astype(F32)
        for other in arrived:
            gate, up = gate + other[0].astype(F32), up + other[1].astype(F32)
        logistic = jax.nn.sigmoid(gate)
        swish = gate * logistic
        slope_up = logistic * (1.0 + gate * (1.0 - logistic)) * up
        hidden_ref[...] = (swish * up).astype(BF16)
        tan_ref[...] = (slope_up * t_ref[0] + swish * t_ref[1]).astype(BF16)
        swish_ref[...] = swish
        slope_up_ref[...] = slope_up

    pair = pl.BlockSpec((2, tokens, width), lambda j, c: (0, 0, j))
    single = pl.BlockSpec((tokens, width), lambda j, c: (0, j))
    return call(
        body,
        (blocks,),
        [pair] * (1 + len(others))
        + [pl.BlockSpec((2, tokens, width), lambda j, c: (0, 0, index * blocks + j))],
        [single] * 4,
        [jax.ShapeDtypeStruct((tokens, chunk), d) for d in (BF16, BF16, F32, F32)],
        cost(20 * tokens * chunk, 24 * tokens * chunk),
    )(core, own, *others, tangents)


def contract(core, own, other, weight, index, carried, pieces):
    tokens, chunk = own.shape
    width = weight.shape[1]
    deep = min(512, chunk)
    blocks = chunk // deep
    rows = tokens // max(pieces, 1)

    def body(core_ref, own_ref, other_ref, w_ref, *refs):
        total = refs[-1]
        side, k = pl.program_id(0), pl.program_id(1)

        @pl.when((side == 0) & (k == 0))
        def _():
            if carried is None:
                total[...] = jnp.zeros_like(total)
            else:
                total[...] = refs[0][...]

        @pl.when(side == 0)
        def _():
            total[...] += jnp.dot(own_ref[...], w_ref[...], preferred_element_type=F32)

        @pl.when(side == 1)
        def _():
            total[...] += jnp.dot(other_ref[...], w_ref[...], preferred_element_type=F32)

        @pl.when((side == 1) & (k == blocks - 1))
        def _():
            outs = refs[(0 if carried is None else 1) : -1]
            if pieces == 0:
                outs[0][...] = total[...]
            else:
                for p, out in enumerate(outs):
                    out[...] = total[p * rows : (p + 1) * rows, :].astype(out.dtype)

    whole = pl.BlockSpec((tokens, width), lambda s, k, c: (0, 0))
    left = pl.BlockSpec((tokens, deep), lambda s, k, c: (0, k))
    if pieces == 0:
        out_specs, out_shape = whole, jax.ShapeDtypeStruct((tokens, width), F32)
    else:
        out_specs = [pl.BlockSpec((rows, width), lambda s, k, c: (0, 0))] * pieces
        out_shape = [
            jax.ShapeDtypeStruct((rows, width), F32 if p == 0 else BF16) for p in range(pieces)
        ]
    return call(
        body,
        (2, blocks),
        [
            left,
            left,
            pl.BlockSpec(
                (deep, width), lambda s, k, c: (((c[0] ^ s) * CHUNKS + index) * blocks + k, 0)
            ),
        ]
        + ([whole] if carried is not None else []),
        out_specs,
        out_shape,
        cost(4 * tokens * chunk * width, 4 * chunk * width),
        [pltpu.VMEM((tokens, width), F32)],
    )(core, own, other, weight, *([carried] if carried is not None else []))


def pull_back(core, weighted, weight, side, index, added):
    tokens, width = weighted.shape
    chunk = weight.shape[0] // 2 // CHUNKS
    high = min(256, chunk)
    blocks = chunk // high

    def body(core_ref, x_ref, w_ref, *refs):
        total = lax.dot_general(
            x_ref[...], w_ref[...], (((1,), (1,)), ((), ())), preferred_element_type=F32
        )
        if added is not None:
            total += refs[0][...].astype(F32)
        refs[-1][...] = total.astype(BF16)

    spec = pl.BlockSpec((tokens, high), lambda j, c: (0, j))
    return call(
        body,
        (blocks,),
        [
            pl.BlockSpec((tokens, width), lambda j, c: (0, 0)),
            pl.BlockSpec(
                (high, width), lambda j, c: (((c[0] ^ side) * CHUNKS + index) * blocks + j, 0)
            ),
        ]
        + ([spec] if added is not None else []),
        spec,
        jax.ShapeDtypeStruct((tokens, chunk), BF16),
        cost(2 * tokens * chunk * width, 2 * chunk * width),
    )(core, weighted, weight, *([added] if added is not None else []))


def cotangents(core, own, others, swish, slope_up):
    tokens, chunk = own.shape
    width = min(512, chunk)

    def body(core_ref, own_ref, *refs):
        back = own_ref[...].astype(F32)
        for other in refs[: len(others)]:
            back += other[...].astype(F32)
        swish_ref, slope_up_ref, out = refs[len(others) :]
        out[0] = (back * slope_up_ref[...]).astype(BF16)
        out[1] = (back * swish_ref[...]).astype(BF16)

    single = pl.BlockSpec((tokens, width), lambda j, c: (0, j))
    return call(
        body,
        (chunk // width,),
        [single] * (3 + len(others)),
        pl.BlockSpec((2, tokens, width), lambda j, c: (0, 0, j)),
        jax.ShapeDtypeStruct((2, tokens, chunk), BF16),
        cost(4 * tokens * chunk, 16 * tokens * chunk),
    )(core, own, *others, swish, slope_up)


def outer_down(core, hiddens, weighted):
    tokens, chunk = hiddens[0].shape
    width = weighted.shape[1]
    high = min(512, chunk)
    blocks = chunk // high

    def body(core_ref, *refs):
        x_ref, out = refs[-2], refs[-1]
        for m in range(len(hiddens)):

            @pl.when(pl.program_id(0) == m)
            def _(m=m):
                out[...] = lax.dot_general(
                    refs[m][...], x_ref[...], (((0,), (0,)), ((), ())), preferred_element_type=F32
                ).astype(BF16)

    return call(
        body,
        (len(hiddens), blocks),
        [pl.BlockSpec((tokens, high), lambda g, k, c: (0, k))] * len(hiddens)
        + [pl.BlockSpec((tokens, width), lambda g, k, c: (0, 0))],
        pl.BlockSpec(
            (high, width),
            lambda g, k, c: (((c[0] ^ (g // CHUNKS)) * CHUNKS + g % CHUNKS) * blocks + k, 0),
        ),
        jax.ShapeDtypeStruct((len(hiddens) * chunk, width), BF16),
        cost(2 * tokens * len(hiddens) * chunk * width, 2 * len(hiddens) * chunk * width),
    )(core, *hiddens, weighted)


def outer_pair(core, rows, backs, side, index, hidden_units, filled):
    tokens, depth = rows.shape
    chunk = backs.shape[2]
    high = min(256, depth)

    def body(core_ref, x_ref, b_ref, *refs):
        for k in range(2):
            refs[k - 2][...] = lax.dot_general(
                x_ref[...], b_ref[k], (((0,), (0,)), ((), ())), preferred_element_type=F32
            ).astype(BF16)

    return call(
        body,
        (depth // high,),
        [
            pl.BlockSpec((tokens, high), lambda r, c: (0, r)),
            pl.BlockSpec((2, tokens, chunk), lambda r, c: (0, 0, 0)),
        ]
        + ([pl.BlockSpec(memory_space=pl.ANY)] * 2 if filled else []),
        [pl.BlockSpec((high, chunk), lambda r, c: (r, (c[0] ^ side) * CHUNKS + index))] * 2,
        [jax.ShapeDtypeStruct((depth, hidden_units), BF16)] * 2,
        cost(4 * tokens * depth * chunk, 4 * depth * chunk),
        aliases={3: 0, 4: 1} if filled else None,
    )(core, rows, backs, *(filled or ()))


def per_device(
    sizes,
    tokens,
    curvature,
    gate_weight,
    up_weight,
    down_weight,
    gate_vector,
    up_vector,
    down_vector,
):
    groups, chips = sizes["dp"], sizes["mp"] // 2
    hidden_units = gate_weight.shape[1]
    group_rows = tokens.shape[0]
    core = lax.rem(lax.axis_index("mp"), 2).astype(jnp.int32)[None]
    mine = lax.dynamic_slice(curvature, (lax.axis_index("dp") * group_rows,), (group_rows,))

    def over_dp(value, step):
        return lax.ppermute(value, "dp", [(i, partner(i, step, groups)) for i in range(groups)])

    def back_over_dp(value, step):
        return lax.ppermute(value, "dp", [(i, giver(i, step, groups)) for i in range(groups)])

    def to_core(value):
        return lax.ppermute(value, "mp", [(i, i ^ 1) for i in range(2 * chips)])

    def over_chips(value):
        return [
            lax.ppermute(
                value,
                "mp",
                [(2 * i + c, 2 * partner(i, k, chips) + c) for i in range(chips) for c in range(2)],
            )
            for k in range(1, chips)
        ]

    rows = jnp.concatenate([tokens] + [over_dp(tokens, p) for p in range(1, groups)], axis=0)

    primal, probe = (gate_weight, up_weight), (gate_vector, up_vector)
    arrived = [
        to_core(project(core, rows, primal, 1, i, 1, None, BF16)) for i in range(CHUNKS)
    ]
    sums = [project(core, rows, primal, 0, i, 1, arrived[i], BF16) for i in range(CHUNKS)]
    others = [over_chips(s) for s in sums]
    probe_arrived = to_core(project(core, rows, probe, 1, 0, CHUNKS, None, BF16))
    tangents = project(core, rows, probe, 0, 0, CHUNKS, probe_arrived, F32)

    acted = [activate(core, sums[i], others[i], tangents, i) for i in range(CHUNKS)]
    hidden = [a[0] for a in acted]
    hidden_other = [to_core(h) for h in hidden]
    hidden_tan = []
    for a in acted:
        total = a[1].astype(F32)
        for other in over_chips(a[1]):
            total += other.astype(F32)
        hidden_tan.append(total.astype(BF16))
    hidden_tan_other = [to_core(h) for h in hidden_tan]

    carried = None
    for i in range(CHUNKS):
        carried = contract(core, hidden[i], hidden_other[i], down_vector, i, carried, 0)
    for i in range(CHUNKS):
        carried = contract(
            core,
            hidden_tan[i],
            hidden_tan_other[i],
            down_weight,
            i,
            carried,
            groups if i == CHUNKS - 1 else 0,
        )
    out_tan = carried[0]
    for p in range(1, groups):
        out_tan += back_over_dp(carried[p], p).astype(F32)
    weighted_mine = (mine[:, None] * out_tan).astype(BF16)
    weighted = jnp.concatenate(
        [weighted_mine] + [over_dp(weighted_mine, p) for p in range(1, groups)], axis=0
    )

    arrived = [to_core(pull_back(core, weighted, down_weight, 1, i, None)) for i in range(CHUNKS)]
    sums = [pull_back(core, weighted, down_weight, 0, i, arrived[i]) for i in range(CHUNKS)]
    others = [over_chips(s) for s in sums]
    fisher_down = outer_down(core, hidden + hidden_other, weighted)
    filled = None
    for i in range(CHUNKS):
        backs = cotangents(core, sums[i], others[i], acted[i][2], acted[i][3])
        backs_other = to_core(backs)
        filled = outer_pair(core, rows, backs, 0, i, hidden_units, filled)
        filled = outer_pair(core, rows, backs_other, 1, i, hidden_units, filled)
    return (filled[0], filled[1], fisher_down)


def solution(mesh):
    placed = (
        P(("parts", "dp"), "mp"),
        P("parts"),
        P("mp", "dp"),
        P("mp", "dp"),
        P("dp", "mp"),
        P(("parts", "mp"), "dp"),
        P(("parts", "mp"), "dp"),
        P(("parts", "dp"), "mp"),
    )
    return jax.shard_map(
        functools.partial(per_device, dict(mesh.shape)),
        mesh=mesh,
        in_specs=placed,
        out_specs=(P(("parts", "mp"), "dp"), P(("parts", "mp"), "dp"), P(("parts", "dp"), "mp")),
        check_vma=False,
    )
```

time: 246 us -> 119 us (0.48)
  waiting for transfers between devices: 133 us -> 33.8 us
  matrix products: 55.1 us -> 0 us
  Pallas kernels: 0 us -> 47.7 us
  starting transfers between devices: 0.3 us -> 24 us
  blocking collectives: 15.7 us -> 0 us
  between operations: 13.8 us -> 1 us
  local copies, waits for them, and re-layouts: 23.9 us -> 12.5 us
  other arithmetic: 2.87 us -> 0.19 us
    psum x3 -> x0, waiting for transfers between devices: 133 us -> none  [the longest x1 69.8 us: per_device(): summed = lax.psum(partials.astype(jnp.bfloat16), 'mp').astype(jnp.float32)]
    dot_general x7 -> x0, matrix products: 55.1 us -> none  [the longest x1 17.1 us: per_device(): partials = jnp.dot(gathered, stacked, preferred_element_type=jnp.float32)]
    pallas_call x0 -> x23, Pallas kernels: none -> 47.7 us  [the longest x6 15.9 us: project(): call(body, (count * blocks,), [pl.BlockSpec((tokens, depth), lambda j, c:...]
    ppermute x0 -> x26, waiting for transfers between devices: none -> 33.8 us  [the longest x6 22.2 us: over_chips(): lax.ppermute(value, 'mp', [(2 * i + c, 2 * partner(i, k, chips) + c) for...]
    ppermute x0 -> x26, starting transfers between devices: none -> 24 us  [the longest x6 10.1 us: over_dp(): lax.ppermute(value, 'dp', [(i, partner(i, step, groups)) for i in range(g...]
    all_gather x1 -> x0, blocking collectives: 15.7 us -> none  [per_device(): gathered = lax.all_gather(tokens, 'dp', axis=0, tiled=True)]
    unnamed x14 -> x25, local copies, waits for them, and re-layouts: 23.9 us -> 12.4 us
    convert_element_type x2 -> x3, other arithmetic: 2.87 us -> 0.17 us  [the longest x2 0.1 us: per_device(): hidden_tan.append(total.astype(BF16))]
  transfers between devices with their start and end apart: 3 -> 26, of which waited for: 3 -> 12; matrix products, arithmetic and copies ran while one was open for 2% -> 1% of each run, Pallas kernels for 0% -> 32%
where the time goes in v1:
time: 119 us
  Pallas kernels  47.7 us (40%)
  waiting for transfers between devices  33.8 us (28%)
  starting transfers between devices  24 us (20%)
  local copies, waits for them, and re-layouts  12.5 us (11%)
    ppermute x6, waiting for transfers between devices, over_chips(): lax.ppermute(value, 'mp', [(2 * i + c, 2 * partner(i, k, chips) + c) for...  22.2 us
    pallas_call x6, Pallas kernels, project(): call(body, (count * blocks,), [pl.BlockSpec((tokens, depth), lambda j, c:...  15.9 us
    unnamed x25, local copies, waits for them, and re-layouts  12.4 us
    pallas_call x4, Pallas kernels, outer_pair(): call(body, (depth // high,), [pl.BlockSpec((tokens, high), lambda r, c: (...  12.4 us
    ppermute x6, starting transfers between devices, over_dp(): lax.ppermute(value, 'dp', [(i, partner(i, step, groups)) for i in range(g...  10.1 us
    ppermute x6, waiting for transfers between devices, over_dp(): lax.ppermute(value, 'dp', [(i, partner(i, step, groups)) for i in range(g...  8.3 us
    ppermute x6, starting transfers between devices, over_chips(): lax.ppermute(value, 'mp', [(2 * i + c, 2 * partner(i, k, chips) + c) for...  7.42 us
    pallas_call x1, Pallas kernels, outer_down(): call(body, (len(hiddens), blocks), [pl.BlockSpec((tokens, high), lambda g...  6.56 us
  transfers between devices with their start and end apart: 26, of which 12 were waited for; matrix products, arithmetic and copies ran while one was open for 1% of the time, Pallas kernels for 32%

profile of v1, /device:TPU:0, one launch (start us, length us, event | category | flops | bytes accessed | tf_op | source)
XLA Modules:
  0.0 119.2 jit_solution(12195537513907801382)
XLA Ops:
  0.6 3.1 %collective-permute-start = (bf16[24,1024]{1,0:T(8,128)(2,1)}, bf16[24,1024]{1,0:T(8,128)(2,1)S(1)}, u32[]{:S(2)}, u32[]{:S(2)}) collective-permute-start(bf16[24,1024]{1,0:T(8,128)(2,1)} %param.8), channel_id=1, source_target_pairs={{0,4},{4,0},{8,12},{12,8},{1,5},{5,1},{9,13},{13,9},{2,6},{6,2},{1... | collective-permute-start | bytes 147464 | tf_op jit(solution)/shard_map/ppermute | solution.py:302
  3.7 2.6 %collective-permute-start.1 = (bf16[24,1024]{1,0:T(8,128)(2,1)}, bf16[24,1024]{1,0:T(8,128)(2,1)S(1)}, u32[]{:S(2)}, u32[]{:S(2)}) collective-permute-start(bf16[24,1024]{1,0:T(8,128)(2,1)} %param.8), channel_id=1, source_target_pairs={{0,8},{4,12},{8,0},{12,4},{1,9},{5,13},{9,1},{13,5},{2,10},{6,14},... | collective-permute-start | bytes 147464 | tf_op jit(solution)/shard_map/ppermute | solution.py:302
  7.2 2.7 %collective-permute-done.1 = bf16[24,1024]{1,0:T(8,128)(2,1)S(1)} collective-permute-done((bf16[24,1024]{1,0:T(8,128)(2,1)}, bf16[24,1024]{1,0:T(8,128)(2,1)S(1)}, u32[]{:S(2)}, u32[]{:S(2)}) %collective-permute-start.1) | collective-permute-done | bytes 49184 | tf_op jit(solution)/shard_map/ppermute | solution.py:302
  9.9 2.5 %collective-permute-done.2 = bf16[24,1024]{1,0:T(8,128)(2,1)S(1)} collective-permute-done((bf16[24,1024]{1,0:T(8,128)(2,1)}, bf16[24,1024]{1,0:T(8,128)(2,1)S(1)}, u32[]{:S(2)}, u32[]{:S(2)}) %collective-permute-start.2) | collective-permute-done | bytes 49184 | tf_op jit(solution)/shard_map/ppermute | solution.py:302
  12.4 3.4 %copy-done.2 = bf16[1024,4096]{1,0:T(8,128)(2,1)S(1)} copy-done((bf16[1024,4096]{1,0:T(8,128)(2,1)S(1)}, bf16[1024,4096]{1,0:T(8,128)(2,1)}, u32[]{:S(2)}) %copy-start.2) | copy-done | bytes 8388632
  15.8 3.4 %copy-done.3 = bf16[1024,4096]{1,0:T(8,128)(2,1)S(1)} copy-done((bf16[1024,4096]{1,0:T(8,128)(2,1)S(1)}, bf16[1024,4096]{1,0:T(8,128)(2,1)}, u32[]{:S(2)}) %copy-start.3) | copy-done | bytes 8388632
  19.2 3.9 %shard_map.105 = bf16[2,96,2048]{2,1,0:T(8,128)(2,1)S(1)} custom-call(s32[1]{0:T(128)} %bitcast.core_ref, bf16[96,1024]{1,0:T(8,128)(2,1)S(1)} %constant_dynamic-update-slice_fusion.x_ref, bf16[1024,4096]{1,0:T(8,128)(2,1)S(1)} %copy-done.2, bf16[1024,4096]{1,0:T(8,128)(2,1)S(1)} %copy-done.3), custom_call_target="tpu_custom_call" | custom-call | flops 805306368 | bytes 8388608 | tf_op jit(solution)/shard_map/pallas_call | solution.py:68
  23.8 2.0 %shard_map.108 = bf16[2,96,1024]{2,1,0:T(8,128)(2,1)S(1)} custom-call(s32[1]{0:T(128)} %bitcast.core_ref, bf16[96,1024]{1,0:T(8,128)(2,1)S(1)} %constant_dynamic-update-slice_fusion.x_ref, bf16[1024,4096]{1,0:T(8,128)(2,1)S(1)} %bitcast.4, bf16[1024,4096]{1,0:T(8,128)(2,1)S(1)} %copy-done.1), custom_call_target="tpu_custom_call" | custom-call | flops 402653184 | bytes 4194304 | tf_op jit(solution)/shard_map/pallas_call | solution.py:68
  25.9 2.0 %shard_map.103 = bf16[2,96,1024]{2,1,0:T(8,128)(2,1)S(1)} custom-call(s32[1]{0:T(128)} %bitcast.core_ref, bf16[96,1024]{1,0:T(8,128)(2,1)S(1)} %constant_dynamic-update-slice_fusion.x_ref, bf16[1024,4096]{1,0:T(8,128)(2,1)S(1)} %bitcast.4, bf16[1024,4096]{1,0:T(8,128)(2,1)S(1)} %copy-done.1), custom_call_target="tpu_custom_call" | custom-call | flops 402653184 | bytes 4194304 | tf_op jit(solution)/shard_map/pallas_call | solution.py:68
  28.4 2.0 %shard_map.109.own_ref = bf16[2,96,1024]{2,1,0:T(8,128)(2,1)S(1)} custom-call(s32[1]{0:T(128)} %bitcast.core_ref, bf16[96,1024]{1,0:T(8,128)(2,1)S(1)} %constant_dynamic-update-slice_fusion.x_ref, bf16[1024,4096]{1,0:T(8,128)(2,1)S(1)} %bitcast.4, bf16[1024,4096]{1,0:T(8,128)(2,1)S(1)} %copy-done.1, bf16[2,96,1024]{2,1,0:T(8,128)(2,1)S(1)} %collective-permute-done.8.refs_2_), custom_call_target="tpu_custom_call" | custom-call | flops 402653184 | bytes 4194304 | tf_op jit(solution)/shard_map/pallas_call | solution.py:68
  30.4 1.6 %collective-permute-start.9 = (bf16[2,96,1024]{2,1,0:T(8,128)(2,1)S(1)}, bf16[2,96,1024]{2,1,0:T(8,128)(2,1)S(1)}, u32[]{:S(2)}, u32[]{:S(2)}) collective-permute-start(bf16[2,96,1024]{2,1,0:T(8,128)(2,1)S(1)} %shard_map.109.own_ref), channel_id=1, source_target_pairs={{0,2},{1,3},{2,0},{3,1},{4,6},{5,7},{6,4},{7,5},{8,10},{9,11},{10,... | collective-permute-start | bytes 1179656 | tf_op jit(solution)/shard_map/ppermute | solution.py:312
  32.0 2.0 %shard_map.104.own_ref = bf16[2,96,1024]{2,1,0:T(8,128)(2,1)S(1)} custom-call(s32[1]{0:T(128)} %bitcast.core_ref, bf16[96,1024]{1,0:T(8,128)(2,1)S(1)} %constant_dynamic-update-slice_fusion.x_ref, bf16[1024,4096]{1,0:T(8,128)(2,1)S(1)} %bitcast.4, bf16[1024,4096]{1,0:T(8,128)(2,1)S(1)} %copy-done.1, bf16[2,96,1024]{2,1,0:T(8,128)(2,1)S(1)} %collective-permute-done.3.refs_2_), custom_call_target="tpu_custom_call" | custom-call | flops 402653184 | bytes 4194304 | tf_op jit(solution)/shard_map/pallas_call | solution.py:68
  34.6 4.0 %shard_map.106.refs_1_ = f32[2,96,2048]{2,1,0:T(8,128)S(1)} custom-call(s32[1]{0:T(128)} %bitcast.core_ref, bf16[96,1024]{1,0:T(8,128)(2,1)S(1)} %constant_dynamic-update-slice_fusion.x_ref, bf16[1024,4096]{1,0:T(8,128)(2,1)S(1)} %copy-done.2, bf16[1024,4096]{1,0:T(8,128)(2,1)S(1)} %copy-done.3, bf16[2,96,2048]{2,1,0:T(8,128)(2,1)S(1)} %collective-permute-done.5.refs_2_), custom_call_target="tpu_custom_call" | custom-call | flops 805306368 | bytes 8388608 | tf_op jit(solution)/shard_map/pallas_call | solution.py:68
  38.7 3.8 %collective-permute-done.9.refs_0_ = bf16[2,96,1024]{2,1,0:T(8,128)(2,1)S(1)} collective-permute-done((bf16[2,96,1024]{2,1,0:T(8,128)(2,1)S(1)}, bf16[2,96,1024]{2,1,0:T(8,128)(2,1)S(1)}, u32[]{:S(2)}, u32[]{:S(2)}) %collective-permute-start.9) | collective-permute-done | bytes 393248 | tf_op jit(solution)/shard_map/ppermute | solution.py:312
  43.0 1.6 %collective-permute-start.10 = (bf16[96,1024]{1,0:T(8,128)(2,1)S(1)}, bf16[96,1024]{1,0:T(8,128)(2,1)S(1)}, u32[]{:S(2)}, u32[]{:S(2)}) collective-permute-start(bf16[96,1024]{1,0:T(8,128)(2,1)S(1)} %get-tuple-element.24), channel_id=1, source_target_pairs={{0,2},{1,3},{2,0},{3,1},{4,6},{5,7},{6,4},{7,5},{8,10},{9,11},{10,... | collective-permute-start | bytes 589832 | tf_op jit(solution)/shard_map/ppermute | solution.py:312
  44.5 6.3 %collective-permute-done.4.refs_0_ = bf16[2,96,1024]{2,1,0:T(8,128)(2,1)S(1)} collective-permute-done((bf16[2,96,1024]{2,1,0:T(8,128)(2,1)S(1)}, bf16[2,96,1024]{2,1,0:T(8,128)(2,1)S(1)}, u32[]{:S(2)}, u32[]{:S(2)}) %collective-permute-start.4) | collective-permute-done | bytes 393248 | tf_op jit(solution)/shard_map/ppermute | solution.py:312
  51.4 1.6 %collective-permute-start.6 = (bf16[96,1024]{1,0:T(8,128)(2,1)S(1)}, bf16[96,1024]{1,0:T(8,128)(2,1)S(1)}, u32[]{:S(2)}, u32[]{:S(2)}) collective-permute-start(bf16[96,1024]{1,0:T(8,128)(2,1)S(1)} %get-tuple-element.23), channel_id=1, source_target_pairs={{0,2},{1,3},{2,0},{3,1},{4,6},{5,7},{6,4},{7,5},{8,10},{9,11},{10,... | collective-permute-start | bytes 589832 | tf_op jit(solution)/shard_map/ppermute | solution.py:312
  53.5 1.6 %collective-permute-done.10 = bf16[96,1024]{1,0:T(8,128)(2,1)S(1)} collective-permute-done((bf16[96,1024]{1,0:T(8,128)(2,1)S(1)}, bf16[96,1024]{1,0:T(8,128)(2,1)S(1)}, u32[]{:S(2)}, u32[]{:S(2)}) %collective-permute-start.10) | collective-permute-done | bytes 196640 | tf_op jit(solution)/shard_map/ppermute | solution.py:312
  55.2 3.2 %collective-permute-done.6 = bf16[96,1024]{1,0:T(8,128)(2,1)S(1)} collective-permute-done((bf16[96,1024]{1,0:T(8,128)(2,1)S(1)}, bf16[96,1024]{1,0:T(8,128)(2,1)S(1)}, u32[]{:S(2)}, u32[]{:S(2)}) %collective-permute-start.6) | collective-permute-done | bytes 196640 | tf_op jit(solution)/shard_map/ppermute | solution.py:312
  66.5 3.4 %collective-permute-start.14 = (bf16[24,1024]{1,0:T(8,128)(2,1)S(1)}, bf16[24,1024]{1,0:T(8,128)(2,1)S(1)}, u32[]{:S(2)}, u32[]{:S(2)}) collective-permute-start(bf16[24,1024]{1,0:T(8,128)(2,1)S(1)} %get-tuple-element.28), channel_id=1, source_target_pairs={{0,4},{4,0},{8,12},{12,8},{1,5},{5,1},{9,13},{13,9},{2,6},{6,2},{1... | collective-permute-start | bytes 147464 | tf_op jit(solution)/shard_map/ppermute | solution.py:305
  70.0 1.9 %collective-permute-done.16 = bf16[24,1024]{1,0:T(8,128)(2,1)S(1)} collective-permute-done((bf16[24,1024]{1,0:T(8,128)(2,1)S(1)}, bf16[24,1024]{1,0:T(8,128)(2,1)S(1)}, u32[]{:S(2)}, u32[]{:S(2)}) %collective-permute-start.16) | collective-permute-done | bytes 49184 | tf_op jit(solution)/shard_map/ppermute | solution.py:305
  75.6 2.1 %collective-permute-start.17 = (bf16[24,1024]{1,0:T(8,128)(2,1)S(1)}, bf16[24,1024]{1,0:T(8,128)(2,1)S(1)}, u32[]{:S(2)}, u32[]{:S(2)}) collective-permute-start(bf16[24,1024]{1,0:T(8,128)(2,1)S(1)} %multiply_convert_fusion), channel_id=1, source_target_pairs={{0,4},{4,0},{8,12},{12,8},{1,5},{5,1},{9,13},{13,9},{2,6},{6,2},{1... | collective-permute-start | bytes 147464 | tf_op jit(solution)/shard_map/ppermute | solution.py:302
  77.7 1.9 %collective-permute-done.19 = bf16[24,1024]{1,0:T(8,128)(2,1)S(1)} collective-permute-done((bf16[24,1024]{1,0:T(8,128)(2,1)S(1)}, bf16[24,1024]{1,0:T(8,128)(2,1)S(1)}, u32[]{:S(2)}, u32[]{:S(2)}) %collective-permute-start.19) | collective-permute-done | bytes 49184 | tf_op jit(solution)/shard_map/ppermute | solution.py:302
  80.9 3.4 %copy-done = bf16[4096,1024]{1,0:T(8,128)(2,1)S(1)} copy-done((bf16[4096,1024]{1,0:T(8,128)(2,1)S(1)}, bf16[4096,1024]{1,0:T(8,128)(2,1)}, u32[]{:S(2)}) %copy-start) | copy-done | bytes 8388632
  88.7 1.6 %collective-permute-start.24 = (bf16[96,1024]{1,0:T(8,128)(2,1)S(1)}, bf16[96,1024]{1,0:T(8,128)(2,1)S(1)}, u32[]{:S(2)}, u32[]{:S(2)}) collective-permute-start(bf16[96,1024]{1,0:T(8,128)(2,1)S(1)} %shard_map.119.own_ref), channel_id=1, source_target_pairs={{0,2},{1,3},{2,0},{3,1},{4,6},{5,7},{6,4},{7,5},{8,10},{9,11},{10,... | collective-permute-start | bytes 589832 | tf_op jit(solution)/shard_map/ppermute | solution.py:312
  92.2 4.3 %collective-permute-done.24.refs_0_ = bf16[96,1024]{1,0:T(8,128)(2,1)S(1)} collective-permute-done((bf16[96,1024]{1,0:T(8,128)(2,1)S(1)}, bf16[96,1024]{1,0:T(8,128)(2,1)S(1)}, u32[]{:S(2)}, u32[]{:S(2)}) %collective-permute-start.24) | collective-permute-done | bytes 196640 | tf_op jit(solution)/shard_map/ppermute | solution.py:312
  96.9 3.0 %collective-permute-done.21.refs_0_ = bf16[96,1024]{1,0:T(8,128)(2,1)S(1)} collective-permute-done((bf16[96,1024]{1,0:T(8,128)(2,1)S(1)}, bf16[96,1024]{1,0:T(8,128)(2,1)S(1)}, u32[]{:S(2)}, u32[]{:S(2)}) %collective-permute-start.21) | collective-permute-done | bytes 196640 | tf_op jit(solution)/shard_map/ppermute | solution.py:312
  100.2 6.6 %shard_map.125 = bf16[4096,1024]{1,0:T(8,128)(2,1)} custom-call(s32[1]{0:T(128)} %bitcast.core_ref, bf16[96,1024]{1,0:T(8,128)(2,1)S(1)} %get-tuple-element.26.own_ref.refs_0_, bf16[96,1024]{1,0:T(8,128)(2,1)S(1)} %get-tuple-element.25.own_ref.refs_1_, bf16[96,1024]{1,0:T(8,128)(2,1)S(1)} %collective-permute-done.13.other_ref.refs_2_, ...), custom_call_target="tpu_custom_call" | custom-call | flops 805306368 | bytes 8388608 | tf_op jit(solution)/shard_map/pallas_call | solution.py:244
  106.7 3.1 %shard_map.121 = (bf16[1024,4096]{1,0:T(8,128)(2,1)}, bf16[1024,4096]{1,0:T(8,128)(2,1)}) custom-call(s32[1]{0:T(128)} %bitcast.core_ref, bf16[96,1024]{1,0:T(8,128)(2,1)S(1)} %constant_dynamic-update-slice_fusion.x_ref, bf16[2,96,1024]{2,1,0:T(8,128)(2,1)S(1)} %shard_map.120.b_ref), custom_call_target="tpu_custom_call" | custom-call | flops 402653184 | bytes 4194304 | tf_op jit(solution)/shard_map/pallas_call | solution.py:269
  109.8 3.1 %shard_map.122 = (bf16[1024,4096]{1,0:T(8,128)(2,1)}, bf16[1024,4096]{1,0:T(8,128)(2,1)}) custom-call(s32[1]{0:T(128)} %bitcast.core_ref, bf16[96,1024]{1,0:T(8,128)(2,1)S(1)} %constant_dynamic-update-slice_fusion.x_ref, bf16[2,96,1024]{2,1,0:T(8,128)(2,1)S(1)} %collective-permute-done.25.b_ref, ...), custom_call_target="tpu_custom_call", output_to_operand_aliasing={{0}: (3, {}), {1}: (4, {})} | custom-call | flops 402653184 | bytes 4194304 | tf_op jit(solution)/shard_map/pallas_call | solution.py:269
  113.0 3.1 %shard_map.123 = (bf16[1024,4096]{1,0:T(8,128)(2,1)}, bf16[1024,4096]{1,0:T(8,128)(2,1)}) custom-call(s32[1]{0:T(128)} %bitcast.core_ref, bf16[96,1024]{1,0:T(8,128)(2,1)S(1)} %constant_dynamic-update-slice_fusion.x_ref, bf16[2,96,1024]{2,1,0:T(8,128)(2,1)S(1)} %shard_map.117.b_ref, ...), custom_call_target="tpu_custom_call", output_to_operand_aliasing={{0}: (3, {}), {1}: (4, {})} | custom-call | flops 402653184 | bytes 4194304 | tf_op jit(solution)/shard_map/pallas_call | solution.py:269
  116.1 3.1 %shard_map.124 = (bf16[1024,4096]{1,0:T(8,128)(2,1)}, bf16[1024,4096]{1,0:T(8,128)(2,1)}) custom-call(s32[1]{0:T(128)} %bitcast.core_ref, bf16[96,1024]{1,0:T(8,128)(2,1)S(1)} %constant_dynamic-update-slice_fusion.x_ref, bf16[2,96,1024]{2,1,0:T(8,128)(2,1)S(1)} %collective-permute-done.22.b_ref, ...), custom_call_target="tpu_custom_call", output_to_operand_aliasing={{0}: (3, {}), {1}: (4, {})} | custom-call | flops 402653184 | bytes 4194304 | tf_op jit(solution)/shard_map/pallas_call | solution.py:269
  (77 shorter events, 24.5 us)
Async XLA Ops:
  0.6 6.6 %collective-permute-start = (bf16[24,1024]{1,0:T(8,128)(2,1)}, bf16[24,1024]{1,0:T(8,128)(2,1)S(1)}, u32[]{:S(2)}, u32[]{:S(2)}) collective-permute-start(bf16[24,1024]{1,0:T(8,128)(2,1)} %param.8), channel_id=1, source_target_pairs={{0,4},{4,0},{8,12},{12,8},{1,5},{5,1},{9,13},{13,9},{2,6},{6,2},{1... | collective-permute-start | bytes 147464 | tf_op jit(solution)/shard_map/ppermute | solution.py:302
  3.7 6.1 %collective-permute-start.1 = (bf16[24,1024]{1,0:T(8,128)(2,1)}, bf16[24,1024]{1,0:T(8,128)(2,1)S(1)}, u32[]{:S(2)}, u32[]{:S(2)}) collective-permute-start(bf16[24,1024]{1,0:T(8,128)(2,1)} %param.8), channel_id=1, source_target_pairs={{0,8},{4,12},{8,0},{12,4},{1,9},{5,13},{9,1},{13,5},{2,10},{6,14},... | collective-permute-start | bytes 147464 | tf_op jit(solution)/shard_map/ppermute | solution.py:302
  6.3 6.1 %collective-permute-start.2 = (bf16[24,1024]{1,0:T(8,128)(2,1)}, bf16[24,1024]{1,0:T(8,128)(2,1)S(1)}, u32[]{:S(2)}, u32[]{:S(2)}) collective-permute-start(bf16[24,1024]{1,0:T(8,128)(2,1)} %param.8), channel_id=1, source_target_pairs={{0,12},{4,8},{8,4},{12,0},{1,13},{5,9},{9,5},{13,1},{2,14},{6,10},... | collective-permute-start | bytes 147464 | tf_op jit(solution)/shard_map/ppermute | solution.py:302
  9.9 13.3 %slice-start.2 = ((s8[8388608]{0:T(1024)(128)(4,1)}), s8[4194304]{0:T(1024)(128)(4,1)S(1)}, s32[]{:S(2)}) async-start(s8[8388608]{0:T(1024)(128)(4,1)} %bitcast.3), calls=%async_computation.2 | async-start | bytes 8388608
  19.2 4.0 %slice-start.3 = ((s8[8388608]{0:T(1024)(128)(4,1)}), s8[4194304]{0:T(1024)(128)(4,1)S(1)}, s32[]{:S(2)}) async-start(s8[8388608]{0:T(1024)(128)(4,1)} %bitcast.3), calls=%async_computation.3 | async-start | bytes 8388608
  19.2 4.7 %copy-start.1 = (bf16[1024,4096]{1,0:T(8,128)(2,1)S(1)}, bf16[1024,4096]{1,0:T(8,128)(2,1)}, u32[]{:S(2)}) copy-start(bf16[1024,4096]{1,0:T(8,128)(2,1)} %refs_1_.11) | copy-start | bytes 25165828
  23.1 11.5 %collective-permute-start.5 = (bf16[2,96,2048]{2,1,0:T(8,128)(2,1)S(1)}, bf16[2,96,2048]{2,1,0:T(8,128)(2,1)S(1)}, u32[]{:S(2)}, u32[]{:S(2)}) collective-permute-start(bf16[2,96,2048]{2,1,0:T(8,128)(2,1)S(1)} %shard_map.105), channel_id=1, source_target_pairs={{0,1},{1,0},{2,3},{3,2},{4,5},{5,4},{6,7},{7,6},{8,9},{9,8},{10,11... | collective-permute-start | bytes 2359304 | tf_op jit(solution)/shard_map/ppermute | solution.py:308
  25.8 2.6 %collective-permute-start.8 = (bf16[2,96,1024]{2,1,0:T(8,128)(2,1)S(1)}, bf16[2,96,1024]{2,1,0:T(8,128)(2,1)S(1)}, u32[]{:S(2)}, u32[]{:S(2)}) collective-permute-start(bf16[2,96,1024]{2,1,0:T(8,128)(2,1)S(1)} %shard_map.108), channel_id=1, source_target_pairs={{0,1},{1,0},{2,3},{3,2},{4,5},{5,4},{6,7},{7,6},{8,9},{9,8},{10,11... | collective-permute-start | bytes 1179656 | tf_op jit(solution)/shard_map/ppermute | solution.py:308
  27.9 4.1 %collective-permute-start.3 = (bf16[2,96,1024]{2,1,0:T(8,128)(2,1)S(1)}, bf16[2,96,1024]{2,1,0:T(8,128)(2,1)S(1)}, u32[]{:S(2)}, u32[]{:S(2)}) collective-permute-start(bf16[2,96,1024]{2,1,0:T(8,128)(2,1)S(1)} %shard_map.103), channel_id=1, source_target_pairs={{0,1},{1,0},{2,3},{3,2},{4,5},{5,4},{6,7},{7,6},{8,9},{9,8},{10,11... | collective-permute-start | bytes 1179656 | tf_op jit(solution)/shard_map/ppermute | solution.py:308
  30.4 12.0 %collective-permute-start.9 = (bf16[2,96,1024]{2,1,0:T(8,128)(2,1)S(1)}, bf16[2,96,1024]{2,1,0:T(8,128)(2,1)S(1)}, u32[]{:S(2)}, u32[]{:S(2)}) collective-permute-start(bf16[2,96,1024]{2,1,0:T(8,128)(2,1)S(1)} %shard_map.109.own_ref), channel_id=1, source_target_pairs={{0,2},{1,3},{2,0},{3,1},{4,6},{5,7},{6,4},{7,5},{8,10},{9,11},{10,... | collective-permute-start | bytes 1179656 | tf_op jit(solution)/shard_map/ppermute | solution.py:312
  32.0 26.6 %slice-start.4 = ((s8[8388608]{0:T(1024)(128)(4,1)}), s8[4194304]{0:T(1024)(128)(4,1)S(1)}, s32[]{:S(2)}) async-start(s8[8388608]{0:T(1024)(128)(4,1)} %bitcast.5), calls=%async_computation.4 | async-start | bytes 8388608
  34.0 24.6 %slice-start.5 = ((s8[8388608]{0:T(1024)(128)(4,1)}), s8[4194304]{0:T(1024)(128)(4,1)S(1)}, s32[]{:S(2)}) async-start(s8[8388608]{0:T(1024)(128)(4,1)} %bitcast.5), calls=%async_computation.5 | async-start | bytes 8388608
  34.0 16.9 %collective-permute-start.4 = (bf16[2,96,1024]{2,1,0:T(8,128)(2,1)S(1)}, bf16[2,96,1024]{2,1,0:T(8,128)(2,1)S(1)}, u32[]{:S(2)}, u32[]{:S(2)}) collective-permute-start(bf16[2,96,1024]{2,1,0:T(8,128)(2,1)S(1)} %shard_map.104.own_ref), channel_id=1, source_target_pairs={{0,2},{1,3},{2,0},{3,1},{4,6},{5,7},{6,4},{7,5},{8,10},{9,11},{10,... | collective-permute-start | bytes 1179656 | tf_op jit(solution)/shard_map/ppermute | solution.py:312
  43.0 12.1 %collective-permute-start.10 = (bf16[96,1024]{1,0:T(8,128)(2,1)S(1)}, bf16[96,1024]{1,0:T(8,128)(2,1)S(1)}, u32[]{:S(2)}, u32[]{:S(2)}) collective-permute-start(bf16[96,1024]{1,0:T(8,128)(2,1)S(1)} %get-tuple-element.24), channel_id=1, source_target_pairs={{0,2},{1,3},{2,0},{3,1},{4,6},{5,7},{6,4},{7,5},{8,10},{9,11},{10,... | collective-permute-start | bytes 589832 | tf_op jit(solution)/shard_map/ppermute | solution.py:312
  51.4 7.0 %collective-permute-start.6 = (bf16[96,1024]{1,0:T(8,128)(2,1)S(1)}, bf16[96,1024]{1,0:T(8,128)(2,1)S(1)}, u32[]{:S(2)}, u32[]{:S(2)}) collective-permute-start(bf16[96,1024]{1,0:T(8,128)(2,1)S(1)} %get-tuple-element.23), channel_id=1, source_target_pairs={{0,2},{1,3},{2,0},{3,1},{4,6},{5,7},{6,4},{7,5},{8,10},{9,11},{10,... | collective-permute-start | bytes 589832 | tf_op jit(solution)/shard_map/ppermute | solution.py:312
  53.0 7.2 %collective-permute-start.12 = (bf16[96,1024]{1,0:T(8,128)(2,1)S(1)}, bf16[96,1024]{1,0:T(8,128)(2,1)S(1)}, u32[]{:S(2)}, u32[]{:S(2)}) collective-permute-start(bf16[96,1024]{1,0:T(8,128)(2,1)S(1)} %get-tuple-element.25.own_ref.refs_1_), channel_id=1, source_target_pairs={{0,1},{1,0},{2,3},{3,2},{4,5},{5,4},{6,7},{7,6},{8,9},{9,8},{10,11... | collective-permute-start | bytes 589832 | tf_op jit(solution)/shard_map/ppermute | solution.py:308
  53.0 5.6 %collective-permute-start.13 = (bf16[96,1024]{1,0:T(8,128)(2,1)S(1)}, bf16[96,1024]{1,0:T(8,128)(2,1)S(1)}, u32[]{:S(2)}, u32[]{:S(2)}) collective-permute-start(bf16[96,1024]{1,0:T(8,128)(2,1)S(1)} %get-tuple-element.26.own_ref.refs_0_), channel_id=1, source_target_pairs={{0,1},{1,0},{2,3},{3,2},{4,5},{5,4},{6,7},{7,6},{8,9},{9,8},{10,11... | collective-permute-start | bytes 589832 | tf_op jit(solution)/shard_map/ppermute | solution.py:308
  55.2 6.5 %collective-permute-start.11 = (bf16[96,1024]{1,0:T(8,128)(2,1)S(1)}, bf16[96,1024]{1,0:T(8,128)(2,1)S(1)}, u32[]{:S(2)}, u32[]{:S(2)}) collective-permute-start(bf16[96,1024]{1,0:T(8,128)(2,1)S(1)} %add_convert_fusion.own_ref), channel_id=1, source_target_pairs={{0,1},{1,0},{2,3},{3,2},{4,5},{5,4},{6,7},{7,6},{8,9},{9,8},{10,11... | collective-permute-start | bytes 589832 | tf_op jit(solution)/shard_map/ppermute | solution.py:308
  58.5 5.5 %collective-permute-start.7 = (bf16[96,1024]{1,0:T(8,128)(2,1)S(1)}, bf16[96,1024]{1,0:T(8,128)(2,1)S(1)}, u32[]{:S(2)}, u32[]{:S(2)}) collective-permute-start(bf16[96,1024]{1,0:T(8,128)(2,1)S(1)} %add_convert_fusion.1.own_ref), channel_id=1, source_target_pairs={{0,1},{1,0},{2,3},{3,2},{4,5},{5,4},{6,7},{7,6},{8,9},{9,8},{10,11... | collective-permute-start | bytes 589832 | tf_op jit(solution)/shard_map/ppermute | solution.py:308
  61.7 8.3 %copy-start.4 = (f32[96]{0:T(128)S(1)}, f32[96]{0:T(128)}, u32[]{:S(2)}) copy-start(f32[96]{0:T(128)} %param.9) | copy-start | bytes 1156
  65.5 6.5 %collective-permute-start.16 = (bf16[24,1024]{1,0:T(8,128)(2,1)S(1)}, bf16[24,1024]{1,0:T(8,128)(2,1)S(1)}, u32[]{:S(2)}, u32[]{:S(2)}) collective-permute-start(bf16[24,1024]{1,0:T(8,128)(2,1)S(1)} %get-tuple-element.30), channel_id=1, source_target_pairs={{0,12},{4,8},{8,4},{12,0},{1,13},{5,9},{9,5},{13,1},{2,14},{6,10},... | collective-permute-start | bytes 147464 | tf_op jit(solution)/shard_map/ppermute | solution.py:305
  66.5 6.7 %collective-permute-start.15 = (bf16[24,1024]{1,0:T(8,128)(2,1)S(1)}, bf16[24,1024]{1,0:T(8,128)(2,1)S(1)}, u32[]{:S(2)}, u32[]{:S(2)}) collective-permute-start(bf16[24,1024]{1,0:T(8,128)(2,1)S(1)} %get-tuple-element.29), channel_id=1, source_target_pairs={{0,8},{4,12},{8,0},{12,4},{1,9},{5,13},{9,1},{13,5},{2,10},{6,14},... | collective-permute-start | bytes 147464 | tf_op jit(solution)/shard_map/ppermute | solution.py:305
  66.5 6.7 %collective-permute-start.14 = (bf16[24,1024]{1,0:T(8,128)(2,1)S(1)}, bf16[24,1024]{1,0:T(8,128)(2,1)S(1)}, u32[]{:S(2)}, u32[]{:S(2)}) collective-permute-start(bf16[24,1024]{1,0:T(8,128)(2,1)S(1)} %get-tuple-element.28), channel_id=1, source_target_pairs={{0,4},{4,0},{8,12},{12,8},{1,5},{5,1},{9,13},{13,9},{2,6},{6,2},{1... | collective-permute-start | bytes 147464 | tf_op jit(solution)/shard_map/ppermute | solution.py:305
  73.3 6.3 %collective-permute-start.19 = (bf16[24,1024]{1,0:T(8,128)(2,1)S(1)}, bf16[24,1024]{1,0:T(8,128)(2,1)S(1)}, u32[]{:S(2)}, u32[]{:S(2)}) collective-permute-start(bf16[24,1024]{1,0:T(8,128)(2,1)S(1)} %multiply_convert_fusion), channel_id=1, source_target_pairs={{0,12},{4,8},{8,4},{12,0},{1,13},{5,9},{9,5},{13,1},{2,14},{6,10},... | collective-permute-start | bytes 147464 | tf_op jit(solution)/shard_map/ppermute | solution.py:302
  74.7 6.1 %collective-permute-start.18 = (bf16[24,1024]{1,0:T(8,128)(2,1)S(1)}, bf16[24,1024]{1,0:T(8,128)(2,1)S(1)}, u32[]{:S(2)}, u32[]{:S(2)}) collective-permute-start(bf16[24,1024]{1,0:T(8,128)(2,1)S(1)} %multiply_convert_fusion), channel_id=1, source_target_pairs={{0,8},{4,12},{8,0},{12,4},{1,9},{5,13},{9,1},{13,5},{2,10},{6,14},... | collective-permute-start | bytes 147464 | tf_op jit(solution)/shard_map/ppermute | solution.py:302
  75.6 5.2 %collective-permute-start.17 = (bf16[24,1024]{1,0:T(8,128)(2,1)S(1)}, bf16[24,1024]{1,0:T(8,128)(2,1)S(1)}, u32[]{:S(2)}, u32[]{:S(2)}) collective-permute-start(bf16[24,1024]{1,0:T(8,128)(2,1)S(1)} %multiply_convert_fusion), channel_id=1, source_target_pairs={{0,4},{4,0},{8,12},{12,8},{1,5},{5,1},{9,13},{13,9},{2,6},{6,2},{1... | collective-permute-start | bytes 147464 | tf_op jit(solution)/shard_map/ppermute | solution.py:302
  85.5 1.9 %collective-permute-start.23 = (bf16[96,1024]{1,0:T(8,128)(2,1)S(1)}, bf16[96,1024]{1,0:T(8,128)(2,1)S(1)}, u32[]{:S(2)}, u32[]{:S(2)}) collective-permute-start(bf16[96,1024]{1,0:T(8,128)(2,1)S(1)} %shard_map.118), channel_id=1, source_target_pairs={{0,1},{1,0},{2,3},{3,2},{4,5},{5,4},{6,7},{7,6},{8,9},{9,8},{10,11... | collective-permute-start | bytes 589832 | tf_op jit(solution)/shard_map/ppermute | solution.py:308
  86.9 3.4 %collective-permute-start.20 = (bf16[96,1024]{1,0:T(8,128)(2,1)S(1)}, bf16[96,1024]{1,0:T(8,128)(2,1)S(1)}, u32[]{:S(2)}, u32[]{:S(2)}) collective-permute-start(bf16[96,1024]{1,0:T(8,128)(2,1)S(1)} %shard_map.115), channel_id=1, source_target_pairs={{0,1},{1,0},{2,3},{3,2},{4,5},{5,4},{6,7},{7,6},{8,9},{9,8},{10,11... | collective-permute-start | bytes 589832 | tf_op jit(solution)/shard_map/ppermute | solution.py:308
  88.7 7.8 %collective-permute-start.24 = (bf16[96,1024]{1,0:T(8,128)(2,1)S(1)}, bf16[96,1024]{1,0:T(8,128)(2,1)S(1)}, u32[]{:S(2)}, u32[]{:S(2)}) collective-permute-start(bf16[96,1024]{1,0:T(8,128)(2,1)S(1)} %shard_map.119.own_ref), channel_id=1, source_target_pairs={{0,2},{1,3},{2,0},{3,1},{4,6},{5,7},{6,4},{7,5},{8,10},{9,11},{10,... | collective-permute-start | bytes 589832 | tf_op jit(solution)/shard_map/ppermute | solution.py:312
  91.6 8.2 %collective-permute-start.21 = (bf16[96,1024]{1,0:T(8,128)(2,1)S(1)}, bf16[96,1024]{1,0:T(8,128)(2,1)S(1)}, u32[]{:S(2)}, u32[]{:S(2)}) collective-permute-start(bf16[96,1024]{1,0:T(8,128)(2,1)S(1)} %shard_map.116.own_ref), channel_id=1, source_target_pairs={{0,2},{1,3},{2,0},{3,1},{4,6},{5,7},{6,4},{7,5},{8,10},{9,11},{10,... | collective-permute-start | bytes 589832 | tf_op jit(solution)/shard_map/ppermute | solution.py:312
  96.8 13.0 %collective-permute-start.25 = (bf16[2,96,1024]{2,1,0:T(8,128)(2,1)S(1)}, bf16[2,96,1024]{2,1,0:T(8,128)(2,1)S(1)}, u32[]{:S(2)}, u32[]{:S(2)}) collective-permute-start(bf16[2,96,1024]{2,1,0:T(8,128)(2,1)S(1)} %shard_map.120.b_ref), channel_id=1, source_target_pairs={{0,1},{1,0},{2,3},{3,2},{4,5},{5,4},{6,7},{7,6},{8,9},{9,8},{10,11... | collective-permute-start | bytes 1179656 | tf_op jit(solution)/shard_map/ppermute | solution.py:308
  100.1 16.0 %collective-permute-start.22 = (bf16[2,96,1024]{2,1,0:T(8,128)(2,1)S(1)}, bf16[2,96,1024]{2,1,0:T(8,128)(2,1)S(1)}, u32[]{:S(2)}, u32[]{:S(2)}) collective-permute-start(bf16[2,96,1024]{2,1,0:T(8,128)(2,1)S(1)} %shard_map.117.b_ref), channel_id=1, source_target_pairs={{0,1},{1,0},{2,3},{3,2},{4,5},{5,4},{6,7},{7,6},{8,9},{9,8},{10,11... | collective-permute-start | bytes 1179656 | tf_op jit(solution)/shard_map/ppermute | solution.py:308
  (5 other events, 15.7 us)

commit v2 on v0

v2 whole, which is shorter than its diff:
```python
import functools

import jax
import jax.numpy as jnp
from jax import lax
from jax.experimental import pallas as pl
from jax.experimental.pallas import tpu as pltpu
from jax.sharding import PartitionSpec as P

F32, BF16 = jnp.float32, jnp.bfloat16
CHUNKS = 2
PIECES = 2
MIB = 1024 * 1024
VMEM = pl.BlockSpec(memory_space=pltpu.VMEM)
SMEM = pl.BlockSpec(memory_space=pltpu.SMEM)
ANY = pl.BlockSpec(memory_space=pl.ANY)
HBM = pl.BlockSpec(memory_space=pltpu.HBM)
ROWS_BY_ROWS = (((0,), (0,)), ((), ()))
COLUMNS_BY_COLUMNS = (((1,), (1,)), ((), ()))


def partner(index, step, count):
    if count & (count - 1) == 0:
        return index ^ step
    return (index + step) % count


def giver(index, step, count):
    if count & (count - 1) == 0:
        return index ^ step
    return (index - step) % count


def shape_of(shape, dtype):
    return jax.ShapeDtypeStruct(shape, dtype)


class Order:
    def __init__(self, core):
        self.core, self.last = core, None


def call(body, order, operands, out_shape, scratch=(), mib=4, out_specs=None, filled=(),
         marked=False):
    after = () if order.last is None else (order.last,)
    idle = len(after) + len(filled)
    plain = [
        pltpu.with_memory_space_constraint(o.array, pltpu.HBM) if isinstance(o, InHbm) else o
        for o in operands
    ]
    single = not isinstance(out_shape, (list, tuple))
    shapes = [out_shape] if single else list(out_shape)
    specs = list(out_specs) if out_specs is not None else [VMEM] * len(shapes)
    if marked:
        shapes, specs = [shape_of((8, 128), F32)] + shapes, [VMEM] + specs

    def kernel(core_ref, *refs):
        outs = refs[len(operands) + idle :]
        if marked:
            outs[0][...] = jnp.zeros((8, 128), F32)
        body(core_ref, *refs[: len(operands)], *outs[marked:])

    outs = pl.pallas_call(
        kernel,
        in_specs=[SMEM]
        + [HBM if isinstance(o, InHbm) else VMEM for o in operands]
        + [ANY] * len(after)
        + [HBM] * len(filled),
        out_specs=specs,
        out_shape=shapes,
        scratch_shapes=scratch,
        compiler_params=pltpu.CompilerParams(vmem_limit_bytes=mib * MIB),
        cost_estimate=pl.CostEstimate(flops=1, bytes_accessed=1, transcendentals=0),
        input_output_aliases={
            1 + len(operands) + len(after) + n: n + marked for n in range(len(filled))
        },
    )(order.core, *plain, *after, *filled)
    order.last = outs[0]
    outs = outs[marked:]
    return outs[0] if single else outs


class InHbm:
    def __init__(self, array):
        self.array = array


def joined(refs):
    return jnp.concatenate([ref[...] for ref in refs], axis=0)


def put(refs, value):
    rows = value.shape[0] // len(refs)
    for p, ref in enumerate(refs):
        ref[...] = value[p * rows : (p + 1) * rows].astype(ref.dtype)


def pieces_of(tokens, width):
    return [shape_of((tokens // PIECES, width), BF16)] * PIECES


def place(core_ref, side, index, chunk):
    return pl.multiple_of(((core_ref[0] ^ side) * CHUNKS + index) * chunk, chunk)


def bring(order, *weights):
    parts = 4

    def body(core_ref, *refs):
        sources, targets, sems = refs[: len(weights)], refs[len(weights) : -1], refs[-1]
        copies = []
        for k in range(len(weights)):
            high = weights[k].shape[0] // parts
            for p in range(parts):
                here = slice(p * high, (p + 1) * high)
                copies.append(
                    pltpu.make_async_copy(
                        sources[k].at[here, :], targets[k].at[here, :], sems.at[k * parts + p]
                    )
                )
                copies[-1].start()
        for copy in copies:
            copy.wait()

    return call(
        body,
        order,
        [InHbm(w) for w in weights],
        [pltpu.VMEM(w.shape, w.dtype) for w in weights],
        scratch=[pltpu.SemaphoreType.DMA((parts * len(weights),))],
        marked=True,
    )


def project(order, rows, weights, side, first, count, added, dtype, pieces=1):
    tokens = rows.shape[0]
    chunk = weights[0].shape[1] // 2 // CHUNKS
    kinds = len(weights)
    high = tokens // pieces

    def body(core_ref, x_ref, *refs):
        arrived, outs = refs[kinds:-pieces], refs[-pieces:]
        for k in range(kinds):
            for i in range(count):
                total = jnp.dot(
                    x_ref[...],
                    refs[k][:, pl.ds(place(core_ref, side, first + i, chunk), chunk)],
                    preferred_element_type=F32,
                )
                here = slice(i * chunk, (i + 1) * chunk)
                if added:
                    total += jnp.concatenate([ref[k, :, here] for ref in arrived], axis=0).astype(F32)
                for p, out in enumerate(outs):
                    out[k, :, here] = total[p * high : (p + 1) * high].astype(dtype)

    return call(
        body,
        order,
        [rows, *weights, *added],
        [shape_of((kinds, high, count * chunk), dtype)] * pieces,
    )


def activate(order, own, others, tangents, index):
    _, tokens, chunk = own.shape
    here = slice(index * chunk, (index + 1) * chunk)

    def body(core_ref, own_ref, *refs):
        arrived, t_ref = refs[: len(others)], refs[len(others)]
        tan_ref, swish_ref, slope_up_ref, *hidden_refs = refs[len(others) + 1 :]
        gate, up = own_ref[0].astype(F32), own_ref[1].astype(F32)
        for other in arrived:
            gate, up = gate + other[0].astype(F32), up + other[1].astype(F32)
        logistic = jax.nn.sigmoid(gate)
        swish = gate * logistic
        slope_up = logistic * (1.0 + gate * (1.0 - logistic)) * up
        put(hidden_refs, swish * up)
        tan_ref[...] = (slope_up * t_ref[0, :, here] + swish * t_ref[1, :, here]).astype(BF16)
        swish_ref[...] = swish
        slope_up_ref[...] = slope_up

    return call(
        body,
        order,
        [own, *others, tangents],
        [shape_of((tokens, chunk), d) for d in (BF16, F32, F32)] + pieces_of(tokens, chunk),
    )


def add_up(order, own, others):
    def body(core_ref, own_ref, *refs):
        total = own_ref[...].astype(F32)
        for other in refs[: len(others)]:
            total += other[...].astype(F32)
        put(refs[len(others) :], total)

    return call(body, order, [own, *others], pieces_of(*own.shape))


def contract(order, terms, weight, carried, groups=0):
    tokens, chunk = terms[0][0][0].shape[0] * PIECES, terms[0][0][0].shape[1]
    width = weight.shape[1]
    rows = tokens // max(groups, 1)
    count = len(terms) * PIECES
    parts = 2
    high = chunk // parts

    def body(core_ref, w_ref, *refs):
        held, sems = refs[-2:]
        copies = []
        for n, (_, side, index) in enumerate(terms):
            start = place(core_ref, side, index, chunk)
            for r in range(parts):
                m = n * parts + r
                here = pl.ds(pl.multiple_of(start + r * high, high), high)
                copies.append(pltpu.make_async_copy(w_ref.at[here, :], held.at[m], sems.at[m]))
                copies[-1].start()
        total = refs[count][...] if carried is not None else None
        for n in range(len(terms)):
            left = joined(refs[n * PIECES : (n + 1) * PIECES])
            for r in range(parts):
                m = n * parts + r
                copies[m].wait()
                term = jnp.dot(
                    left[:, r * high : (r + 1) * high], held[m], preferred_element_type=F32
                )
                total = term if total is None else total + term
        outs = refs[count + (carried is not None) : -2]
        for p, out in enumerate(outs):
            out[...] = total[p * rows : (p + 1) * rows, :].astype(out.dtype)

    out_shape = [shape_of((rows, width), BF16 if p else F32) for p in range(max(groups, 1))]
    outs = call(
        body,
        order,
        [InHbm(weight)]
        + [piece for t in terms for piece in t[0]]
        + ([carried] if carried is not None else []),
        out_shape,
        scratch=[
            pltpu.VMEM((len(terms) * parts, high, width), BF16),
            pltpu.SemaphoreType.DMA((len(terms) * parts,)),
        ],
        mib=4 + 2 * len(terms),
    )
    return outs if groups else outs[0]


def weigh(order, own, others, curvature):
    def body(core_ref, own_ref, *refs):
        total = own_ref[...]
        for other in refs[: len(others)]:
            total += other[...].astype(F32)
        refs[-1][...] = (refs[-2][...] * total).astype(BF16)

    return call(body, order, [own, *others, curvature], shape_of(own.shape, BF16))


def pull_back(order, weighted, weight, side, index, added):
    tokens, width = weighted.shape
    chunk = weight.shape[0] // 2 // CHUNKS

    def body(core_ref, x_ref, w_ref, *refs):
        total = lax.dot_general(
            x_ref[...],
            w_ref[pl.ds(place(core_ref, side, index, chunk), chunk), :],
            COLUMNS_BY_COLUMNS,
            preferred_element_type=F32,
        )
        if added is not None:
            total += refs[0][...].astype(F32)
        refs[-1][...] = total.astype(BF16)

    return call(
        body,
        order,
        [weighted, weight] + ([added] if added is not None else []),
        shape_of((tokens, chunk), BF16),
    )


def cotangents(order, own, others, swish, slope_up):
    def body(core_ref, own_ref, *refs):
        back = own_ref[...].astype(F32)
        for other in refs[: len(others)]:
            back += other[...].astype(F32)
        swish_ref, slope_up_ref, *outs = refs[len(others) :]
        put(outs[:PIECES], back * slope_up_ref[...])
        put(outs[PIECES:], back * swish_ref[...])

    return call(body, order, [own, *others, swish, slope_up], pieces_of(*own.shape) * 2)


def outer_down(order, hiddens, weighted, filled):
    tokens, width = weighted.shape
    chunk = hiddens[0][0][0].shape[1]
    count = len(hiddens)
    high = max(chunk // 4, 16)
    parts = chunk // high

    def body(core_ref, *refs):
        x_ref, out, held, sems = refs[count * PIECES :]
        copies = []
        for m, (_, side, index) in enumerate(hiddens):
            hidden = joined(refs[m * PIECES : (m + 1) * PIECES])
            start = place(core_ref, side, index, chunk)
            for r in range(parts):
                n = m * parts + r
                held[n] = lax.dot_general(
                    hidden[:, r * high : (r + 1) * high],
                    x_ref[...],
                    ROWS_BY_ROWS,
                    preferred_element_type=F32,
                ).astype(BF16)
                there = pl.ds(pl.multiple_of(start + r * high, high), high)
                copies.append(
                    pltpu.make_async_copy(held.at[n], out.at[there, :], sems.at[n])
                )
                copies[-1].start()
        for copy in copies:
            copy.wait()

    return call(
        body,
        order,
        [piece for h in hiddens for piece in h[0]] + [weighted],
        [pltpu.HBM((2 * CHUNKS * chunk, width), BF16)],
        scratch=[
            pltpu.VMEM((count * parts, high, width), BF16),
            pltpu.SemaphoreType.DMA((count * parts,)),
        ],
        mib=12,
        out_specs=[HBM],
        filled=filled,
        marked=True,
    )


def outer_pair(order, rows, terms, hidden_units, filled):
    depth, chunk = rows.shape[1], terms[0][0][0].shape[1]
    high = min(256, depth)
    parts = depth // high
    count = len(terms)

    def body(core_ref, x_ref, *refs):
        *pieces, gate_out, up_out, held, sems = refs
        copies = []
        for t, (_, side, index) in enumerate(terms):
            columns = pl.ds(place(core_ref, side, index, chunk), chunk)
            for k, out in enumerate((gate_out, up_out)):
                n = t * 2 + k
                back = joined(pieces[n * PIECES : (n + 1) * PIECES])
                for r in range(parts):
                    m = n * parts + r
                    held[m] = lax.dot_general(
                        x_ref[:, r * high : (r + 1) * high],
                        back,
                        ROWS_BY_ROWS,
                        preferred_element_type=F32,
                    ).astype(BF16)
                    copies.append(
                        pltpu.make_async_copy(
                            held.at[m], out.at[r * high : (r + 1) * high, columns], sems.at[m]
                        )
                    )
                    copies[-1].start()
        for copy in copies:
            copy.wait()

    return call(
        body,
        order,
        [rows] + [piece for t in terms for piece in t[0]],
        [pltpu.HBM((depth, hidden_units), BF16)] * 2,
        scratch=[
            pltpu.VMEM((2 * count * parts, high, chunk), BF16),
            pltpu.SemaphoreType.DMA((2 * count * parts,)),
        ],
        mib=4 + 4 * count,
        out_specs=[HBM, HBM],
        filled=filled,
        marked=True,
    )


def per_device(
    sizes,
    tokens,
    curvature,
    gate_weight,
    up_weight,
    down_weight,
    gate_vector,
    up_vector,
    down_vector,
):
    groups, chips = sizes["dp"], sizes["mp"] // 2
    hidden_units = gate_weight.shape[1]
    group_rows = tokens.shape[0]
    order = Order(lax.rem(lax.axis_index("mp"), 2).astype(jnp.int32)[None])
    mine = lax.dynamic_slice(curvature, (lax.axis_index("dp") * group_rows,), (group_rows,))[:, None]
    def over_dp(value, step):
        return lax.ppermute(value, "dp", [(i, partner(i, step, groups)) for i in range(groups)])

    def back_over_dp(value, step):
        return lax.ppermute(value, "dp", [(i, giver(i, step, groups)) for i in range(groups)])

    def to_core(value):
        return lax.ppermute(value, "mp", [(i, i ^ 1) for i in range(2 * chips)])

    def over_chips(value):
        return [
            lax.ppermute(
                value,
                "mp",
                [(2 * i + c, 2 * partner(i, k, chips) + c) for i in range(chips) for c in range(2)],
            )
            for k in range(1, chips)
        ]

    primal = bring(order, gate_weight, up_weight)
    rows = jnp.concatenate([tokens] + [over_dp(tokens, p) for p in range(1, groups)], axis=0)
    sent = [project(order, rows, primal, 1, i, 1, [], BF16) for i in range(CHUNKS)]
    sent = [[to_core(piece) for piece in s] for s in sent]
    sums = [project(order, rows, primal, 0, i, 1, sent[i], BF16)[0] for i in range(CHUNKS)]
    others = [over_chips(s) for s in sums]
    probe = bring(order, gate_vector, up_vector)
    sent = [to_core(piece) for piece in project(order, rows, probe, 1, 0, CHUNKS, [], BF16, 3)]
    (tangents,) = project(order, rows, probe, 0, 0, CHUNKS, sent, F32)

    acted = [activate(order, sums[i], others[i], tangents, i) for i in range(CHUNKS)]
    tan_others = [over_chips(a[0]) for a in acted]
    hidden = [(a[3:], 0, i) for i, a in enumerate(acted)]
    hidden_other = [([to_core(piece) for piece in h[0]], 1, h[2]) for h in hidden]
    carried = contract(order, hidden + hidden_other, down_vector, None)
    for i in range(CHUNKS):
        last = i == CHUNKS - 1
        hidden_tan = add_up(order, acted[i][0], tan_others[i])
        tan_other = [to_core(piece) for piece in hidden_tan]
        terms = [(hidden_tan, 0, i), (tan_other, 1, i)]
        if not last:
            carried = contract(order, terms, down_weight, carried)
        else:
            carried = contract(order, terms[:1], down_weight, carried)
            carried = contract(order, terms[1:], down_weight, carried, groups)
    (brought,) = bring(order, down_weight)
    weighted_mine = weigh(
        order, carried[0], [back_over_dp(carried[p], p) for p in range(1, groups)], mine
    )
    weighted = jnp.concatenate(
        [weighted_mine] + [over_dp(weighted_mine, p) for p in range(1, groups)], axis=0
    )

    sent = [to_core(pull_back(order, weighted, brought, 1, i, None)) for i in range(CHUNKS)]
    sums, fisher_down, filled = [], (), ()
    for i in range(CHUNKS):
        sums.append(pull_back(order, weighted, brought, 0, i, sent[i]))
        if i == 0:
            fisher_down = outer_down(order, hidden, weighted, fisher_down)
    fisher_down = outer_down(order, hidden_other, weighted, fisher_down)
    others = [over_chips(s) for s in sums]
    for i in range(CHUNKS):
        backs = cotangents(order, sums[i], others[i], acted[i][1], acted[i][2])
        backs_other = [to_core(piece) for piece in backs]
        terms = [(backs, 0, i), (backs_other, 1, i)]
        if i == 0:
            filled = outer_pair(order, rows, terms, hidden_units, filled)
        else:
            filled = outer_pair(order, rows, terms[:1], hidden_units, filled)
            filled = outer_pair(order, rows, terms[1:], hidden_units, filled)
    return (filled[0], filled[1], fisher_down[0])


def solution(mesh):
    placed = (
        P(("parts", "dp"), "mp"),
        P("parts"),
        P("mp", "dp"),
        P("mp", "dp"),
        P("dp", "mp"),
        P(("parts", "mp"), "dp"),
        P(("parts", "mp"), "dp"),
        P(("parts", "dp"), "mp"),
    )
    return jax.shard_map(
        functools.partial(per_device, dict(mesh.shape)),
        mesh=mesh,
        in_specs=placed,
        out_specs=(P(("parts", "mp"), "dp"), P(("parts", "mp"), "dp"), P(("parts", "dp"), "mp")),
        check_vma=False,
    )
```

time: 246 us -> 94.1 us (0.38)
  waiting for transfers between devices: 133 us -> 13.3 us
  matrix products: 55.1 us -> 0 us
  Pallas kernels: 0 us -> 49.7 us
  starting transfers between devices: 0.3 us -> 28.6 us
  local copies, waits for them, and re-layouts: 23.9 us -> 1.06 us
  blocking collectives: 15.7 us -> 0 us
  between operations: 13.8 us -> 1.2 us
  other arithmetic: 2.87 us -> 0.01 us
    psum x3 -> x0, waiting for transfers between devices: 133 us -> none  [the longest x1 69.8 us: per_device(): summed = lax.psum(partials.astype(jnp.bfloat16), 'mp').astype(jnp.float32)]
    dot_general x7 -> x0, matrix products: 55.1 us -> none  [the longest x1 17.1 us: per_device(): partials = jnp.dot(gathered, stacked, preferred_element_type=jnp.float32)]
    pallas_call x0 -> x29, Pallas kernels: none -> 49.7 us  [call(): pl.pallas_call(kernel, in_specs=[SMEM] + [HBM if isinstance(o, InHbm) els...]
    ppermute x0 -> x38, starting transfers between devices: none -> 28.6 us  [the longest x6 10.1 us: over_dp(): lax.ppermute(value, 'dp', [(i, partner(i, step, groups)) for i in range(g...]
    unnamed x14 -> x5, local copies, waits for them, and re-layouts: 23.9 us -> 0.89 us
    all_gather x1 -> x0, blocking collectives: 15.7 us -> none  [per_device(): gathered = lax.all_gather(tokens, 'dp', axis=0, tiled=True)]
    ppermute x0 -> x38, waiting for transfers between devices: none -> 13.3 us  [the longest x23 4.32 us: to_core(): return lax.ppermute(value, 'mp', [(i, i ^ 1) for i in range(2 * chips)])]
    convert_element_type x2 -> x0, other arithmetic: 2.87 us -> none  [the longest x1 2.45 us: per_device(): summed = lax.psum(partials.astype(jnp.bfloat16), 'mp').astype(jnp.float32)]
  transfers between devices with their start and end apart: 3 -> 38, of which waited for: 3 -> 16; matrix products, arithmetic and copies ran while one was open for 2% -> 1% of each run, Pallas kernels for 0% -> 46%
where the time goes in v2:
time: 94.1 us; the launch traced here: 93.9 us
  Pallas kernels  49.7 us (53%)
  starting transfers between devices  28.6 us (30%)
  waiting for transfers between devices  13.3 us (14%)
  between operations  1.2 us (1%)
  local copies, waits for them, and re-layouts  1.06 us (1%)
    pallas_call x29, Pallas kernels, call(): pl.pallas_call(kernel, in_specs=[SMEM] + [HBM if isinstance(o, InHbm) els...  49.7 us
    ppermute x6, starting transfers between devices, over_dp(): lax.ppermute(value, 'dp', [(i, partner(i, step, groups)) for i in range(g...  10.1 us
    ppermute x6, starting transfers between devices, over_chips(): lax.ppermute(value, 'mp', [(2 * i + c, 2 * partner(i, k, chips) + c) for...  7.74 us
    ppermute x23, starting transfers between devices, to_core(): return lax.ppermute(value, 'mp', [(i, i ^ 1) for i in range(2 * chips)])  6.27 us
    ppermute x3, starting transfers between devices, back_over_dp(): lax.ppermute(value, 'dp', [(i, giver(i, step, groups)) for i in range(gro...  4.47 us
    ppermute x23, waiting for transfers between devices, to_core(): return lax.ppermute(value, 'mp', [(i, i ^ 1) for i in range(2 * chips)])  4.32 us
    ppermute x6, waiting for transfers between devices, over_chips(): lax.ppermute(value, 'mp', [(2 * i + c, 2 * partner(i, k, chips) + c) for...  4.19 us
    ppermute x6, waiting for transfers between devices, over_dp(): lax.ppermute(value, 'dp', [(i, partner(i, step, groups)) for i in range(g...  2.84 us
  transfers between devices with their start and end apart: 38, of which 16 were waited for; matrix products, arithmetic and copies ran while one was open for 1% of the time, Pallas kernels for 46%

profile of v2, /device:TPU:0, one launch (start us, length us, event | category | flops | bytes accessed | tf_op | source)
XLA Modules:
  0.0 93.9 jit_solution(5417392120630599522)
XLA Ops:
  0.6 4.1 %collective-permute-start.1 = (bf16[24,1024]{1,0:T(8,128)(2,1)}, bf16[24,1024]{1,0:T(8,128)(2,1)S(1)}, u32[]{:S(2)}, u32[]{:S(2)}) collective-permute-start(bf16[24,1024]{1,0:T(8,128)(2,1)} %param.8), channel_id=1, source_target_pairs={{0,8},{4,12},{8,0},{12,4},{1,9},{5,13},{9,1},{13,5},{2,10},{6,14},... | collective-permute-start | bytes 147464 | tf_op jit(solution)/shard_map/ppermute | solution.py:403
  4.7 1.6 %collective-permute-start = (bf16[24,1024]{1,0:T(8,128)(2,1)}, bf16[24,1024]{1,0:T(8,128)(2,1)S(1)}, u32[]{:S(2)}, u32[]{:S(2)}) collective-permute-start(bf16[24,1024]{1,0:T(8,128)(2,1)} %param.8), channel_id=1, source_target_pairs={{0,4},{4,0},{8,12},{12,8},{1,5},{5,1},{9,13},{13,9},{2,6},{6,2},{1... | collective-permute-start | bytes 147464 | tf_op jit(solution)/shard_map/ppermute | solution.py:403
  6.3 0.9 constant_dynamic-update-slice_fusion.3
  7.2 5.9 %shard_map.103 = (f32[8,128]{1,0:T(8,128)S(1)}, bf16[1024,4096]{1,0:T(8,128)(2,1)S(1)}, bf16[1024,4096]{1,0:T(8,128)(2,1)S(1)}) custom-call(s32[1]{0:T(128)} %bitcast.core_ref, bf16[1024,4096]{1,0:T(8,128)(2,1)} %refs_0_.7, bf16[1024,4096]{1,0:T(8,128)(2,1)} %refs_1_.2), custom_call_target="tpu_custom_call" | custom-call | flops 1 | bytes 1 | tf_op jit(solution)/shard_map/pallas_call | solution.py:63
  15.8 0.8 shard_map.106.refs_4_.refs_0_
  16.6 1.7 %collective-permute-start.9 = (bf16[2,96,1024]{2,1,0:T(8,128)(2,1)S(1)}, bf16[2,96,1024]{2,1,0:T(8,128)(2,1)S(1)}, u32[]{:S(2)}, u32[]{:S(2)}) collective-permute-start(bf16[2,96,1024]{2,1,0:T(8,128)(2,1)S(1)} %shard_map.106.refs_4_.refs_0_), channel_id=1, source_target_pairs={{0,2},{1,3},{2,0},{3,1},{4,6},{5,7},{6,4},{7,5},{8,10},{9,11},{10,... | collective-permute-start | bytes 1179656 | tf_op jit(solution)/shard_map/ppermute | solution.py:413
  18.4 0.8 shard_map.107.refs_2_.refs_0_
  19.6 5.9 %shard_map.108 = (f32[8,128]{1,0:T(8,128)S(1)}, bf16[1024,4096]{1,0:T(8,128)(2,1)S(1)}, bf16[1024,4096]{1,0:T(8,128)(2,1)S(1)}) custom-call(s32[1]{0:T(128)} %bitcast.core_ref, bf16[1024,4096]{1,0:T(8,128)(2,1)} %refs_0_.8, bf16[1024,4096]{1,0:T(8,128)(2,1)} %refs_1_.3, bf16[2,96,1024]{2,1,0:T(8,128)(2,1)S(1)} %shard_map.107.refs_2_.refs_0_), custom_call_target="tpu_custom_call" | custom-call | flops 1 | bytes 1 | tf_op jit(solution)/shard_map/pallas_call | solution.py:63
  25.5 1.5 %shard_map.109 = (bf16[2,32,2048]{2,1,0:T(8,128)(2,1)S(1)}, bf16[2,32,2048]{2,1,0:T(8,128)(2,1)S(1)}, bf16[2,32,2048]{2,1,0:T(8,128)(2,1)S(1)}) custom-call(s32[1]{0:T(128)} %bitcast.core_ref, bf16[96,1024]{1,0:T(8,128)(2,1)S(1)} %constant_dynamic-update-slice_fusion.refs_0_, bf16[1024,4096]{1,0:T(8,128)(2,1)S(1)} %get-tuple-element.55.refs_1_, ...), custom_call_target="tpu_custom_call" | custom-call | flops 1 | bytes 1 | tf_op jit(solution)/shard_map/pallas_call | solution.py:63
  27.6 0.9 %collective-permute-done.7.refs_4_ = bf16[2,32,2048]{2,1,0:T(8,128)(2,1)S(1)} collective-permute-done((bf16[2,32,2048]{2,1,0:T(8,128)(2,1)S(1)}, bf16[2,32,2048]{2,1,0:T(8,128)(2,1)S(1)}, u32[]{:S(2)}, u32[]{:S(2)}) %collective-permute-start.7) | collective-permute-done | bytes 262176 | tf_op jit(solution)/shard_map/ppermute | solution.py:409
  29.3 1.5 %shard_map.110.refs_2_.refs_3_ = f32[2,96,2048]{2,1,0:T(8,128)S(1)} custom-call(s32[1]{0:T(128)} %bitcast.core_ref, bf16[96,1024]{1,0:T(8,128)(2,1)S(1)} %constant_dynamic-update-slice_fusion.refs_0_, bf16[1024,4096]{1,0:T(8,128)(2,1)S(1)} %get-tuple-element.55.refs_1_, bf16[1024,4096]{1,0:T(8,128)(2,1)S(1)} %get-tuple-element.56.refs_2_, ...), custom_call_target="tpu_custom_call" | custom-call | flops 1 | bytes 1 | tf_op jit(solution)/shard_map/pallas_call | solution.py:63
  31.1 1.7 %collective-permute-start.11 = (bf16[96,1024]{1,0:T(8,128)(2,1)S(1)}, bf16[96,1024]{1,0:T(8,128)(2,1)S(1)}, u32[]{:S(2)}, u32[]{:S(2)}) collective-permute-start(bf16[96,1024]{1,0:T(8,128)(2,1)S(1)} %get-tuple-element.61.refs_3_.refs_0_), channel_id=1, source_target_pairs={{0,2},{1,3},{2,0},{3,1},{4,6},{5,7},{6,4},{7,5},{8,10},{9,11},{10,... | collective-permute-start | bytes 589832 | tf_op jit(solution)/shard_map/ppermute | solution.py:413
  32.9 4.2 %collective-permute-done.5.refs_1_ = bf16[2,96,1024]{2,1,0:T(8,128)(2,1)S(1)} collective-permute-done((bf16[2,96,1024]{2,1,0:T(8,128)(2,1)S(1)}, bf16[2,96,1024]{2,1,0:T(8,128)(2,1)S(1)}, u32[]{:S(2)}, u32[]{:S(2)}) %collective-permute-start.5) | collective-permute-done | bytes 393248 | tf_op jit(solution)/shard_map/ppermute | solution.py:413
  38.8 1.7 %collective-permute-start.10 = (bf16[96,1024]{1,0:T(8,128)(2,1)S(1)}, bf16[96,1024]{1,0:T(8,128)(2,1)S(1)}, u32[]{:S(2)}, u32[]{:S(2)}) collective-permute-start(bf16[96,1024]{1,0:T(8,128)(2,1)S(1)} %get-tuple-element.62.refs_9_.refs_0_), channel_id=1, source_target_pairs={{0,2},{1,3},{2,0},{3,1},{4,6},{5,7},{6,4},{7,5},{8,10},{9,11},{10,... | collective-permute-start | bytes 589832 | tf_op jit(solution)/shard_map/ppermute | solution.py:413
  40.4 3.8 %shard_map.113.refs_2_.refs_5_ = f32[96,1024]{1,0:T(8,128)S(1)} custom-call(s32[1]{0:T(128)} %bitcast.core_ref, bf16[4096,1024]{1,0:T(8,128)(2,1)} %refs_0_.9, bf16[48,1024]{1,0:T(8,128)(2,1)S(1)} %get-tuple-element.63.refs_1_.refs_0_, bf16[48,1024]{1,0:T(8,128)(2,1)S(1)} %get-tuple-element.64.refs_2_.refs_1_, ...), custom_call_target="tpu_custom_call" | custom-call | flops 1 | bytes 1 | tf_op jit(solution)/shard_map/pallas_call | solution.py:63
  45.8 2.5 %shard_map.115.refs_2_.refs_3_ = f32[96,1024]{1,0:T(8,128)S(1)} custom-call(s32[1]{0:T(128)} %bitcast.core_ref, bf16[4096,1024]{1,0:T(8,128)(2,1)} %refs_0_.13, bf16[48,1024]{1,0:T(8,128)(2,1)S(1)} %get-tuple-element.67.refs_1_.refs_6_, bf16[48,1024]{1,0:T(8,128)(2,1)S(1)} %get-tuple-element.68.refs_2_, ...), custom_call_target="tpu_custom_call" | custom-call | flops 1 | bytes 1 | tf_op jit(solution)/shard_map/pallas_call | solution.py:63
  49.0 1.9 %shard_map.117.refs_3_.refs_4_ = f32[96,1024]{1,0:T(8,128)S(1)} custom-call(s32[1]{0:T(128)} %bitcast.core_ref, bf16[4096,1024]{1,0:T(8,128)(2,1)} %refs_0_.13, bf16[48,1024]{1,0:T(8,128)(2,1)S(1)} %get-tuple-element.69.refs_1_.refs_4_, bf16[48,1024]{1,0:T(8,128)(2,1)S(1)} %get-tuple-element.70.refs_2_, f32[96,1024]{1,0:T(8,128)S(1)} %shard_map.115.refs_2_.refs_3_, ...), custom_call_target="tpu_custom_call" | custom-call | flops 1 | bytes 1 | tf_op jit(solution)/shard_map/pallas_call | solution.py:63
  50.9 1.9 %shard_map.118 = (f32[24,1024]{1,0:T(8,128)S(1)}, bf16[24,1024]{1,0:T(8,128)(2,1)S(1)}, bf16[24,1024]{1,0:T(8,128)(2,1)S(1)}, bf16[24,1024]{1,0:T(8,128)(2,1)S(1)}) custom-call(s32[1]{0:T(128)} %bitcast.core_ref, bf16[4096,1024]{1,0:T(8,128)(2,1)} %refs_0_.13, bf16[48,1024]{1,0:T(8,128)(2,1)S(1)} %collective-permute-done.18.refs_1_, ...), custom_call_target="tpu_custom_call" | custom-call | flops 1 | bytes 1 | tf_op jit(solution)/shard_map/pallas_call | solution.py:63
  53.5 3.5 %collective-permute-start.21 = (bf16[24,1024]{1,0:T(8,128)(2,1)S(1)}, bf16[24,1024]{1,0:T(8,128)(2,1)S(1)}, u32[]{:S(2)}, u32[]{:S(2)}) collective-permute-start(bf16[24,1024]{1,0:T(8,128)(2,1)S(1)} %get-tuple-element.73), channel_id=1, source_target_pairs={{0,8},{4,12},{8,0},{12,4},{1,9},{5,13},{9,1},{13,5},{2,10},{6,14},... | collective-permute-start | bytes 147464 | tf_op jit(solution)/shard_map/ppermute | solution.py:406
  57.4 3.5 %shard_map.119 = (f32[8,128]{1,0:T(8,128)S(1)}, bf16[4096,1024]{1,0:T(8,128)(2,1)S(1)}) custom-call(s32[1]{0:T(128)} %bitcast.core_ref, bf16[4096,1024]{1,0:T(8,128)(2,1)} %refs_0_.13, f32[24,1024]{1,0:T(8,128)S(1)} %get-tuple-element.71.refs_1_.refs_0_), custom_call_target="tpu_custom_call" | custom-call | flops 1 | bytes 1 | tf_op jit(solution)/shard_map/pallas_call | solution.py:63
  61.0 2.0 %collective-permute-done.22.refs_3_ = bf16[24,1024]{1,0:T(8,128)(2,1)S(1)} collective-permute-done((bf16[24,1024]{1,0:T(8,128)(2,1)S(1)}, bf16[24,1024]{1,0:T(8,128)(2,1)S(1)}, u32[]{:S(2)}, u32[]{:S(2)}) %collective-permute-start.22) | collective-permute-done | bytes 49184 | tf_op jit(solution)/shard_map/ppermute | solution.py:406
  63.0 1.7 %collective-permute-start.25 = (bf16[24,1024]{1,0:T(8,128)(2,1)S(1)}, bf16[24,1024]{1,0:T(8,128)(2,1)S(1)}, u32[]{:S(2)}, u32[]{:S(2)}) collective-permute-start(bf16[24,1024]{1,0:T(8,128)(2,1)S(1)} %shard_map.120.refs_2_), channel_id=1, source_target_pairs={{0,12},{4,8},{8,4},{12,0},{1,13},{5,9},{9,5},{13,1},{2,14},{6,10},... | collective-permute-start | bytes 147464 | tf_op jit(solution)/shard_map/ppermute | solution.py:403
  64.7 2.7 %collective-permute-start.23 = (bf16[24,1024]{1,0:T(8,128)(2,1)S(1)}, bf16[24,1024]{1,0:T(8,128)(2,1)S(1)}, u32[]{:S(2)}, u32[]{:S(2)}) collective-permute-start(bf16[24,1024]{1,0:T(8,128)(2,1)S(1)} %shard_map.120.refs_2_), channel_id=1, source_target_pairs={{0,4},{4,0},{8,12},{12,8},{1,5},{5,1},{9,13},{13,9},{2,6},{6,2},{1... | collective-permute-start | bytes 147464 | tf_op jit(solution)/shard_map/ppermute | solution.py:403
  67.4 1.9 %collective-permute-done.25 = bf16[24,1024]{1,0:T(8,128)(2,1)S(1)} collective-permute-done((bf16[24,1024]{1,0:T(8,128)(2,1)S(1)}, bf16[24,1024]{1,0:T(8,128)(2,1)S(1)}, u32[]{:S(2)}, u32[]{:S(2)}) %collective-permute-start.25) | collective-permute-done | bytes 49184 | tf_op jit(solution)/shard_map/ppermute | solution.py:403
  69.3 0.9 collective-permute-done.24
  73.3 1.0 %collective-permute-start.29 = (bf16[96,1024]{1,0:T(8,128)(2,1)S(1)}, bf16[96,1024]{1,0:T(8,128)(2,1)S(1)}, u32[]{:S(2)}, u32[]{:S(2)}) collective-permute-start(bf16[96,1024]{1,0:T(8,128)(2,1)S(1)} %shard_map.123.refs_5_.refs_0_), channel_id=1, source_target_pairs={{0,2},{1,3},{2,0},{3,1},{4,6},{5,7},{6,4},{7,5},{8,10},{9,11},{10,... | collective-permute-start | bytes 589832 | tf_op jit(solution)/shard_map/ppermute | solution.py:413
  74.3 2.5 %shard_map.124 = (f32[8,128]{1,0:T(8,128)S(1)}, bf16[4096,1024]{1,0:T(8,128)(2,1)}) custom-call(s32[1]{0:T(128)} %bitcast.core_ref, bf16[48,1024]{1,0:T(8,128)(2,1)S(1)} %get-tuple-element.63.refs_1_.refs_0_, bf16[48,1024]{1,0:T(8,128)(2,1)S(1)} %get-tuple-element.64.refs_2_.refs_1_, bf16[48,1024]{1,0:T(8,128)(2,1)S(1)} %get-tuple-element.65.refs_3_.refs_2_, ...), custom_call_target="tpu_custom_call" | custom-call | flops 1 | bytes 1 | tf_op jit(solution)/shard_map/pallas_call | solution.py:63
  77.7 1.2 %collective-permute-start.28 = (bf16[96,1024]{1,0:T(8,128)(2,1)S(1)}, bf16[96,1024]{1,0:T(8,128)(2,1)S(1)}, u32[]{:S(2)}, u32[]{:S(2)}) collective-permute-start(bf16[96,1024]{1,0:T(8,128)(2,1)S(1)} %shard_map.125.refs_5_.refs_0_), channel_id=1, source_target_pairs={{0,2},{1,3},{2,0},{3,1},{4,6},{5,7},{6,4},{7,5},{8,10},{9,11},{10,... | collective-permute-start | bytes 589832 | tf_op jit(solution)/shard_map/ppermute | solution.py:413
  78.8 2.4 %shard_map.126 = (f32[8,128]{1,0:T(8,128)S(1)}, bf16[4096,1024]{1,0:T(8,128)(2,1)}) custom-call(s32[1]{0:T(128)} %bitcast.core_ref, bf16[48,1024]{1,0:T(8,128)(2,1)S(1)} %collective-permute-done.12.refs_5_.refs_0_, bf16[48,1024]{1,0:T(8,128)(2,1)S(1)} %collective-permute-done.13.refs_6_.refs_1_, ...), custom_call_target="tpu_custom_call", output_to_operand_aliasing={{1}: (7, {})} | custom-call | flops 1 | bytes 1 | tf_op jit(solution)/shard_map/pallas_call | solution.py:63
  83.4 3.7 %shard_map.128 = (f32[8,128]{1,0:T(8,128)S(1)}, bf16[1024,4096]{1,0:T(8,128)(2,1)}, bf16[1024,4096]{1,0:T(8,128)(2,1)}) custom-call(s32[1]{0:T(128)} %bitcast.core_ref, bf16[96,1024]{1,0:T(8,128)(2,1)S(1)} %constant_dynamic-update-slice_fusion.refs_0_, bf16[48,1024]{1,0:T(8,128)(2,1)S(1)} %get-tuple-element.84.refs_1_.refs_9_, ...), custom_call_target="tpu_custom_call" | custom-call | flops 1 | bytes 1 | tf_op jit(solution)/shard_map/pallas_call | solution.py:63
  88.3 2.4 %shard_map.130 = (f32[8,128]{1,0:T(8,128)S(1)}, bf16[1024,4096]{1,0:T(8,128)(2,1)}, bf16[1024,4096]{1,0:T(8,128)(2,1)}) custom-call(s32[1]{0:T(128)} %bitcast.core_ref, bf16[96,1024]{1,0:T(8,128)(2,1)S(1)} %constant_dynamic-update-slice_fusion.refs_0_, ...), custom_call_target="tpu_custom_call", output_to_operand_aliasing={{1}: (7, {}), {2}: (8, {})} | custom-call | flops 1 | bytes 1 | tf_op jit(solution)/shard_map/pallas_call | solution.py:63
  90.7 3.0 %shard_map.131 = (f32[8,128]{1,0:T(8,128)}, bf16[1024,4096]{1,0:T(8,128)(2,1)}, bf16[1024,4096]{1,0:T(8,128)(2,1)}) custom-call(s32[1]{0:T(128)} %bitcast.core_ref, bf16[96,1024]{1,0:T(8,128)(2,1)S(1)} %constant_dynamic-update-slice_fusion.refs_0_, ...), custom_call_target="tpu_custom_call", output_to_operand_aliasing={{1}: (7, {}), {2}: (8, {})} | custom-call | flops 1 | bytes 1 | tf_op jit(solution)/shard_map/pallas_call | solution.py:63
  (82 shorter events, 17.0 us)
Async XLA Ops:
  0.6 12.5 %collective-permute-start.1 = (bf16[24,1024]{1,0:T(8,128)(2,1)}, bf16[24,1024]{1,0:T(8,128)(2,1)S(1)}, u32[]{:S(2)}, u32[]{:S(2)}) collective-permute-start(bf16[24,1024]{1,0:T(8,128)(2,1)} %param.8), channel_id=1, source_target_pairs={{0,8},{4,12},{8,0},{12,4},{1,9},{5,13},{9,1},{13,5},{2,10},{6,14},... | collective-permute-start | bytes 147464 | tf_op jit(solution)/shard_map/ppermute | solution.py:403
  4.7 8.4 %collective-permute-start = (bf16[24,1024]{1,0:T(8,128)(2,1)}, bf16[24,1024]{1,0:T(8,128)(2,1)S(1)}, u32[]{:S(2)}, u32[]{:S(2)}) collective-permute-start(bf16[24,1024]{1,0:T(8,128)(2,1)} %param.8), channel_id=1, source_target_pairs={{0,4},{4,0},{8,12},{12,8},{1,5},{5,1},{9,13},{13,9},{2,6},{6,2},{1... | collective-permute-start | bytes 147464 | tf_op jit(solution)/shard_map/ppermute | solution.py:403
  6.3 6.9 %collective-permute-start.2 = (bf16[24,1024]{1,0:T(8,128)(2,1)}, bf16[24,1024]{1,0:T(8,128)(2,1)S(1)}, u32[]{:S(2)}, u32[]{:S(2)}) collective-permute-start(bf16[24,1024]{1,0:T(8,128)(2,1)} %param.8), channel_id=1, source_target_pairs={{0,12},{4,8},{8,4},{12,0},{1,13},{5,9},{9,5},{13,1},{2,14},{6,10},... | collective-permute-start | bytes 147464 | tf_op jit(solution)/shard_map/ppermute | solution.py:403
  14.0 1.8 %collective-permute-start.4 = (bf16[2,96,1024]{2,1,0:T(8,128)(2,1)S(1)}, bf16[2,96,1024]{2,1,0:T(8,128)(2,1)S(1)}, u32[]{:S(2)}, u32[]{:S(2)}) collective-permute-start(bf16[2,96,1024]{2,1,0:T(8,128)(2,1)S(1)} %shard_map.104.refs_3_), channel_id=1, source_target_pairs={{0,1},{1,0},{2,3},{3,2},{4,5},{5,4},{6,7},{7,6},{8,9},{9,8},{10,11... | collective-permute-start | bytes 1179656 | tf_op jit(solution)/shard_map/ppermute | solution.py:409
  14.9 3.5 %collective-permute-start.3 = (bf16[2,96,1024]{2,1,0:T(8,128)(2,1)S(1)}, bf16[2,96,1024]{2,1,0:T(8,128)(2,1)S(1)}, u32[]{:S(2)}, u32[]{:S(2)}) collective-permute-start(bf16[2,96,1024]{2,1,0:T(8,128)(2,1)S(1)} %shard_map.105.refs_4_), channel_id=1, source_target_pairs={{0,1},{1,0},{2,3},{3,2},{4,5},{5,4},{6,7},{7,6},{8,9},{9,8},{10,11... | collective-permute-start | bytes 1179656 | tf_op jit(solution)/shard_map/ppermute | solution.py:409
  16.6 14.2 %collective-permute-start.9 = (bf16[2,96,1024]{2,1,0:T(8,128)(2,1)S(1)}, bf16[2,96,1024]{2,1,0:T(8,128)(2,1)S(1)}, u32[]{:S(2)}, u32[]{:S(2)}) collective-permute-start(bf16[2,96,1024]{2,1,0:T(8,128)(2,1)S(1)} %shard_map.106.refs_4_.refs_0_), channel_id=1, source_target_pairs={{0,2},{1,3},{2,0},{3,1},{4,6},{5,7},{6,4},{7,5},{8,10},{9,11},{10,... | collective-permute-start | bytes 1179656 | tf_op jit(solution)/shard_map/ppermute | solution.py:413
  19.2 17.9 %collective-permute-start.5 = (bf16[2,96,1024]{2,1,0:T(8,128)(2,1)S(1)}, bf16[2,96,1024]{2,1,0:T(8,128)(2,1)S(1)}, u32[]{:S(2)}, u32[]{:S(2)}) collective-permute-start(bf16[2,96,1024]{2,1,0:T(8,128)(2,1)S(1)} %shard_map.107.refs_2_.refs_0_), channel_id=1, source_target_pairs={{0,2},{1,3},{2,0},{3,1},{4,6},{5,7},{6,4},{7,5},{8,10},{9,11},{10,... | collective-permute-start | bytes 1179656 | tf_op jit(solution)/shard_map/ppermute | solution.py:413
  27.0 1.6 %collective-permute-start.7 = (bf16[2,32,2048]{2,1,0:T(8,128)(2,1)S(1)}, bf16[2,32,2048]{2,1,0:T(8,128)(2,1)S(1)}, u32[]{:S(2)}, u32[]{:S(2)}) collective-permute-start(bf16[2,32,2048]{2,1,0:T(8,128)(2,1)S(1)} %get-tuple-element.59), channel_id=1, source_target_pairs={{0,1},{1,0},{2,3},{3,2},{4,5},{5,4},{6,7},{7,6},{8,9},{9,8},{10,11... | collective-permute-start | bytes 786440 | tf_op jit(solution)/shard_map/ppermute | solution.py:409
  27.1 1.9 %collective-permute-start.8 = (bf16[2,32,2048]{2,1,0:T(8,128)(2,1)S(1)}, bf16[2,32,2048]{2,1,0:T(8,128)(2,1)S(1)}, u32[]{:S(2)}, u32[]{:S(2)}) collective-permute-start(bf16[2,32,2048]{2,1,0:T(8,128)(2,1)S(1)} %get-tuple-element.60), channel_id=1, source_target_pairs={{0,1},{1,0},{2,3},{3,2},{4,5},{5,4},{6,7},{7,6},{8,9},{9,8},{10,11... | collective-permute-start | bytes 786440 | tf_op jit(solution)/shard_map/ppermute | solution.py:409
  27.6 1.8 %collective-permute-start.6 = (bf16[2,32,2048]{2,1,0:T(8,128)(2,1)S(1)}, bf16[2,32,2048]{2,1,0:T(8,128)(2,1)S(1)}, u32[]{:S(2)}, u32[]{:S(2)}) collective-permute-start(bf16[2,32,2048]{2,1,0:T(8,128)(2,1)S(1)} %get-tuple-element.58.refs_6_), channel_id=1, source_target_pairs={{0,1},{1,0},{2,3},{3,2},{4,5},{5,4},{6,7},{7,6},{8,9},{9,8},{10,11... | collective-permute-start | bytes 786440 | tf_op jit(solution)/shard_map/ppermute | solution.py:409
  31.1 13.1 %collective-permute-start.11 = (bf16[96,1024]{1,0:T(8,128)(2,1)S(1)}, bf16[96,1024]{1,0:T(8,128)(2,1)S(1)}, u32[]{:S(2)}, u32[]{:S(2)}) collective-permute-start(bf16[96,1024]{1,0:T(8,128)(2,1)S(1)} %get-tuple-element.61.refs_3_.refs_0_), channel_id=1, source_target_pairs={{0,2},{1,3},{2,0},{3,1},{4,6},{5,7},{6,4},{7,5},{8,10},{9,11},{10,... | collective-permute-start | bytes 589832 | tf_op jit(solution)/shard_map/ppermute | solution.py:413
  37.5 3.0 %collective-permute-start.15 = (bf16[48,1024]{1,0:T(8,128)(2,1)S(1)}, bf16[48,1024]{1,0:T(8,128)(2,1)S(1)}, u32[]{:S(2)}, u32[]{:S(2)}) collective-permute-start(bf16[48,1024]{1,0:T(8,128)(2,1)S(1)} %get-tuple-element.66.refs_4_.refs_3_), channel_id=1, source_target_pairs={{0,1},{1,0},{2,3},{3,2},{4,5},{5,4},{6,7},{7,6},{8,9},{9,8},{10,11... | collective-permute-start | bytes 294920 | tf_op jit(solution)/shard_map/ppermute | solution.py:409
  38.0 2.5 %collective-permute-start.12 = (bf16[48,1024]{1,0:T(8,128)(2,1)S(1)}, bf16[48,1024]{1,0:T(8,128)(2,1)S(1)}, u32[]{:S(2)}, u32[]{:S(2)}) collective-permute-start(bf16[48,1024]{1,0:T(8,128)(2,1)S(1)} %get-tuple-element.63.refs_1_.refs_0_), channel_id=1, source_target_pairs={{0,1},{1,0},{2,3},{3,2},{4,5},{5,4},{6,7},{7,6},{8,9},{9,8},{10,11... | collective-permute-start | bytes 294920 | tf_op jit(solution)/shard_map/ppermute | solution.py:409
  38.0 2.4 %collective-permute-start.13 = (bf16[48,1024]{1,0:T(8,128)(2,1)S(1)}, bf16[48,1024]{1,0:T(8,128)(2,1)S(1)}, u32[]{:S(2)}, u32[]{:S(2)}) collective-permute-start(bf16[48,1024]{1,0:T(8,128)(2,1)S(1)} %get-tuple-element.64.refs_2_.refs_1_), channel_id=1, source_target_pairs={{0,1},{1,0},{2,3},{3,2},{4,5},{5,4},{6,7},{7,6},{8,9},{9,8},{10,11... | collective-permute-start | bytes 294920 | tf_op jit(solution)/shard_map/ppermute | solution.py:409
  38.8 9.6 %collective-permute-start.10 = (bf16[96,1024]{1,0:T(8,128)(2,1)S(1)}, bf16[96,1024]{1,0:T(8,128)(2,1)S(1)}, u32[]{:S(2)}, u32[]{:S(2)}) collective-permute-start(bf16[96,1024]{1,0:T(8,128)(2,1)S(1)} %get-tuple-element.62.refs_9_.refs_0_), channel_id=1, source_target_pairs={{0,2},{1,3},{2,0},{3,1},{4,6},{5,7},{6,4},{7,5},{8,10},{9,11},{10,... | collective-permute-start | bytes 589832 | tf_op jit(solution)/shard_map/ppermute | solution.py:413
  44.4 1.4 %collective-permute-start.17 = (bf16[48,1024]{1,0:T(8,128)(2,1)S(1)}, bf16[48,1024]{1,0:T(8,128)(2,1)S(1)}, u32[]{:S(2)}, u32[]{:S(2)}) collective-permute-start(bf16[48,1024]{1,0:T(8,128)(2,1)S(1)} %get-tuple-element.68.refs_2_), channel_id=1, source_target_pairs={{0,1},{1,0},{2,3},{3,2},{4,5},{5,4},{6,7},{7,6},{8,9},{9,8},{10,11... | collective-permute-start | bytes 294920 | tf_op jit(solution)/shard_map/ppermute | solution.py:409
  48.4 2.5 %collective-permute-start.18 = (bf16[48,1024]{1,0:T(8,128)(2,1)S(1)}, bf16[48,1024]{1,0:T(8,128)(2,1)S(1)}, u32[]{:S(2)}, u32[]{:S(2)}) collective-permute-start(bf16[48,1024]{1,0:T(8,128)(2,1)S(1)} %get-tuple-element.69.refs_1_.refs_4_), channel_id=1, source_target_pairs={{0,1},{1,0},{2,3},{3,2},{4,5},{5,4},{6,7},{7,6},{8,9},{9,8},{10,11... | collective-permute-start | bytes 294920 | tf_op jit(solution)/shard_map/ppermute | solution.py:409
  48.9 2.0 %collective-permute-start.19 = (bf16[48,1024]{1,0:T(8,128)(2,1)S(1)}, bf16[48,1024]{1,0:T(8,128)(2,1)S(1)}, u32[]{:S(2)}, u32[]{:S(2)}) collective-permute-start(bf16[48,1024]{1,0:T(8,128)(2,1)S(1)} %get-tuple-element.70.refs_2_), channel_id=1, source_target_pairs={{0,1},{1,0},{2,3},{3,2},{4,5},{5,4},{6,7},{7,6},{8,9},{9,8},{10,11... | collective-permute-start | bytes 294920 | tf_op jit(solution)/shard_map/ppermute | solution.py:409
  52.8 8.1 %collective-permute-start.20 = (bf16[24,1024]{1,0:T(8,128)(2,1)S(1)}, bf16[24,1024]{1,0:T(8,128)(2,1)S(1)}, u32[]{:S(2)}, u32[]{:S(2)}) collective-permute-start(bf16[24,1024]{1,0:T(8,128)(2,1)S(1)} %get-tuple-element.72), channel_id=1, source_target_pairs={{0,4},{4,0},{8,12},{12,8},{1,5},{5,1},{9,13},{13,9},{2,6},{6,2},{1... | collective-permute-start | bytes 147464 | tf_op jit(solution)/shard_map/ppermute | solution.py:406
  53.5 7.4 %collective-permute-start.21 = (bf16[24,1024]{1,0:T(8,128)(2,1)S(1)}, bf16[24,1024]{1,0:T(8,128)(2,1)S(1)}, u32[]{:S(2)}, u32[]{:S(2)}) collective-permute-start(bf16[24,1024]{1,0:T(8,128)(2,1)S(1)} %get-tuple-element.73), channel_id=1, source_target_pairs={{0,8},{4,12},{8,0},{12,4},{1,9},{5,13},{9,1},{13,5},{2,10},{6,14},... | collective-permute-start | bytes 147464 | tf_op jit(solution)/shard_map/ppermute | solution.py:406
  57.0 5.9 %collective-permute-start.22 = (bf16[24,1024]{1,0:T(8,128)(2,1)S(1)}, bf16[24,1024]{1,0:T(8,128)(2,1)S(1)}, u32[]{:S(2)}, u32[]{:S(2)}) collective-permute-start(bf16[24,1024]{1,0:T(8,128)(2,1)S(1)} %get-tuple-element.74), channel_id=1, source_target_pairs={{0,12},{4,8},{8,4},{12,0},{1,13},{5,9},{9,5},{13,1},{2,14},{6,10},... | collective-permute-start | bytes 147464 | tf_op jit(solution)/shard_map/ppermute | solution.py:406
  63.0 6.3 %collective-permute-start.25 = (bf16[24,1024]{1,0:T(8,128)(2,1)S(1)}, bf16[24,1024]{1,0:T(8,128)(2,1)S(1)}, u32[]{:S(2)}, u32[]{:S(2)}) collective-permute-start(bf16[24,1024]{1,0:T(8,128)(2,1)S(1)} %shard_map.120.refs_2_), channel_id=1, source_target_pairs={{0,12},{4,8},{8,4},{12,0},{1,13},{5,9},{9,5},{13,1},{2,14},{6,10},... | collective-permute-start | bytes 147464 | tf_op jit(solution)/shard_map/ppermute | solution.py:403
  64.7 5.6 %collective-permute-start.24 = (bf16[24,1024]{1,0:T(8,128)(2,1)S(1)}, bf16[24,1024]{1,0:T(8,128)(2,1)S(1)}, u32[]{:S(2)}, u32[]{:S(2)}) collective-permute-start(bf16[24,1024]{1,0:T(8,128)(2,1)S(1)} %shard_map.120.refs_2_), channel_id=1, source_target_pairs={{0,8},{4,12},{8,0},{12,4},{1,9},{5,13},{9,1},{13,5},{2,10},{6,14},... | collective-permute-start | bytes 147464 | tf_op jit(solution)/shard_map/ppermute | solution.py:403
  64.7 5.6 %collective-permute-start.23 = (bf16[24,1024]{1,0:T(8,128)(2,1)S(1)}, bf16[24,1024]{1,0:T(8,128)(2,1)S(1)}, u32[]{:S(2)}, u32[]{:S(2)}) collective-permute-start(bf16[24,1024]{1,0:T(8,128)(2,1)S(1)} %shard_map.120.refs_2_), channel_id=1, source_target_pairs={{0,4},{4,0},{8,12},{12,8},{1,5},{5,1},{9,13},{13,9},{2,6},{6,2},{1... | collective-permute-start | bytes 147464 | tf_op jit(solution)/shard_map/ppermute | solution.py:403
  71.0 1.5 %collective-permute-start.27 = (bf16[96,1024]{1,0:T(8,128)(2,1)S(1)}, bf16[96,1024]{1,0:T(8,128)(2,1)S(1)}, u32[]{:S(2)}, u32[]{:S(2)}) collective-permute-start(bf16[96,1024]{1,0:T(8,128)(2,1)S(1)} %shard_map.121.refs_2_), channel_id=1, source_target_pairs={{0,1},{1,0},{2,3},{3,2},{4,5},{5,4},{6,7},{7,6},{8,9},{9,8},{10,11... | collective-permute-start | bytes 589832 | tf_op jit(solution)/shard_map/ppermute | solution.py:409
  71.9 5.0 %collective-permute-start.26 = (bf16[96,1024]{1,0:T(8,128)(2,1)S(1)}, bf16[96,1024]{1,0:T(8,128)(2,1)S(1)}, u32[]{:S(2)}, u32[]{:S(2)}) collective-permute-start(bf16[96,1024]{1,0:T(8,128)(2,1)S(1)} %shard_map.122.refs_3_), channel_id=1, source_target_pairs={{0,1},{1,0},{2,3},{3,2},{4,5},{5,4},{6,7},{7,6},{8,9},{9,8},{10,11... | collective-permute-start | bytes 589832 | tf_op jit(solution)/shard_map/ppermute | solution.py:409
  73.3 7.9 %collective-permute-start.29 = (bf16[96,1024]{1,0:T(8,128)(2,1)S(1)}, bf16[96,1024]{1,0:T(8,128)(2,1)S(1)}, u32[]{:S(2)}, u32[]{:S(2)}) collective-permute-start(bf16[96,1024]{1,0:T(8,128)(2,1)S(1)} %shard_map.123.refs_5_.refs_0_), channel_id=1, source_target_pairs={{0,2},{1,3},{2,0},{3,1},{4,6},{5,7},{6,4},{7,5},{8,10},{9,11},{10,... | collective-permute-start | bytes 589832 | tf_op jit(solution)/shard_map/ppermute | solution.py:413
  77.7 9.4 %collective-permute-start.28 = (bf16[96,1024]{1,0:T(8,128)(2,1)S(1)}, bf16[96,1024]{1,0:T(8,128)(2,1)S(1)}, u32[]{:S(2)}, u32[]{:S(2)}) collective-permute-start(bf16[96,1024]{1,0:T(8,128)(2,1)S(1)} %shard_map.125.refs_5_.refs_0_), channel_id=1, source_target_pairs={{0,2},{1,3},{2,0},{3,1},{4,6},{5,7},{6,4},{7,5},{8,10},{9,11},{10,... | collective-permute-start | bytes 589832 | tf_op jit(solution)/shard_map/ppermute | solution.py:413
  87.2 3.5 %collective-permute-start.34 = (bf16[48,1024]{1,0:T(8,128)(2,1)S(1)}, bf16[48,1024]{1,0:T(8,128)(2,1)S(1)}, u32[]{:S(2)}, u32[]{:S(2)}) collective-permute-start(bf16[48,1024]{1,0:T(8,128)(2,1)S(1)} %get-tuple-element.89.refs_1_.refs_5_), channel_id=1, source_target_pairs={{0,1},{1,0},{2,3},{3,2},{4,5},{5,4},{6,7},{7,6},{8,9},{9,8},{10,11... | collective-permute-start | bytes 294920 | tf_op jit(solution)/shard_map/ppermute | solution.py:409
  87.6 3.1 %collective-permute-start.35 = (bf16[48,1024]{1,0:T(8,128)(2,1)S(1)}, bf16[48,1024]{1,0:T(8,128)(2,1)S(1)}, u32[]{:S(2)}, u32[]{:S(2)}) collective-permute-start(bf16[48,1024]{1,0:T(8,128)(2,1)S(1)} %get-tuple-element.90.refs_2_), channel_id=1, source_target_pairs={{0,1},{1,0},{2,3},{3,2},{4,5},{5,4},{6,7},{7,6},{8,9},{9,8},{10,11... | collective-permute-start | bytes 294920 | tf_op jit(solution)/shard_map/ppermute | solution.py:409
  87.8 2.9 %collective-permute-start.36 = (bf16[48,1024]{1,0:T(8,128)(2,1)S(1)}, bf16[48,1024]{1,0:T(8,128)(2,1)S(1)}, u32[]{:S(2)}, u32[]{:S(2)}) collective-permute-start(bf16[48,1024]{1,0:T(8,128)(2,1)S(1)} %get-tuple-element.91.refs_3_), channel_id=1, source_target_pairs={{0,1},{1,0},{2,3},{3,2},{4,5},{5,4},{6,7},{7,6},{8,9},{9,8},{10,11... | collective-permute-start | bytes 294920 | tf_op jit(solution)/shard_map/ppermute | solution.py:409
  88.2 2.6 %collective-permute-start.37 = (bf16[48,1024]{1,0:T(8,128)(2,1)S(1)}, bf16[48,1024]{1,0:T(8,128)(2,1)S(1)}, u32[]{:S(2)}, u32[]{:S(2)}) collective-permute-start(bf16[48,1024]{1,0:T(8,128)(2,1)S(1)} %get-tuple-element.92.refs_4_), channel_id=1, source_target_pairs={{0,1},{1,0},{2,3},{3,2},{4,5},{5,4},{6,7},{7,6},{8,9},{9,8},{10,11... | collective-permute-start | bytes 294920 | tf_op jit(solution)/shard_map/ppermute | solution.py:409
  (7 other events, 64.8 us)

commit v3 on v2

--- a/solution.py
+++ b/solution.py
@@ -10,6 +10,7 @@
 F32, BF16 = jnp.float32, jnp.bfloat16
 CHUNKS = 2
 PIECES = 2
+BACK_PIECES = 3
 MIB = 1024 * 1024
 VMEM = pl.BlockSpec(memory_space=pltpu.VMEM)
 SMEM = pl.BlockSpec(memory_space=pltpu.SMEM)
@@ -69,7 +70,7 @@
         out_specs=specs,
         out_shape=shapes,
         scratch_shapes=scratch,
-        compiler_params=pltpu.CompilerParams(vmem_limit_bytes=mib * MIB),
+        compiler_params=pltpu.CompilerParams(vmem_limit_bytes=16 * MIB),
         cost_estimate=pl.CostEstimate(flops=1, bytes_accessed=1, transcendentals=0),
         input_output_aliases={
             1 + len(operands) + len(after) + n: n + marked for n in range(len(filled))
@@ -103,20 +104,28 @@
     return pl.multiple_of(((core_ref[0] ^ side) * CHUNKS + index) * chunk, chunk)
 
 
-def bring(order, *weights):
+def bring(order, wanted):
     parts = 4
+    shapes = []
+    for weight, dim, _, _ in wanted:
+        shape = list(weight.shape)
+        shape[dim] = shape[dim] // 2 // CHUNKS
+        shapes.append(tuple(shape))
 
     def body(core_ref, *refs):
-        sources, targets, sems = refs[: len(weights)], refs[len(weights) : -1], refs[-1]
+        sources, targets, sems = refs[: len(wanted)], refs[len(wanted) : -1], refs[-1]
         copies = []
-        for k in range(len(weights)):
-            high = weights[k].shape[0] // parts
+        for k, (_, dim, side, index) in enumerate(wanted):
+            start = place(core_ref, side, index, shapes[k][dim])
+            high = shapes[k][0] // parts
             for p in range(parts):
-                here = slice(p * high, (p + 1) * high)
+                here = pl.ds(p * high, high)
+                if dim == 0:
+                    source = sources[k].at[pl.ds(pl.multiple_of(start + p * high, high), high), :]
+                else:
+                    source = sources[k].at[here, pl.ds(start, shapes[k][1])]
                 copies.append(
-                    pltpu.make_async_copy(
-                        sources[k].at[here, :], targets[k].at[here, :], sems.at[k * parts + p]
-                    )
+                    pltpu.make_async_copy(source, targets[k].at[here, :], sems.at[k * parts + p])
                 )
                 copies[-1].start()
         for copy in copies:
@@ -125,27 +134,25 @@
     return call(
         body,
         order,
-        [InHbm(w) for w in weights],
-        [pltpu.VMEM(w.shape, w.dtype) for w in weights],
-        scratch=[pltpu.SemaphoreType.DMA((parts * len(weights),))],
+        [InHbm(w[0]) for w in wanted],
+        [pltpu.VMEM(shape, w[0].dtype) for shape, w in zip(shapes, wanted)],
+        scratch=[pltpu.SemaphoreType.DMA((parts * len(wanted),))],
         marked=True,
     )
 
 
-def project(order, rows, weights, side, first, count, added, dtype, pieces=1):
+def project(order, rows, weights, added, dtype, pieces=1):
     tokens = rows.shape[0]
-    chunk = weights[0].shape[1] // 2 // CHUNKS
-    kinds = len(weights)
+    kinds, count = len(weights), len(weights[0])
+    chunk = weights[0][0].shape[1]
     high = tokens // pieces
 
     def body(core_ref, x_ref, *refs):
-        arrived, outs = refs[kinds:-pieces], refs[-pieces:]
+        arrived, outs = refs[kinds * count : -pieces], refs[-pieces:]
         for k in range(kinds):
             for i in range(count):
                 total = jnp.dot(
-                    x_ref[...],
-                    refs[k][:, pl.ds(place(core_ref, side, first + i, chunk), chunk)],
-                    preferred_element_type=F32,
+                    x_ref[...], refs[k * count + i][...], preferred_element_type=F32
                 )
                 here = slice(i * chunk, (i + 1) * chunk)
                 if added:
@@ -156,7 +163,7 @@
     return call(
         body,
         order,
-        [rows, *weights, *added],
+        [rows, *(w for kind in weights for w in kind), *added],
         [shape_of((kinds, high, count * chunk), dtype)] * pieces,
     )
 
@@ -197,35 +204,39 @@
     return call(body, order, [own, *others], pieces_of(*own.shape))
 
 
-def contract(order, terms, weight, carried, groups=0):
+def contract(order, terms, weight, carried, groups=0, brought=None):
     tokens, chunk = terms[0][0][0].shape[0] * PIECES, terms[0][0][0].shape[1]
     width = weight.shape[1]
     rows = tokens // max(groups, 1)
     count = len(terms) * PIECES
-    parts = 2
+    parts = 1 if brought else 2
     high = chunk // parts
 
-    def body(core_ref, w_ref, *refs):
-        held, sems = refs[-2:]
-        copies = []
-        for n, (_, side, index) in enumerate(terms):
-            start = place(core_ref, side, index, chunk)
-            for r in range(parts):
-                m = n * parts + r
-                here = pl.ds(pl.multiple_of(start + r * high, high), high)
-                copies.append(pltpu.make_async_copy(w_ref.at[here, :], held.at[m], sems.at[m]))
-                copies[-1].start()
+    def body(core_ref, *refs):
+        if brought:
+            weights, refs, copies = refs[: len(terms)], refs[len(terms) :], []
+        else:
+            w_ref, *refs, held, sems = refs
+            weights, copies = [held.at[m] for m in range(len(terms) * parts)], []
+            for n, (_, side, index) in enumerate(terms):
+                start = place(core_ref, side, index, chunk)
+                for r in range(parts):
+                    m = n * parts + r
+                    here = pl.ds(pl.multiple_of(start + r * high, high), high)
+                    copies.append(pltpu.make_async_copy(w_ref.at[here, :], held.at[m], sems.at[m]))
+                    copies[-1].start()
         total = refs[count][...] if carried is not None else None
         for n in range(len(terms)):
             left = joined(refs[n * PIECES : (n + 1) * PIECES])
             for r in range(parts):
                 m = n * parts + r
-                copies[m].wait()
+                if copies:
+                    copies[m].wait()
                 term = jnp.dot(
-                    left[:, r * high : (r + 1) * high], held[m], preferred_element_type=F32
+                    left[:, r * high : (r + 1) * high], weights[m][...], preferred_element_type=F32
                 )
                 total = term if total is None else total + term
-        outs = refs[count + (carried is not None) : -2]
+        outs = refs[count + (carried is not None) :]
         for p, out in enumerate(outs):
             out[...] = total[p * rows : (p + 1) * rows, :].astype(out.dtype)
 
@@ -233,11 +244,13 @@
     outs = call(
         body,
         order,
-        [InHbm(weight)]
+        (list(brought) if brought else [InHbm(weight)])
         + [piece for t in terms for piece in t[0]]
         + ([carried] if carried is not None else []),
         out_shape,
-        scratch=[
+        scratch=[]
+        if brought
+        else [
             pltpu.VMEM((len(terms) * parts, high, width), BF16),
             pltpu.SemaphoreType.DMA((len(terms) * parts,)),
         ],
@@ -256,16 +269,10 @@
     return call(body, order, [own, *others, curvature], shape_of(own.shape, BF16))
 
 
-def pull_back(order, weighted, weight, side, index, added):
-    tokens, width = weighted.shape
-    chunk = weight.shape[0] // 2 // CHUNKS
-
+def pull_back(order, weighted, weight, added):
     def body(core_ref, x_ref, w_ref, *refs):
         total = lax.dot_general(
-            x_ref[...],
-            w_ref[pl.ds(place(core_ref, side, index, chunk), chunk), :],
-            COLUMNS_BY_COLUMNS,
-            preferred_element_type=F32,
+            x_ref[...], w_ref[...], COLUMNS_BY_COLUMNS, preferred_element_type=F32
         )
         if added is not None:
             total += refs[0][...].astype(F32)
@@ -275,20 +282,30 @@
         body,
         order,
         [weighted, weight] + ([added] if added is not None else []),
-        shape_of((tokens, chunk), BF16),
+        shape_of((weighted.shape[0], weight.shape[0]), BF16),
     )
 
 
 def cotangents(order, own, others, swish, slope_up):
+    tokens, chunk = own.shape
+    high = tokens // BACK_PIECES
+
     def body(core_ref, own_ref, *refs):
         back = own_ref[...].astype(F32)
         for other in refs[: len(others)]:
             back += other[...].astype(F32)
         swish_ref, slope_up_ref, *outs = refs[len(others) :]
-        put(outs[:PIECES], back * slope_up_ref[...])
-        put(outs[PIECES:], back * swish_ref[...])
-
-    return call(body, order, [own, *others, swish, slope_up], pieces_of(*own.shape) * 2)
+        for k, by in enumerate((slope_up_ref, swish_ref)):
+            term = (back * by[...]).astype(BF16)
+            for p, out in enumerate(outs):
+                out[k] = term[p * high : (p + 1) * high]
+
+    return call(
+        body,
+        order,
+        [own, *others, swish, slope_up],
+        [shape_of((2, high, chunk), BF16)] * BACK_PIECES,
+    )
 
 
 def outer_down(order, hiddens, weighted, filled):
@@ -329,15 +346,15 @@
             pltpu.VMEM((count * parts, high, width), BF16),
             pltpu.SemaphoreType.DMA((count * parts,)),
         ],
-        mib=12,
+        mib=4 + 2 * count,
         out_specs=[HBM],
         filled=filled,
         marked=True,
     )
 
 
-def outer_pair(order, rows, terms, hidden_units, filled):
-    depth, chunk = rows.shape[1], terms[0][0][0].shape[1]
+def outer_pair(order, rows, terms, hidden_units, filled, marked=True):
+    depth, chunk = rows.shape[1], terms[0][0][0].shape[2]
     high = min(256, depth)
     parts = depth // high
     count = len(terms)
@@ -349,7 +366,9 @@
             columns = pl.ds(place(core_ref, side, index, chunk), chunk)
             for k, out in enumerate((gate_out, up_out)):
                 n = t * 2 + k
-                back = joined(pieces[n * PIECES : (n + 1) * PIECES])
+                back = jnp.concatenate(
+                    [ref[k] for ref in pieces[t * BACK_PIECES : (t + 1) * BACK_PIECES]], axis=0
+                )
                 for r in range(parts):
                     m = n * parts + r
                     held[m] = lax.dot_general(
@@ -376,10 +395,10 @@
             pltpu.VMEM((2 * count * parts, high, chunk), BF16),
             pltpu.SemaphoreType.DMA((2 * count * parts,)),
         ],
-        mib=4 + 4 * count,
+        mib=6 + 4 * count,
         out_specs=[HBM, HBM],
         filled=filled,
-        marked=True,
+        marked=marked,
     )
 
 
@@ -418,32 +437,49 @@
             for k in range(1, chips)
         ]
 
-    primal = bring(order, gate_weight, up_weight)
+    each = range(CHUNKS)
+    own = [[(w, 1, 0, i) for w in (gate_weight, up_weight)] for i in each]
+    other = [[(w, 1, 1, i) for w in (gate_weight, up_weight)] for i in each]
+    wanted = sum(other, []) + sum(own[:-1], [])
+    held = bring(order, wanted)
     rows = jnp.concatenate([tokens] + [over_dp(tokens, p) for p in range(1, groups)], axis=0)
-    sent = [project(order, rows, primal, 1, i, 1, [], BF16) for i in range(CHUNKS)]
-    sent = [[to_core(piece) for piece in s] for s in sent]
-    sums = [project(order, rows, primal, 0, i, 1, sent[i], BF16)[0] for i in range(CHUNKS)]
+
+    def pair(n):
+        return [[w] for w in held[2 * n : 2 * n + 2]]
+
+    sent = [to_core(project(order, rows, pair(i), [], BF16)[0]) for i in each]
+    sums = []
+    for i in each:
+        if i == CHUNKS - 1:
+            held = held + bring(order, own[i])
+        sums.append(project(order, rows, pair(CHUNKS + i), [sent[i]], BF16)[0])
     others = [over_chips(s) for s in sums]
-    probe = bring(order, gate_vector, up_vector)
-    sent = [to_core(piece) for piece in project(order, rows, probe, 1, 0, CHUNKS, [], BF16, 3)]
-    (tangents,) = project(order, rows, probe, 0, 0, CHUNKS, sent, F32)
-
-    acted = [activate(order, sums[i], others[i], tangents, i) for i in range(CHUNKS)]
-    tan_others = [over_chips(a[0]) for a in acted]
-    hidden = [(a[3:], 0, i) for i, a in enumerate(acted)]
-    hidden_other = [([to_core(piece) for piece in h[0]], 1, h[2]) for h in hidden]
-    carried = contract(order, hidden + hidden_other, down_vector, None)
-    for i in range(CHUNKS):
-        last = i == CHUNKS - 1
+
+    def probes(side):
+        held = bring(order, [(w, 1, side, i) for w in (gate_vector, up_vector) for i in each])
+        return [held[:CHUNKS], held[CHUNKS:]]
+
+    sent = [to_core(piece) for piece in project(order, rows, probes(1), [], BF16, 3)]
+    (tangents,) = project(order, rows, probes(0), sent, F32)
+
+    acted, carried, tan_others = [], None, []
+    for i in each:
+        acted.append(activate(order, sums[i], others[i], tangents, i))
+        tan_others.append(over_chips(acted[i][0]))
+        hidden = (acted[i][3:], 0, i)
+        hidden_other = ([to_core(piece) for piece in hidden[0]], 1, i)
+        carried = contract(order, [hidden, hidden_other], down_vector, carried)
+        acted[i] = (*acted[i][:3], hidden, hidden_other)
+    for i in each:
         hidden_tan = add_up(order, acted[i][0], tan_others[i])
         tan_other = [to_core(piece) for piece in hidden_tan]
         terms = [(hidden_tan, 0, i), (tan_other, 1, i)]
-        if not last:
+        if i < CHUNKS - 1:
             carried = contract(order, terms, down_weight, carried)
         else:
             carried = contract(order, terms[:1], down_weight, carried)
             carried = contract(order, terms[1:], down_weight, carried, groups)
-    (brought,) = bring(order, down_weight)
+    held = bring(order, [(down_weight, 0, side, i) for side in (1, 0) for i in each])
     weighted_mine = weigh(
         order, carried[0], [back_over_dp(carried[p], p) for p in range(1, groups)], mine
     )
@@ -451,24 +487,20 @@
         [weighted_mine] + [over_dp(weighted_mine, p) for p in range(1, groups)], axis=0
     )
 
-    sent = [to_core(pull_back(order, weighted, brought, 1, i, None)) for i in range(CHUNKS)]
-    sums, fisher_down, filled = [], (), ()
-    for i in range(CHUNKS):
-        sums.append(pull_back(order, weighted, brought, 0, i, sent[i]))
-        if i == 0:
-            fisher_down = outer_down(order, hidden, weighted, fisher_down)
-    fisher_down = outer_down(order, hidden_other, weighted, fisher_down)
+    sent = [to_core(pull_back(order, weighted, held[i], None)) for i in each]
+    sums = [pull_back(order, weighted, held[CHUNKS + i], sent[i]) for i in each]
     others = [over_chips(s) for s in sums]
-    for i in range(CHUNKS):
+    (fisher_down,) = outer_down(
+        order, [a[3] for a in acted] + [a[4] for a in acted], weighted, ()
+    )
+    filled, waiting = (), []
+    for i in each:
         backs = cotangents(order, sums[i], others[i], acted[i][1], acted[i][2])
         backs_other = [to_core(piece) for piece in backs]
-        terms = [(backs, 0, i), (backs_other, 1, i)]
-        if i == 0:
-            filled = outer_pair(order, rows, terms, hidden_units, filled)
-        else:
-            filled = outer_pair(order, rows, terms[:1], hidden_units, filled)
-            filled = outer_pair(order, rows, terms[1:], hidden_units, filled)
-    return (filled[0], filled[1], fisher_down[0])
+        filled = outer_pair(order, rows, waiting + [(backs, 0, i)], hidden_units, filled)
+        waiting = [(backs_other, 1, i)]
+    filled = outer_pair(order, rows, waiting, hidden_units, filled, False)
+    return (filled[0], filled[1], fisher_down)
 
 
 def solution(mesh):

time: 94.1 us -> 89.3 us (0.949)
  waiting for transfers between devices: 13.3 us -> 7.84 us
  Pallas kernels: 49.7 us -> 51.6 us
  starting transfers between devices: 28.6 us -> 27.3 us
    ppermute x23 -> x21, waiting for transfers between devices: 4.32 us -> 1.42 us  [to_core(): return lax.ppermute(value, 'mp', [(i, i ^ 1) for i in range(2 * chips)])]
    ppermute x6, waiting for transfers between devices: 4.19 us -> 1.4 us  [over_chips(): lax.ppermute(value, 'mp', [(2 * i + c, 2 * partner(i, k, chips) + c) for...]
    pallas_call x29 -> x31, Pallas kernels: 49.7 us -> 51.6 us  [call(): pl.pallas_call(kernel, in_specs=[SMEM] + [HBM if isinstance(o, InHbm) els...]
    ppermute x23 -> x21, starting transfers between devices: 6.27 us -> 5.61 us  [to_core(): return lax.ppermute(value, 'mp', [(i, i ^ 1) for i in range(2 * chips)])]
  transfers between devices with their start and end apart: 38 -> 36, of which waited for: 16 -> 10; matrix products, arithmetic and copies ran while one was open for 1% -> 1% of each run, Pallas kernels for 46% -> 51%
where the time goes in v3:
time: 89.3 us; the launch traced here: 89 us
  Pallas kernels  51.6 us (58%)
  starting transfers between devices  27.3 us (31%)
  waiting for transfers between devices  7.84 us (9%)
  between operations  1.19 us (1%)
  local copies, waits for them, and re-layouts  1.05 us (1%)
    pallas_call x31, Pallas kernels, call(): pl.pallas_call(kernel, in_specs=[SMEM] + [HBM if isinstance(o, InHbm) els...  51.6 us
    ppermute x6, starting transfers between devices, over_dp(): lax.ppermute(value, 'dp', [(i, partner(i, step, groups)) for i in range(g...  10.1 us
    ppermute x6, starting transfers between devices, over_chips(): lax.ppermute(value, 'mp', [(2 * i + c, 2 * partner(i, k, chips) + c) for...  7.18 us
    ppermute x21, starting transfers between devices, to_core(): return lax.ppermute(value, 'mp', [(i, i ^ 1) for i in range(2 * chips)])  5.61 us
    ppermute x3, starting transfers between devices, back_over_dp(): lax.ppermute(value, 'dp', [(i, giver(i, step, groups)) for i in range(gro...  4.45 us
    ppermute x6, waiting for transfers between devices, over_dp(): lax.ppermute(value, 'dp', [(i, partner(i, step, groups)) for i in range(g...  3.19 us
    ppermute x3, waiting for transfers between devices, back_over_dp(): lax.ppermute(value, 'dp', [(i, giver(i, step, groups)) for i in range(gro...  1.83 us
  transfers between devices with their start and end apart: 36, of which 10 were waited for; matrix products, arithmetic and copies ran while one was open for 1% of the time, Pallas kernels for 51%

profile of v3, /device:TPU:0, one launch (start us, length us, event | category | flops | bytes accessed | tf_op | source)
XLA Modules:
  0.0 89.0 jit_solution(6303623728162912291)
XLA Ops:
  0.6 4.1 %collective-permute-start.1 = (bf16[24,1024]{1,0:T(8,128)(2,1)}, bf16[24,1024]{1,0:T(8,128)(2,1)S(1)}, u32[]{:S(2)}, u32[]{:S(2)}) collective-permute-start(bf16[24,1024]{1,0:T(8,128)(2,1)} %param.8), channel_id=1, source_target_pairs={{0,8},{4,12},{8,0},{12,4},{1,9},{5,13},{9,1},{13,5},{2,10},{6,14},... | collective-permute-start | bytes 147464 | tf_op jit(solution)/shard_map/ppermute | solution.py:422
  4.7 1.6 %collective-permute-start = (bf16[24,1024]{1,0:T(8,128)(2,1)}, bf16[24,1024]{1,0:T(8,128)(2,1)S(1)}, u32[]{:S(2)}, u32[]{:S(2)}) collective-permute-start(bf16[24,1024]{1,0:T(8,128)(2,1)} %param.8), channel_id=1, source_target_pairs={{0,4},{4,0},{8,12},{12,8},{1,5},{5,1},{9,13},{13,9},{2,6},{6,2},{1... | collective-permute-start | bytes 147464 | tf_op jit(solution)/shard_map/ppermute | solution.py:422
  6.3 0.9 constant_dynamic-update-slice_fusion.3
  7.2 4.8 %shard_map.103 = (f32[8,128]{1,0:T(8,128)S(1)}, bf16[1024,1024]{1,0:T(8,128)(2,1)S(1)}, bf16[1024,1024]{1,0:T(8,128)(2,1)S(1)}, bf16[1024,1024]{1,0:T(8,128)(2,1...) custom-call(s32[1]{0:T(128)} %bitcast.core_ref, ...), custom_call_target="tpu_custom_call" | custom-call | flops 1 | bytes 1 | tf_op jit(solution)/shard_map/pallas_call | solution.py:64
  15.9 1.5 %collective-permute-start.9 = (bf16[2,96,1024]{2,1,0:T(8,128)(2,1)S(1)}, bf16[2,96,1024]{2,1,0:T(8,128)(2,1)S(1)}, u32[]{:S(2)}, u32[]{:S(2)}) collective-permute-start(bf16[2,96,1024]{2,1,0:T(8,128)(2,1)S(1)} %shard_map.106.refs_2_.refs_0_), channel_id=1, source_target_pairs={{0,2},{1,3},{2,0},{3,1},{4,6},{5,7},{6,4},{7,5},{8,10},{9,11},{10,... | collective-permute-start | bytes 1179656 | tf_op jit(solution)/shard_map/ppermute | solution.py:432
  17.4 2.2 %shard_map.107 = (f32[8,128]{1,0:T(8,128)S(1)}, bf16[1024,1024]{1,0:T(8,128)(2,1)S(1)}, bf16[1024,1024]{1,0:T(8,128)(2,1)S(1)}) custom-call(s32[1]{0:T(128)} %bitcast.core_ref, bf16[1024,4096]{1,0:T(8,128)(2,1)} %refs_0_.11, bf16[1024,4096]{1,0:T(8,128)(2,1)} %refs_1_.6, bf16[2,96,1024]{2,1,0:T(8,128)(2,1)S(1)} %shard_map.106.refs_2_.refs_0_), custom_call_target="tpu_custom_call" | custom-call | flops 1 | bytes 1 | tf_op jit(solution)/shard_map/pallas_call | solution.py:64
  19.6 0.8 shard_map.108.refs_4_.refs_0_
  21.1 3.5 %shard_map.109 = (f32[8,128]{1,0:T(8,128)S(1)}, bf16[1024,1024]{1,0:T(8,128)(2,1)S(1)}, bf16[1024,1024]{1,0:T(8,128)(2,1)S(1)}, bf16[1024,1024]{1,0:T(8,128)(2,1)S(1)}, bf16[1024,1024]{1,0:T(8,128)(2,1)S(1)}) custom-call(s32[1]{0:T(128)} %bitcast.core_ref, bf16[1024,4096]{1,0:T(8,128)(2,1)} %refs_1_.8, bf16[1024,4096]{1,0:T(8,128)(2,1)} %refs_1_.8, ...), custom_call_target="tpu_custom_call" | custom-call | flops 1 | bytes 1 | tf_op jit(solution)/shard_map/pallas_call | solution.py:64
  24.6 1.5 %shard_map.110 = (bf16[2,32,2048]{2,1,0:T(8,128)(2,1)S(1)}, bf16[2,32,2048]{2,1,0:T(8,128)(2,1)S(1)}, bf16[2,32,2048]{2,1,0:T(8,128)(2,1)S(1)}) custom-call(s32[1]{0:T(128)} %bitcast.core_ref, bf16[96,1024]{1,0:T(8,128)(2,1)S(1)} %constant_dynamic-update-slice_fusion.refs_0_, bf16[1024,1024]{1,0:T(8,128)(2,1)S(1)} %get-tuple-element.75.refs_1_, ...), custom_call_target="tpu_custom_call" | custom-call | flops 1 | bytes 1 | tf_op jit(solution)/shard_map/pallas_call | solution.py:64
  26.8 3.5 %shard_map.111 = (f32[8,128]{1,0:T(8,128)S(1)}, bf16[1024,1024]{1,0:T(8,128)(2,1)S(1)}, bf16[1024,1024]{1,0:T(8,128)(2,1)S(1)}, bf16[1024,1024]{1,0:T(8,128)(2,1)S(1)}, bf16[1024,1024]{1,0:T(8,128)(2,1)S(1)}) custom-call(s32[1]{0:T(128)} %bitcast.core_ref, bf16[1024,4096]{1,0:T(8,128)(2,1)} %refs_1_.8, bf16[1024,4096]{1,0:T(8,128)(2,1)} %refs_1_.8, ...), custom_call_target="tpu_custom_call" | custom-call | flops 1 | bytes 1 | tf_op jit(solution)/shard_map/pallas_call | solution.py:64
  30.4 1.5 %shard_map.112.refs_2_.refs_3_ = f32[2,96,2048]{2,1,0:T(8,128)S(1)} custom-call(s32[1]{0:T(128)} %bitcast.core_ref, bf16[96,1024]{1,0:T(8,128)(2,1)S(1)} %constant_dynamic-update-slice_fusion.refs_0_, bf16[1024,1024]{1,0:T(8,128)(2,1)S(1)} %get-tuple-element.81.refs_1_, bf16[1024,1024]{1,0:T(8,128)(2,1)S(1)} %get-tuple-element.82.refs_2_, ...), custom_call_target="tpu_custom_call" | custom-call | flops 1 | bytes 1 | tf_op jit(solution)/shard_map/pallas_call | solution.py:64
  32.8 1.5 %collective-permute-start.13 = (bf16[96,1024]{1,0:T(8,128)(2,1)S(1)}, bf16[96,1024]{1,0:T(8,128)(2,1)S(1)}, u32[]{:S(2)}, u32[]{:S(2)}) collective-permute-start(bf16[96,1024]{1,0:T(8,128)(2,1)S(1)} %get-tuple-element.90.refs_5_.refs_0_), channel_id=1, source_target_pairs={{0,2},{1,3},{2,0},{3,1},{4,6},{5,7},{6,4},{7,5},{8,10},{9,11},{10,... | collective-permute-start | bytes 589832 | tf_op jit(solution)/shard_map/ppermute | solution.py:432
  34.3 2.5 %shard_map.114.refs_3_.refs_5_ = f32[96,1024]{1,0:T(8,128)S(1)} custom-call(s32[1]{0:T(128)} %bitcast.core_ref, bf16[4096,1024]{1,0:T(8,128)(2,1)} %refs_0_.15, bf16[48,1024]{1,0:T(8,128)(2,1)S(1)} %get-tuple-element.88.refs_1_.refs_0_, bf16[48,1024]{1,0:T(8,128)(2,1)S(1)} %get-tuple-element.89.refs_2_.refs_1_, ...), custom_call_target="tpu_custom_call" | custom-call | flops 1 | bytes 1 | tf_op jit(solution)/shard_map/pallas_call | solution.py:64
  37.7 1.2 %collective-permute-start.12 = (bf16[96,1024]{1,0:T(8,128)(2,1)S(1)}, bf16[96,1024]{1,0:T(8,128)(2,1)S(1)}, u32[]{:S(2)}, u32[]{:S(2)}) collective-permute-start(bf16[96,1024]{1,0:T(8,128)(2,1)S(1)} %get-tuple-element.91.refs_6_.refs_0_), channel_id=1, source_target_pairs={{0,2},{1,3},{2,0},{3,1},{4,6},{5,7},{6,4},{7,5},{8,10},{9,11},{10,... | collective-permute-start | bytes 589832 | tf_op jit(solution)/shard_map/ppermute | solution.py:432
  38.9 2.5 %shard_map.116.refs_2_.refs_5_ = f32[96,1024]{1,0:T(8,128)S(1)} custom-call(s32[1]{0:T(128)} %bitcast.core_ref, bf16[4096,1024]{1,0:T(8,128)(2,1)} %refs_0_.15, bf16[48,1024]{1,0:T(8,128)(2,1)S(1)} %get-tuple-element.92.refs_1_.refs_2_, bf16[48,1024]{1,0:T(8,128)(2,1)S(1)} %get-tuple-element.93.refs_2_.refs_3_, ...), custom_call_target="tpu_custom_call" | custom-call | flops 1 | bytes 1 | tf_op jit(solution)/shard_map/pallas_call | solution.py:64
  43.0 2.5 %shard_map.118.refs_2_.refs_3_ = f32[96,1024]{1,0:T(8,128)S(1)} custom-call(s32[1]{0:T(128)} %bitcast.core_ref, bf16[4096,1024]{1,0:T(8,128)(2,1)} %refs_3_.7, bf16[48,1024]{1,0:T(8,128)(2,1)S(1)} %get-tuple-element.94.refs_1_.refs_6_, bf16[48,1024]{1,0:T(8,128)(2,1)S(1)} %get-tuple-element.95.refs_2_, bf16[48,1024]{1,0:T(8,128)(2,1)S(1)} %collective-permute-done.16.refs_3_, ...), custom_call_target="tpu_custom_call" | custom-call | flops 1 | bytes 1 | tf_op jit(solution)/shard_map/pallas_call | solution.py:64
  46.2 1.9 %shard_map.120.refs_3_.refs_4_ = f32[96,1024]{1,0:T(8,128)S(1)} custom-call(s32[1]{0:T(128)} %bitcast.core_ref, bf16[4096,1024]{1,0:T(8,128)(2,1)} %refs_3_.7, bf16[48,1024]{1,0:T(8,128)(2,1)S(1)} %get-tuple-element.96.refs_1_.refs_4_, bf16[48,1024]{1,0:T(8,128)(2,1)S(1)} %get-tuple-element.97.refs_2_, f32[96,1024]{1,0:T(8,128)S(1)} %shard_map.118.refs_2_.refs_3_, ...), custom_call_target="tpu_custom_call" | custom-call | flops 1 | bytes 1 | tf_op jit(solution)/shard_map/pallas_call | solution.py:64
  48.1 1.9 %shard_map.121 = (f32[24,1024]{1,0:T(8,128)S(1)}, bf16[24,1024]{1,0:T(8,128)(2,1)S(1)}, bf16[24,1024]{1,0:T(8,128)(2,1)S(1)}, bf16[24,1024]{1,0:T(8,128)(2,1)S(1)}) custom-call(s32[1]{0:T(128)} %bitcast.core_ref, bf16[4096,1024]{1,0:T(8,128)(2,1)} %refs_3_.7, bf16[48,1024]{1,0:T(8,128)(2,1)S(1)} %collective-permute-done.18.refs_1_, ...), custom_call_target="tpu_custom_call" | custom-call | flops 1 | bytes 1 | tf_op jit(solution)/shard_map/pallas_call | solution.py:64
  50.6 3.5 %collective-permute-start.21 = (bf16[24,1024]{1,0:T(8,128)(2,1)S(1)}, bf16[24,1024]{1,0:T(8,128)(2,1)S(1)}, u32[]{:S(2)}, u32[]{:S(2)}) collective-permute-start(bf16[24,1024]{1,0:T(8,128)(2,1)S(1)} %get-tuple-element.100), channel_id=1, source_target_pairs={{0,8},{4,12},{8,0},{12,4},{1,9},{5,13},{9,1},{13,5},{2,10},{6,14},... | collective-permute-start | bytes 147464 | tf_op jit(solution)/shard_map/ppermute | solution.py:425
  54.6 3.5 %shard_map.122 = (f32[8,128]{1,0:T(8,128)S(1)}, bf16[1024,1024]{1,0:T(8,128)(2,1)S(1)}, bf16[1024,1024]{1,0:T(8,128)(2,1)S(1)}, bf16[1024,1024]{1,0:T(8,128)(2,1)S(1)}, bf16[1024,1024]{1,0:T(8,128)(2,1)S(1)}) custom-call(s32[1]{0:T(128)} %bitcast.core_ref, bf16[4096,1024]{1,0:T(8,128)(2,1)} %refs_3_.7, bf16[4096,1024]{1,0:T(8,128)(2,1)} %refs_3_.7, ...), custom_call_target="tpu_custom_call" | custom-call | flops 1 | bytes 1 | tf_op jit(solution)/shard_map/pallas_call | solution.py:64
  58.2 1.8 %collective-permute-done.22.refs_3_ = bf16[24,1024]{1,0:T(8,128)(2,1)S(1)} collective-permute-done((bf16[24,1024]{1,0:T(8,128)(2,1)S(1)}, bf16[24,1024]{1,0:T(8,128)(2,1)S(1)}, u32[]{:S(2)}, u32[]{:S(2)}) %collective-permute-start.22) | collective-permute-done | bytes 49184 | tf_op jit(solution)/shard_map/ppermute | solution.py:425
  60.1 1.7 %collective-permute-start.25 = (bf16[24,1024]{1,0:T(8,128)(2,1)S(1)}, bf16[24,1024]{1,0:T(8,128)(2,1)S(1)}, u32[]{:S(2)}, u32[]{:S(2)}) collective-permute-start(bf16[24,1024]{1,0:T(8,128)(2,1)S(1)} %shard_map.123.refs_2_), channel_id=1, source_target_pairs={{0,12},{4,8},{8,4},{12,0},{1,13},{5,9},{9,5},{13,1},{2,14},{6,10},... | collective-permute-start | bytes 147464 | tf_op jit(solution)/shard_map/ppermute | solution.py:422
  61.7 2.7 %collective-permute-start.23 = (bf16[24,1024]{1,0:T(8,128)(2,1)S(1)}, bf16[24,1024]{1,0:T(8,128)(2,1)S(1)}, u32[]{:S(2)}, u32[]{:S(2)}) collective-permute-start(bf16[24,1024]{1,0:T(8,128)(2,1)S(1)} %shard_map.123.refs_2_), channel_id=1, source_target_pairs={{0,4},{4,0},{8,12},{12,8},{1,5},{5,1},{9,13},{13,9},{2,6},{6,2},{1... | collective-permute-start | bytes 147464 | tf_op jit(solution)/shard_map/ppermute | solution.py:422
  64.5 1.9 %collective-permute-done.25 = bf16[24,1024]{1,0:T(8,128)(2,1)S(1)} collective-permute-done((bf16[24,1024]{1,0:T(8,128)(2,1)S(1)}, bf16[24,1024]{1,0:T(8,128)(2,1)S(1)}, u32[]{:S(2)}, u32[]{:S(2)}) %collective-permute-start.25) | collective-permute-done | bytes 49184 | tf_op jit(solution)/shard_map/ppermute | solution.py:422
  66.4 0.9 %collective-permute-done.24 = bf16[24,1024]{1,0:T(8,128)(2,1)S(1)} collective-permute-done((bf16[24,1024]{1,0:T(8,128)(2,1)S(1)}, bf16[24,1024]{1,0:T(8,128)(2,1)S(1)}, u32[]{:S(2)}, u32[]{:S(2)}) %collective-permute-start.24) | collective-permute-done | bytes 49184 | tf_op jit(solution)/shard_map/ppermute | solution.py:422
  70.4 1.5 %collective-permute-start.29 = (bf16[96,1024]{1,0:T(8,128)(2,1)S(1)}, bf16[96,1024]{1,0:T(8,128)(2,1)S(1)}, u32[]{:S(2)}, u32[]{:S(2)}) collective-permute-start(bf16[96,1024]{1,0:T(8,128)(2,1)S(1)} %shard_map.126.refs_3_.refs_0_), channel_id=1, source_target_pairs={{0,2},{1,3},{2,0},{3,1},{4,6},{5,7},{6,4},{7,5},{8,10},{9,11},{10,... | collective-permute-start | bytes 589832 | tf_op jit(solution)/shard_map/ppermute | solution.py:432
  72.7 0.9 collective-permute-start.28
  73.5 3.7 %shard_map.128 = (f32[8,128]{1,0:T(8,128)S(1)}, bf16[4096,1024]{1,0:T(8,128)(2,1)}) custom-call(s32[1]{0:T(128)} %bitcast.core_ref, bf16[48,1024]{1,0:T(8,128)(2,1)S(1)} %get-tuple-element.88.refs_1_.refs_0_, bf16[48,1024]{1,0:T(8,128)(2,1)S(1)} %get-tuple-element.89.refs_2_.refs_1_, bf16[48,1024]{1,0:T(8,128)(2,1)S(1)} %get-tuple-element.92.refs_1_.refs_2_, ...), custom_call_target="tpu_custom_call" | custom-call | flops 1 | bytes 1 | tf_op jit(solution)/shard_map/pallas_call | solution.py:64
  77.3 1.1 %collective-permute-done.29.refs_1_ = bf16[96,1024]{1,0:T(8,128)(2,1)S(1)} collective-permute-done((bf16[96,1024]{1,0:T(8,128)(2,1)S(1)}, bf16[96,1024]{1,0:T(8,128)(2,1)S(1)}, u32[]{:S(2)}, u32[]{:S(2)}) %collective-permute-start.29) | collective-permute-done | bytes 196640 | tf_op jit(solution)/shard_map/ppermute | solution.py:432
  79.1 2.4 %shard_map.130 = (f32[8,128]{1,0:T(8,128)S(1)}, bf16[1024,4096]{1,0:T(8,128)(2,1)}, bf16[1024,4096]{1,0:T(8,128)(2,1)}) custom-call(s32[1]{0:T(128)} %bitcast.core_ref, bf16[96,1024]{1,0:T(8,128)(2,1)S(1)} %constant_dynamic-update-slice_fusion.refs_0_, bf16[2,32,1024]{2,1,0:T(8,128)(2,1)S(1)} %get-tuple-element.112.refs_1_.refs_4_, ...), custom_call_target="tpu_custom_call" | custom-call | flops 1 | bytes 1 | tf_op jit(solution)/shard_map/pallas_call | solution.py:64
  82.7 3.7 %shard_map.132 = (f32[8,128]{1,0:T(8,128)S(1)}, bf16[1024,4096]{1,0:T(8,128)(2,1)}, bf16[1024,4096]{1,0:T(8,128)(2,1)}) custom-call(s32[1]{0:T(128)} %bitcast.core_ref, bf16[96,1024]{1,0:T(8,128)(2,1)S(1)} %constant_dynamic-update-slice_fusion.refs_0_, ...), custom_call_target="tpu_custom_call", output_to_operand_aliasing={{1}: (9, {}), {2}: (10, {})} | custom-call | flops 1 | bytes 1 | tf_op jit(solution)/shard_map/pallas_call | solution.py:64
  86.4 2.4 %shard_map.133 = (bf16[1024,4096]{1,0:T(8,128)(2,1)}, bf16[1024,4096]{1,0:T(8,128)(2,1)}) custom-call(s32[1]{0:T(128)} %bitcast.core_ref, bf16[96,1024]{1,0:T(8,128)(2,1)S(1)} %constant_dynamic-update-slice_fusion.refs_0_, bf16[2,32,1024]{2,1,0:T(8,128)(2,1)S(1)} %collective-permute-done.30.refs_1_, ...), custom_call_target="tpu_custom_call", output_to_operand_aliasing={{0}: (6, {}), {1}: (7, {})} | custom-call | flops 1 | bytes 1 | tf_op jit(solution)/shard_map/pallas_call | solution.py:64
  (80 shorter events, 16.0 us)
Async XLA Ops:
  0.6 11.4 %collective-permute-start.1 = (bf16[24,1024]{1,0:T(8,128)(2,1)}, bf16[24,1024]{1,0:T(8,128)(2,1)S(1)}, u32[]{:S(2)}, u32[]{:S(2)}) collective-permute-start(bf16[24,1024]{1,0:T(8,128)(2,1)} %param.8), channel_id=1, source_target_pairs={{0,8},{4,12},{8,0},{12,4},{1,9},{5,13},{9,1},{13,5},{2,10},{6,14},... | collective-permute-start | bytes 147464 | tf_op jit(solution)/shard_map/ppermute | solution.py:422
  4.7 7.3 %collective-permute-start = (bf16[24,1024]{1,0:T(8,128)(2,1)}, bf16[24,1024]{1,0:T(8,128)(2,1)S(1)}, u32[]{:S(2)}, u32[]{:S(2)}) collective-permute-start(bf16[24,1024]{1,0:T(8,128)(2,1)} %param.8), channel_id=1, source_target_pairs={{0,4},{4,0},{8,12},{12,8},{1,5},{5,1},{9,13},{13,9},{2,6},{6,2},{1... | collective-permute-start | bytes 147464 | tf_op jit(solution)/shard_map/ppermute | solution.py:422
  6.3 6.1 %collective-permute-start.2 = (bf16[24,1024]{1,0:T(8,128)(2,1)}, bf16[24,1024]{1,0:T(8,128)(2,1)S(1)}, u32[]{:S(2)}, u32[]{:S(2)}) collective-permute-start(bf16[24,1024]{1,0:T(8,128)(2,1)} %param.8), channel_id=1, source_target_pairs={{0,12},{4,8},{8,4},{12,0},{1,13},{5,9},{9,5},{13,1},{2,14},{6,10},... | collective-permute-start | bytes 147464 | tf_op jit(solution)/shard_map/ppermute | solution.py:422
  13.2 1.8 %collective-permute-start.3 = (bf16[2,96,1024]{2,1,0:T(8,128)(2,1)S(1)}, bf16[2,96,1024]{2,1,0:T(8,128)(2,1)S(1)}, u32[]{:S(2)}, u32[]{:S(2)}) collective-permute-start(bf16[2,96,1024]{2,1,0:T(8,128)(2,1)S(1)} %shard_map.104.refs_3_), channel_id=1, source_target_pairs={{0,1},{1,0},{2,3},{3,2},{4,5},{5,4},{6,7},{7,6},{8,9},{9,8},{10,11... | collective-permute-start | bytes 1179656 | tf_op jit(solution)/shard_map/ppermute | solution.py:428
  14.1 5.5 %collective-permute-start.4 = (bf16[2,96,1024]{2,1,0:T(8,128)(2,1)S(1)}, bf16[2,96,1024]{2,1,0:T(8,128)(2,1)S(1)}, u32[]{:S(2)}, u32[]{:S(2)}) collective-permute-start(bf16[2,96,1024]{2,1,0:T(8,128)(2,1)S(1)} %shard_map.105.refs_4_), channel_id=1, source_target_pairs={{0,1},{1,0},{2,3},{3,2},{4,5},{5,4},{6,7},{7,6},{8,9},{9,8},{10,11... | collective-permute-start | bytes 1179656 | tf_op jit(solution)/shard_map/ppermute | solution.py:428
  15.9 16.0 %collective-permute-start.9 = (bf16[2,96,1024]{2,1,0:T(8,128)(2,1)S(1)}, bf16[2,96,1024]{2,1,0:T(8,128)(2,1)S(1)}, u32[]{:S(2)}, u32[]{:S(2)}) collective-permute-start(bf16[2,96,1024]{2,1,0:T(8,128)(2,1)S(1)} %shard_map.106.refs_2_.refs_0_), channel_id=1, source_target_pairs={{0,2},{1,3},{2,0},{3,1},{4,6},{5,7},{6,4},{7,5},{8,10},{9,11},{10,... | collective-permute-start | bytes 1179656 | tf_op jit(solution)/shard_map/ppermute | solution.py:432
  20.5 16.3 %collective-permute-start.5 = (bf16[2,96,1024]{2,1,0:T(8,128)(2,1)S(1)}, bf16[2,96,1024]{2,1,0:T(8,128)(2,1)S(1)}, u32[]{:S(2)}, u32[]{:S(2)}) collective-permute-start(bf16[2,96,1024]{2,1,0:T(8,128)(2,1)S(1)} %shard_map.108.refs_4_.refs_0_), channel_id=1, source_target_pairs={{0,2},{1,3},{2,0},{3,1},{4,6},{5,7},{6,4},{7,5},{8,10},{9,11},{10,... | collective-permute-start | bytes 1179656 | tf_op jit(solution)/shard_map/ppermute | solution.py:432
  26.1 4.2 %collective-permute-start.7 = (bf16[2,32,2048]{2,1,0:T(8,128)(2,1)S(1)}, bf16[2,32,2048]{2,1,0:T(8,128)(2,1)S(1)}, u32[]{:S(2)}, u32[]{:S(2)}) collective-permute-start(bf16[2,32,2048]{2,1,0:T(8,128)(2,1)S(1)} %get-tuple-element.85), channel_id=1, source_target_pairs={{0,1},{1,0},{2,3},{3,2},{4,5},{5,4},{6,7},{7,6},{8,9},{9,8},{10,11... | collective-permute-start | bytes 786440 | tf_op jit(solution)/shard_map/ppermute | solution.py:428
  26.2 4.1 %collective-permute-start.8 = (bf16[2,32,2048]{2,1,0:T(8,128)(2,1)S(1)}, bf16[2,32,2048]{2,1,0:T(8,128)(2,1)S(1)}, u32[]{:S(2)}, u32[]{:S(2)}) collective-permute-start(bf16[2,32,2048]{2,1,0:T(8,128)(2,1)S(1)} %get-tuple-element.86), channel_id=1, source_target_pairs={{0,1},{1,0},{2,3},{3,2},{4,5},{5,4},{6,7},{7,6},{8,9},{9,8},{10,11... | collective-permute-start | bytes 786440 | tf_op jit(solution)/shard_map/ppermute | solution.py:428
  26.7 3.7 %collective-permute-start.6 = (bf16[2,32,2048]{2,1,0:T(8,128)(2,1)S(1)}, bf16[2,32,2048]{2,1,0:T(8,128)(2,1)S(1)}, u32[]{:S(2)}, u32[]{:S(2)}) collective-permute-start(bf16[2,32,2048]{2,1,0:T(8,128)(2,1)S(1)} %get-tuple-element.80.refs_4_), channel_id=1, source_target_pairs={{0,1},{1,0},{2,3},{3,2},{4,5},{5,4},{6,7},{7,6},{8,9},{9,8},{10,11... | collective-permute-start | bytes 786440 | tf_op jit(solution)/shard_map/ppermute | solution.py:428
  32.2 2.1 %collective-permute-start.10 = (bf16[48,1024]{1,0:T(8,128)(2,1)S(1)}, bf16[48,1024]{1,0:T(8,128)(2,1)S(1)}, u32[]{:S(2)}, u32[]{:S(2)}) collective-permute-start(bf16[48,1024]{1,0:T(8,128)(2,1)S(1)} %get-tuple-element.88.refs_1_.refs_0_), channel_id=1, source_target_pairs={{0,1},{1,0},{2,3},{3,2},{4,5},{5,4},{6,7},{7,6},{8,9},{9,8},{10,11... | collective-permute-start | bytes 294920 | tf_op jit(solution)/shard_map/ppermute | solution.py:428
  32.7 1.6 %collective-permute-start.11 = (bf16[48,1024]{1,0:T(8,128)(2,1)S(1)}, bf16[48,1024]{1,0:T(8,128)(2,1)S(1)}, u32[]{:S(2)}, u32[]{:S(2)}) collective-permute-start(bf16[48,1024]{1,0:T(8,128)(2,1)S(1)} %get-tuple-element.89.refs_2_.refs_1_), channel_id=1, source_target_pairs={{0,1},{1,0},{2,3},{3,2},{4,5},{5,4},{6,7},{7,6},{8,9},{9,8},{10,11... | collective-permute-start | bytes 294920 | tf_op jit(solution)/shard_map/ppermute | solution.py:428
  32.8 8.7 %collective-permute-start.13 = (bf16[96,1024]{1,0:T(8,128)(2,1)S(1)}, bf16[96,1024]{1,0:T(8,128)(2,1)S(1)}, u32[]{:S(2)}, u32[]{:S(2)}) collective-permute-start(bf16[96,1024]{1,0:T(8,128)(2,1)S(1)} %get-tuple-element.90.refs_5_.refs_0_), channel_id=1, source_target_pairs={{0,2},{1,3},{2,0},{3,1},{4,6},{5,7},{6,4},{7,5},{8,10},{9,11},{10,... | collective-permute-start | bytes 589832 | tf_op jit(solution)/shard_map/ppermute | solution.py:432
  37.1 1.8 %collective-permute-start.14 = (bf16[48,1024]{1,0:T(8,128)(2,1)S(1)}, bf16[48,1024]{1,0:T(8,128)(2,1)S(1)}, u32[]{:S(2)}, u32[]{:S(2)}) collective-permute-start(bf16[48,1024]{1,0:T(8,128)(2,1)S(1)} %get-tuple-element.92.refs_1_.refs_2_), channel_id=1, source_target_pairs={{0,1},{1,0},{2,3},{3,2},{4,5},{5,4},{6,7},{7,6},{8,9},{9,8},{10,11... | collective-permute-start | bytes 294920 | tf_op jit(solution)/shard_map/ppermute | solution.py:428
  37.7 7.9 %collective-permute-start.12 = (bf16[96,1024]{1,0:T(8,128)(2,1)S(1)}, bf16[96,1024]{1,0:T(8,128)(2,1)S(1)}, u32[]{:S(2)}, u32[]{:S(2)}) collective-permute-start(bf16[96,1024]{1,0:T(8,128)(2,1)S(1)} %get-tuple-element.91.refs_6_.refs_0_), channel_id=1, source_target_pairs={{0,2},{1,3},{2,0},{3,1},{4,6},{5,7},{6,4},{7,5},{8,10},{9,11},{10,... | collective-permute-start | bytes 589832 | tf_op jit(solution)/shard_map/ppermute | solution.py:432
  45.6 2.5 %collective-permute-start.18 = (bf16[48,1024]{1,0:T(8,128)(2,1)S(1)}, bf16[48,1024]{1,0:T(8,128)(2,1)S(1)}, u32[]{:S(2)}, u32[]{:S(2)}) collective-permute-start(bf16[48,1024]{1,0:T(8,128)(2,1)S(1)} %get-tuple-element.96.refs_1_.refs_4_), channel_id=1, source_target_pairs={{0,1},{1,0},{2,3},{3,2},{4,5},{5,4},{6,7},{7,6},{8,9},{9,8},{10,11... | collective-permute-start | bytes 294920 | tf_op jit(solution)/shard_map/ppermute | solution.py:428
  46.1 2.0 %collective-permute-start.19 = (bf16[48,1024]{1,0:T(8,128)(2,1)S(1)}, bf16[48,1024]{1,0:T(8,128)(2,1)S(1)}, u32[]{:S(2)}, u32[]{:S(2)}) collective-permute-start(bf16[48,1024]{1,0:T(8,128)(2,1)S(1)} %get-tuple-element.97.refs_2_), channel_id=1, source_target_pairs={{0,1},{1,0},{2,3},{3,2},{4,5},{5,4},{6,7},{7,6},{8,9},{9,8},{10,11... | collective-permute-start | bytes 294920 | tf_op jit(solution)/shard_map/ppermute | solution.py:428
  50.0 8.1 %collective-permute-start.20 = (bf16[24,1024]{1,0:T(8,128)(2,1)S(1)}, bf16[24,1024]{1,0:T(8,128)(2,1)S(1)}, u32[]{:S(2)}, u32[]{:S(2)}) collective-permute-start(bf16[24,1024]{1,0:T(8,128)(2,1)S(1)} %get-tuple-element.99), channel_id=1, source_target_pairs={{0,4},{4,0},{8,12},{12,8},{1,5},{5,1},{9,13},{13,9},{2,6},{6,2},{1... | collective-permute-start | bytes 147464 | tf_op jit(solution)/shard_map/ppermute | solution.py:425
  50.6 7.5 %collective-permute-start.21 = (bf16[24,1024]{1,0:T(8,128)(2,1)S(1)}, bf16[24,1024]{1,0:T(8,128)(2,1)S(1)}, u32[]{:S(2)}, u32[]{:S(2)}) collective-permute-start(bf16[24,1024]{1,0:T(8,128)(2,1)S(1)} %get-tuple-element.100), channel_id=1, source_target_pairs={{0,8},{4,12},{8,0},{12,4},{1,9},{5,13},{9,1},{13,5},{2,10},{6,14},... | collective-permute-start | bytes 147464 | tf_op jit(solution)/shard_map/ppermute | solution.py:425
  54.1 5.9 %collective-permute-start.22 = (bf16[24,1024]{1,0:T(8,128)(2,1)S(1)}, bf16[24,1024]{1,0:T(8,128)(2,1)S(1)}, u32[]{:S(2)}, u32[]{:S(2)}) collective-permute-start(bf16[24,1024]{1,0:T(8,128)(2,1)S(1)} %get-tuple-element.101), channel_id=1, source_target_pairs={{0,12},{4,8},{8,4},{12,0},{1,13},{5,9},{9,5},{13,1},{2,14},{6,10},... | collective-permute-start | bytes 147464 | tf_op jit(solution)/shard_map/ppermute | solution.py:425
  60.1 6.3 %collective-permute-start.25 = (bf16[24,1024]{1,0:T(8,128)(2,1)S(1)}, bf16[24,1024]{1,0:T(8,128)(2,1)S(1)}, u32[]{:S(2)}, u32[]{:S(2)}) collective-permute-start(bf16[24,1024]{1,0:T(8,128)(2,1)S(1)} %shard_map.123.refs_2_), channel_id=1, source_target_pairs={{0,12},{4,8},{8,4},{12,0},{1,13},{5,9},{9,5},{13,1},{2,14},{6,10},... | collective-permute-start | bytes 147464 | tf_op jit(solution)/shard_map/ppermute | solution.py:422
  61.7 5.6 %collective-permute-start.24 = (bf16[24,1024]{1,0:T(8,128)(2,1)S(1)}, bf16[24,1024]{1,0:T(8,128)(2,1)S(1)}, u32[]{:S(2)}, u32[]{:S(2)}) collective-permute-start(bf16[24,1024]{1,0:T(8,128)(2,1)S(1)} %shard_map.123.refs_2_), channel_id=1, source_target_pairs={{0,8},{4,12},{8,0},{12,4},{1,9},{5,13},{9,1},{13,5},{2,10},{6,14},... | collective-permute-start | bytes 147464 | tf_op jit(solution)/shard_map/ppermute | solution.py:422
  61.7 5.6 %collective-permute-start.23 = (bf16[24,1024]{1,0:T(8,128)(2,1)S(1)}, bf16[24,1024]{1,0:T(8,128)(2,1)S(1)}, u32[]{:S(2)}, u32[]{:S(2)}) collective-permute-start(bf16[24,1024]{1,0:T(8,128)(2,1)S(1)} %shard_map.123.refs_2_), channel_id=1, source_target_pairs={{0,4},{4,0},{8,12},{12,8},{1,5},{5,1},{9,13},{13,9},{2,6},{6,2},{1... | collective-permute-start | bytes 147464 | tf_op jit(solution)/shard_map/ppermute | solution.py:422
  69.0 2.9 %collective-permute-start.26 = (bf16[96,1024]{1,0:T(8,128)(2,1)S(1)}, bf16[96,1024]{1,0:T(8,128)(2,1)S(1)}, u32[]{:S(2)}, u32[]{:S(2)}) collective-permute-start(bf16[96,1024]{1,0:T(8,128)(2,1)S(1)} %shard_map.125.refs_3_), channel_id=1, source_target_pairs={{0,1},{1,0},{2,3},{3,2},{4,5},{5,4},{6,7},{7,6},{8,9},{9,8},{10,11... | collective-permute-start | bytes 589832 | tf_op jit(solution)/shard_map/ppermute | solution.py:428
  70.4 8.0 %collective-permute-start.29 = (bf16[96,1024]{1,0:T(8,128)(2,1)S(1)}, bf16[96,1024]{1,0:T(8,128)(2,1)S(1)}, u32[]{:S(2)}, u32[]{:S(2)}) collective-permute-start(bf16[96,1024]{1,0:T(8,128)(2,1)S(1)} %shard_map.126.refs_3_.refs_0_), channel_id=1, source_target_pairs={{0,2},{1,3},{2,0},{3,1},{4,6},{5,7},{6,4},{7,5},{8,10},{9,11},{10,... | collective-permute-start | bytes 589832 | tf_op jit(solution)/shard_map/ppermute | solution.py:432
  72.7 9.1 %collective-permute-start.28 = (bf16[96,1024]{1,0:T(8,128)(2,1)S(1)}, bf16[96,1024]{1,0:T(8,128)(2,1)S(1)}, u32[]{:S(2)}, u32[]{:S(2)}) collective-permute-start(bf16[96,1024]{1,0:T(8,128)(2,1)S(1)} %shard_map.127.refs_9_.refs_0_), channel_id=1, source_target_pairs={{0,2},{1,3},{2,0},{3,1},{4,6},{5,7},{6,4},{7,5},{8,10},{9,11},{10,... | collective-permute-start | bytes 589832 | tf_op jit(solution)/shard_map/ppermute | solution.py:432
  78.5 4.0 %collective-permute-start.33 = (bf16[2,32,1024]{2,1,0:T(8,128)(2,1)S(1)}, bf16[2,32,1024]{2,1,0:T(8,128)(2,1)S(1)}, u32[]{:S(2)}, u32[]{:S(2)}) collective-permute-start(bf16[2,32,1024]{2,1,0:T(8,128)(2,1)S(1)} %get-tuple-element.112.refs_1_.refs_4_), channel_id=1, source_target_pairs={{0,1},{1,0},{2,3},{3,2},{4,5},{5,4},{6,7},{7,6},{8,9},{9,8},{10,11... | collective-permute-start | bytes 393224 | tf_op jit(solution)/shard_map/ppermute | solution.py:428
  78.6 4.1 %collective-permute-start.34 = (bf16[2,32,1024]{2,1,0:T(8,128)(2,1)S(1)}, bf16[2,32,1024]{2,1,0:T(8,128)(2,1)S(1)}, u32[]{:S(2)}, u32[]{:S(2)}) collective-permute-start(bf16[2,32,1024]{2,1,0:T(8,128)(2,1)S(1)} %get-tuple-element.113.refs_2_), channel_id=1, source_target_pairs={{0,1},{1,0},{2,3},{3,2},{4,5},{5,4},{6,7},{7,6},{8,9},{9,8},{10,11... | collective-permute-start | bytes 393224 | tf_op jit(solution)/shard_map/ppermute | solution.py:428
  79.1 3.6 %collective-permute-start.35 = (bf16[2,32,1024]{2,1,0:T(8,128)(2,1)S(1)}, bf16[2,32,1024]{2,1,0:T(8,128)(2,1)S(1)}, u32[]{:S(2)}, u32[]{:S(2)}) collective-permute-start(bf16[2,32,1024]{2,1,0:T(8,128)(2,1)S(1)} %get-tuple-element.114.refs_3_), channel_id=1, source_target_pairs={{0,1},{1,0},{2,3},{3,2},{4,5},{5,4},{6,7},{7,6},{8,9},{9,8},{10,11... | collective-permute-start | bytes 393224 | tf_op jit(solution)/shard_map/ppermute | solution.py:428
  81.9 4.5 %collective-permute-start.30 = (bf16[2,32,1024]{2,1,0:T(8,128)(2,1)S(1)}, bf16[2,32,1024]{2,1,0:T(8,128)(2,1)S(1)}, u32[]{:S(2)}, u32[]{:S(2)}) collective-permute-start(bf16[2,32,1024]{2,1,0:T(8,128)(2,1)S(1)} %get-tuple-element.116.refs_4_.refs_7_), channel_id=1, source_target_pairs={{0,1},{1,0},{2,3},{3,2},{4,5},{5,4},{6,7},{7,6},{8,9},{9,8},{10,11... | collective-permute-start | bytes 393224 | tf_op jit(solution)/shard_map/ppermute | solution.py:428
  82.1 4.3 %collective-permute-start.31 = (bf16[2,32,1024]{2,1,0:T(8,128)(2,1)S(1)}, bf16[2,32,1024]{2,1,0:T(8,128)(2,1)S(1)}, u32[]{:S(2)}, u32[]{:S(2)}) collective-permute-start(bf16[2,32,1024]{2,1,0:T(8,128)(2,1)S(1)} %get-tuple-element.117.refs_5_), channel_id=1, source_target_pairs={{0,1},{1,0},{2,3},{3,2},{4,5},{5,4},{6,7},{7,6},{8,9},{9,8},{10,11... | collective-permute-start | bytes 393224 | tf_op jit(solution)/shard_map/ppermute | solution.py:428
  82.5 4.0 %collective-permute-start.32 = (bf16[2,32,1024]{2,1,0:T(8,128)(2,1)S(1)}, bf16[2,32,1024]{2,1,0:T(8,128)(2,1)S(1)}, u32[]{:S(2)}, u32[]{:S(2)}) collective-permute-start(bf16[2,32,1024]{2,1,0:T(8,128)(2,1)S(1)} %get-tuple-element.118.refs_6_), channel_id=1, source_target_pairs={{0,1},{1,0},{2,3},{3,2},{4,5},{5,4},{6,7},{7,6},{8,9},{9,8},{10,11... | collective-permute-start | bytes 393224 | tf_op jit(solution)/shard_map/ppermute | solution.py:428
  (5 other events, 59.6 us)

commit v4 on v3

--- a/solution.py
+++ b/solution.py
@@ -96,8 +96,8 @@
         ref[...] = value[p * rows : (p + 1) * rows].astype(ref.dtype)
 
 
-def pieces_of(tokens, width):
-    return [shape_of((tokens // PIECES, width), BF16)] * PIECES
+def pieces_of(tokens, width, pieces):
+    return [shape_of((tokens // pieces, width), BF16)] * pieces
 
 
 def place(core_ref, side, index, chunk):
@@ -141,19 +141,50 @@
     )
 
 
-def project(order, rows, weights, added, dtype, pieces=1):
-    tokens = rows.shape[0]
-    kinds, count = len(weights), len(weights[0])
-    chunk = weights[0][0].shape[1]
+def assemble(order, parts):
+    tokens = sum(part.shape[0] for part in parts)
+
+    def body(core_ref, *refs):
+        rows = jnp.concatenate([ref[...].astype(F32) for ref in refs[:-1]], axis=0)
+        refs[-1][...] = rows.astype(BF16)
+
+    return call(body, order, parts, shape_of((tokens, parts[0].shape[1]), BF16))
+
+
+def project(order, rows, weights, added, dtype, pieces=1, side=0, chunks=()):
+    tokens, depth = rows.shape
+    kinds, count = len(weights), len(chunks) or len(weights[0])
+    chunk = weights[0].shape[1] // 2 // CHUNKS if chunks else weights[0][0].shape[1]
     high = tokens // pieces
+    given = kinds if chunks else kinds * count
+    parts = 2
+    deep = depth // parts
 
     def body(core_ref, x_ref, *refs):
-        arrived, outs = refs[kinds * count : -pieces], refs[-pieces:]
+        copies = []
+        if chunks:
+            *refs, held, sems = refs
+            for k in range(kinds):
+                for i, index in enumerate(chunks):
+                    columns = pl.ds(place(core_ref, side, index, chunk), chunk)
+                    for r in range(parts):
+                        m = (k * count + i) * parts + r
+                        copies.append(
+                            pltpu.make_async_copy(
+                                refs[k].at[r * deep : (r + 1) * deep, columns],
+                                held.at[k * count + i, r * deep : (r + 1) * deep, :],
+                                sems.at[m],
+                            )
+                        )
+                        copies[-1].start()
+        arrived, outs = refs[given:-pieces], refs[-pieces:]
         for k in range(kinds):
             for i in range(count):
-                total = jnp.dot(
-                    x_ref[...], refs[k * count + i][...], preferred_element_type=F32
-                )
+                n = k * count + i
+                for copy in copies[n * parts : (n + 1) * parts]:
+                    copy.wait()
+                weight = held[n] if chunks else refs[n][...]
+                total = jnp.dot(x_ref[...], weight, preferred_element_type=F32)
                 here = slice(i * chunk, (i + 1) * chunk)
                 if added:
                     total += jnp.concatenate([ref[k, :, here] for ref in arrived], axis=0).astype(F32)
@@ -163,8 +194,16 @@
     return call(
         body,
         order,
-        [rows, *(w for kind in weights for w in kind), *added],
+        [rows]
+        + ([InHbm(w) for w in weights] if chunks else [w for kind in weights for w in kind])
+        + list(added),
         [shape_of((kinds, high, count * chunk), dtype)] * pieces,
+        scratch=[
+            pltpu.VMEM((kinds * count, depth, chunk), BF16),
+            pltpu.SemaphoreType.DMA((kinds * count * parts,)),
+        ]
+        if chunks
+        else [],
     )
 
 
@@ -190,50 +229,47 @@
         body,
         order,
         [own, *others, tangents],
-        [shape_of((tokens, chunk), d) for d in (BF16, F32, F32)] + pieces_of(tokens, chunk),
-    )
-
-
-def add_up(order, own, others):
+        [shape_of((tokens, chunk), d) for d in (BF16, F32, F32)] + pieces_of(tokens, chunk, PIECES),
+    )
+
+
+def add_up(order, own, others, pieces):
     def body(core_ref, own_ref, *refs):
         total = own_ref[...].astype(F32)
         for other in refs[: len(others)]:
             total += other[...].astype(F32)
         put(refs[len(others) :], total)
 
-    return call(body, order, [own, *others], pieces_of(*own.shape))
-
-
-def contract(order, terms, weight, carried, groups=0, brought=None):
-    tokens, chunk = terms[0][0][0].shape[0] * PIECES, terms[0][0][0].shape[1]
+    return call(body, order, [own, *others], pieces_of(*own.shape, pieces))
+
+
+def contract(order, terms, weight, carried, groups=0):
+    pieces = len(terms[0][0])
+    tokens, chunk = terms[0][0][0].shape[0] * pieces, terms[0][0][0].shape[1]
     width = weight.shape[1]
     rows = tokens // max(groups, 1)
-    count = len(terms) * PIECES
-    parts = 1 if brought else 2
-    high = chunk // parts
+    count = len(terms) * pieces
+    high = min(256, chunk)
+    parts = chunk // high
 
     def body(core_ref, *refs):
-        if brought:
-            weights, refs, copies = refs[: len(terms)], refs[len(terms) :], []
-        else:
-            w_ref, *refs, held, sems = refs
-            weights, copies = [held.at[m] for m in range(len(terms) * parts)], []
-            for n, (_, side, index) in enumerate(terms):
-                start = place(core_ref, side, index, chunk)
-                for r in range(parts):
-                    m = n * parts + r
-                    here = pl.ds(pl.multiple_of(start + r * high, high), high)
-                    copies.append(pltpu.make_async_copy(w_ref.at[here, :], held.at[m], sems.at[m]))
-                    copies[-1].start()
+        w_ref, *refs, held, sems = refs
+        copies = []
+        for n, (_, side, index) in enumerate(terms):
+            start = place(core_ref, side, index, chunk)
+            for r in range(parts):
+                m = n * parts + r
+                here = pl.ds(pl.multiple_of(start + r * high, high), high)
+                copies.append(pltpu.make_async_copy(w_ref.at[here, :], held.at[m], sems.at[m]))
+                copies[-1].start()
         total = refs[count][...] if carried is not None else None
         for n in range(len(terms)):
-            left = joined(refs[n * PIECES : (n + 1) * PIECES])
+            left = joined(refs[n * pieces : (n + 1) * pieces])
             for r in range(parts):
                 m = n * parts + r
-                if copies:
-                    copies[m].wait()
+                copies[m].wait()
                 term = jnp.dot(
-                    left[:, r * high : (r + 1) * high], weights[m][...], preferred_element_type=F32
+                    left[:, r * high : (r + 1) * high], held[m], preferred_element_type=F32
                 )
                 total = term if total is None else total + term
         outs = refs[count + (carried is not None) :]
@@ -244,13 +280,11 @@
     outs = call(
         body,
         order,
-        (list(brought) if brought else [InHbm(weight)])
+        [InHbm(weight)]
         + [piece for t in terms for piece in t[0]]
         + ([carried] if carried is not None else []),
         out_shape,
-        scratch=[]
-        if brought
-        else [
+        scratch=[
             pltpu.VMEM((len(terms) * parts, high, width), BF16),
             pltpu.SemaphoreType.DMA((len(terms) * parts,)),
         ],
@@ -286,9 +320,9 @@
     )
 
 
-def cotangents(order, own, others, swish, slope_up):
+def cotangents(order, own, others, swish, slope_up, pieces):
     tokens, chunk = own.shape
-    high = tokens // BACK_PIECES
+    high = tokens // pieces
 
     def body(core_ref, own_ref, *refs):
         back = own_ref[...].astype(F32)
@@ -304,7 +338,7 @@
         body,
         order,
         [own, *others, swish, slope_up],
-        [shape_of((2, high, chunk), BF16)] * BACK_PIECES,
+        [shape_of((2, high, chunk), BF16)] * pieces,
     )
 
 
@@ -361,14 +395,13 @@
 
     def body(core_ref, x_ref, *refs):
         *pieces, gate_out, up_out, held, sems = refs
-        copies = []
-        for t, (_, side, index) in enumerate(terms):
+        copies, used = [], 0
+        for t, (backs, side, index) in enumerate(terms):
+            given, used = pieces[used : used + len(backs)], used + len(backs)
             columns = pl.ds(place(core_ref, side, index, chunk), chunk)
             for k, out in enumerate((gate_out, up_out)):
                 n = t * 2 + k
-                back = jnp.concatenate(
-                    [ref[k] for ref in pieces[t * BACK_PIECES : (t + 1) * BACK_PIECES]], axis=0
-                )
+                back = jnp.concatenate([ref[k] for ref in given], axis=0)
                 for r in range(parts):
                     m = n * parts + r
                     held[m] = lax.dot_general(
@@ -438,29 +471,24 @@
         ]
 
     each = range(CHUNKS)
-    own = [[(w, 1, 0, i) for w in (gate_weight, up_weight)] for i in each]
-    other = [[(w, 1, 1, i) for w in (gate_weight, up_weight)] for i in each]
-    wanted = sum(other, []) + sum(own[:-1], [])
-    held = bring(order, wanted)
-    rows = jnp.concatenate([tokens] + [over_dp(tokens, p) for p in range(1, groups)], axis=0)
-
-    def pair(n):
-        return [[w] for w in held[2 * n : 2 * n + 2]]
-
-    sent = [to_core(project(order, rows, pair(i), [], BF16)[0]) for i in each]
-    sums = []
-    for i in each:
-        if i == CHUNKS - 1:
-            held = held + bring(order, own[i])
-        sums.append(project(order, rows, pair(CHUNKS + i), [sent[i]], BF16)[0])
+    primal, probe = (gate_weight, up_weight), (gate_vector, up_vector)
+    wanted = [(w, 1, side, i) for side in (1, 0) for i in each for w in primal]
+    held = bring(order, wanted[:-2])
+    rows = assemble(order, [tokens] + [over_dp(tokens, p) for p in range(1, groups)])
+    sent, sums = [], []
+    for n in range(0, len(wanted), 2):
+        if n == len(held):
+            held += bring(order, wanted[-2:])
+        weights = [[w] for w in held[n : n + 2]]
+        if n < 2 * CHUNKS:
+            sent.append(to_core(project(order, rows, weights, [], BF16)[0]))
+        else:
+            sums.append(project(order, rows, weights, [sent[len(sums)]], BF16)[0])
     others = [over_chips(s) for s in sums]
-
-    def probes(side):
-        held = bring(order, [(w, 1, side, i) for w in (gate_vector, up_vector) for i in each])
-        return [held[:CHUNKS], held[CHUNKS:]]
-
-    sent = [to_core(piece) for piece in project(order, rows, probes(1), [], BF16, 3)]
-    (tangents,) = project(order, rows, probes(0), sent, F32)
+    sent = project(order, rows, probe, [], BF16, 3, 1, tuple(each))
+    sent = [to_core(piece) for piece in sent]
+    held = bring(order, [(w, 1, 0, i) for w in probe for i in each])
+    (tangents,) = project(order, rows, [held[:CHUNKS], held[CHUNKS:]], sent, F32)
 
     acted, carried, tan_others = [], None, []
     for i in each:
@@ -471,20 +499,22 @@
         carried = contract(order, [hidden, hidden_other], down_vector, carried)
         acted[i] = (*acted[i][:3], hidden, hidden_other)
     for i in each:
-        hidden_tan = add_up(order, acted[i][0], tan_others[i])
+        last = i == CHUNKS - 1
+        hidden_tan = add_up(order, acted[i][0], tan_others[i], 1 if last else PIECES)
         tan_other = [to_core(piece) for piece in hidden_tan]
         terms = [(hidden_tan, 0, i), (tan_other, 1, i)]
-        if i < CHUNKS - 1:
+        if not last:
             carried = contract(order, terms, down_weight, carried)
         else:
             carried = contract(order, terms[:1], down_weight, carried)
             carried = contract(order, terms[1:], down_weight, carried, groups)
-    held = bring(order, [(down_weight, 0, side, i) for side in (1, 0) for i in each])
+    held = bring(order, [(down_weight, 0, 1, i) for i in each])
     weighted_mine = weigh(
         order, carried[0], [back_over_dp(carried[p], p) for p in range(1, groups)], mine
     )
-    weighted = jnp.concatenate(
-        [weighted_mine] + [over_dp(weighted_mine, p) for p in range(1, groups)], axis=0
+    held += bring(order, [(down_weight, 0, 0, i) for i in each])
+    weighted = assemble(
+        order, [weighted_mine] + [over_dp(weighted_mine, p) for p in range(1, groups)]
     )
 
     sent = [to_core(pull_back(order, weighted, held[i], None)) for i in each]
@@ -495,7 +525,7 @@
     )
     filled, waiting = (), []
     for i in each:
-        backs = cotangents(order, sums[i], others[i], acted[i][1], acted[i][2])
+        backs = cotangents(order, sums[i], others[i], acted[i][1], acted[i][2], BACK_PIECES)
         backs_other = [to_core(piece) for piece in backs]
         filled = outer_pair(order, rows, waiting + [(backs, 0, i)], hidden_units, filled)
         waiting = [(backs_other, 1, i)]

time: 89.3 us -> 87.3 us (0.978)
    ppermute x6, waiting for transfers between devices: 3.19 us -> 1.59 us  [over_dp(): lax.ppermute(value, 'dp', [(i, partner(i, step, groups)) for i in range(g...]
    pallas_call x31 -> x33, Pallas kernels: 51.6 us -> 51 us  [call(): pl.pallas_call(kernel, in_specs=[SMEM] + [HBM if isinstance(o, InHbm) els...]
    ppermute x21 -> x20, starting transfers between devices: 5.61 us -> 5.44 us  [to_core(): return lax.ppermute(value, 'mp', [(i, i ^ 1) for i in range(2 * chips)])]
  transfers between devices with their start and end apart: 36 -> 35, of which waited for: 10 -> 10; matrix products, arithmetic and copies ran while one was open for 1% -> 0% of each run, Pallas kernels for 51% -> 52%
where the time goes in v4:
time: 87.3 us; the launch traced here: 87.1 us
  Pallas kernels  51 us (58%)
  starting transfers between devices  27.4 us (31%)
  waiting for transfers between devices  7.2 us (8%)
  between operations  1.19 us (1%)
    pallas_call x33, Pallas kernels, call(): pl.pallas_call(kernel, in_specs=[SMEM] + [HBM if isinstance(o, InHbm) els...  51 us
    ppermute x6, starting transfers between devices, over_dp(): lax.ppermute(value, 'dp', [(i, partner(i, step, groups)) for i in range(g...  10.1 us
    ppermute x6, starting transfers between devices, over_chips(): lax.ppermute(value, 'mp', [(2 * i + c, 2 * partner(i, k, chips) + c) for...  7.48 us
    ppermute x20, starting transfers between devices, to_core(): return lax.ppermute(value, 'mp', [(i, i ^ 1) for i in range(2 * chips)])  5.44 us
    ppermute x3, starting transfers between devices, back_over_dp(): lax.ppermute(value, 'dp', [(i, giver(i, step, groups)) for i in range(gro...  4.44 us
    ppermute x3, waiting for transfers between devices, back_over_dp(): lax.ppermute(value, 'dp', [(i, giver(i, step, groups)) for i in range(gro...  2.26 us
    ppermute x6, waiting for transfers between devices, over_chips(): lax.ppermute(value, 'mp', [(2 * i + c, 2 * partner(i, k, chips) + c) for...  1.93 us
  transfers between devices with their start and end apart: 35, of which 10 were waited for; matrix products, arithmetic and copies ran while one was open for 0% of the time, Pallas kernels for 52%

profile of v4, /device:TPU:0, one launch (start us, length us, event | category | flops | bytes accessed | tf_op | source)
XLA Modules:
  0.0 87.1 jit_solution(353469274577347188)
XLA Ops:
  0.6 4.1 %collective-permute-start.1 = (bf16[24,1024]{1,0:T(8,128)(2,1)}, bf16[24,1024]{1,0:T(8,128)(2,1)S(1)}, u32[]{:S(2)}, u32[]{:S(2)}) collective-permute-start(bf16[24,1024]{1,0:T(8,128)(2,1)} %refs_0_.12), channel_id=1, source_target_pairs={{0,8},{4,12},{8,0},{12,4},{1,9},{5,13},{9,1},{13,5},{2,10},{6,14},... | collective-permute-start | bytes 147464 | tf_op jit(solution)/shard_map/ppermute | solution.py:455
  4.7 1.6 %collective-permute-start = (bf16[24,1024]{1,0:T(8,128)(2,1)}, bf16[24,1024]{1,0:T(8,128)(2,1)S(1)}, u32[]{:S(2)}, u32[]{:S(2)}) collective-permute-start(bf16[24,1024]{1,0:T(8,128)(2,1)} %refs_0_.12), channel_id=1, source_target_pairs={{0,4},{4,0},{8,12},{12,8},{1,5},{5,1},{9,13},{13,9},{2,6},{6,2},{1... | collective-permute-start | bytes 147464 | tf_op jit(solution)/shard_map/ppermute | solution.py:455
  6.3 4.8 %shard_map.103 = (f32[8,128]{1,0:T(8,128)S(1)}, bf16[1024,1024]{1,0:T(8,128)(2,1)S(1)}, bf16[1024,1024]{1,0:T(8,128)(2,1)S(1)}, bf16[1024,1024]{1,0:T(8,128)(2,1...) custom-call(s32[1]{0:T(128)} %bitcast.core_ref, ...), custom_call_target="tpu_custom_call" | custom-call | flops 1 | bytes 1 | tf_op jit(solution)/shard_map/pallas_call | solution.py:64
  11.2 1.2 %collective-permute-done.2.refs_3_ = bf16[24,1024]{1,0:T(8,128)(2,1)S(1)} collective-permute-done((bf16[24,1024]{1,0:T(8,128)(2,1)}, bf16[24,1024]{1,0:T(8,128)(2,1)S(1)}, u32[]{:S(2)}, u32[]{:S(2)}) %collective-permute-start.2) | collective-permute-done | bytes 49184 | tf_op jit(solution)/shard_map/ppermute | solution.py:455
  15.0 0.8 shard_map.107.refs_2_.refs_0_
  15.9 1.6 %collective-permute-start.9 = (bf16[2,96,1024]{2,1,0:T(8,128)(2,1)S(1)}, bf16[2,96,1024]{2,1,0:T(8,128)(2,1)S(1)}, u32[]{:S(2)}, u32[]{:S(2)}) collective-permute-start(bf16[2,96,1024]{2,1,0:T(8,128)(2,1)S(1)} %shard_map.107.refs_2_.refs_0_), channel_id=1, source_target_pairs={{0,2},{1,3},{2,0},{3,1},{4,6},{5,7},{6,4},{7,5},{8,10},{9,11},{10,... | collective-permute-start | bytes 1179656 | tf_op jit(solution)/shard_map/ppermute | solution.py:465
  17.4 2.2 %shard_map.108 = (f32[8,128]{1,0:T(8,128)S(1)}, bf16[1024,1024]{1,0:T(8,128)(2,1)S(1)}, bf16[1024,1024]{1,0:T(8,128)(2,1)S(1)}) custom-call(s32[1]{0:T(128)} %bitcast.core_ref, bf16[1024,4096]{1,0:T(8,128)(2,1)} %refs_0_.13, bf16[1024,4096]{1,0:T(8,128)(2,1)} %refs_1_.7, bf16[2,96,1024]{2,1,0:T(8,128)(2,1)S(1)} %shard_map.107.refs_2_.refs_0_), custom_call_target="tpu_custom_call" | custom-call | flops 1 | bytes 1 | tf_op jit(solution)/shard_map/pallas_call | solution.py:64
  19.7 0.8 shard_map.109.refs_3_.refs_0_
  21.1 4.0 %shard_map.110 = (bf16[2,32,2048]{2,1,0:T(8,128)(2,1)S(1)}, bf16[2,32,2048]{2,1,0:T(8,128)(2,1)S(1)}, bf16[2,32,2048]{2,1,0:T(8,128)(2,1)S(1)}) custom-call(s32[1]{0:T(128)} %bitcast.core_ref, bf16[96,1024]{1,0:T(8,128)(2,1)S(1)} %shard_map.104.refs_0_.refs_3_, bf16[1024,4096]{1,0:T(8,128)(2,1)} %refs_1_.9, bf16[1024,4096]{1,0:T(8,128)(2,1)} %refs_3_.3, ...), custom_call_target="tpu_custom_call" | custom-call | flops 1 | bytes 1 | tf_op jit(solution)/shard_map/pallas_call | solution.py:64
  25.7 3.5 %shard_map.111 = (f32[8,128]{1,0:T(8,128)S(1)}, bf16[1024,1024]{1,0:T(8,128)(2,1)S(1)}, bf16[1024,1024]{1,0:T(8,128)(2,1)S(1)}, bf16[1024,1024]{1,0:T(8,128)(2,1)S(1)}, bf16[1024,1024]{1,0:T(8,128)(2,1)S(1)}) custom-call(s32[1]{0:T(128)} %bitcast.core_ref, bf16[1024,4096]{1,0:T(8,128)(2,1)} %refs_1_.9, bf16[1024,4096]{1,0:T(8,128)(2,1)} %refs_1_.9, ...), custom_call_target="tpu_custom_call" | custom-call | flops 1 | bytes 1 | tf_op jit(solution)/shard_map/pallas_call | solution.py:64
  29.3 1.5 %shard_map.112.refs_2_.refs_3_ = f32[2,96,2048]{2,1,0:T(8,128)S(1)} custom-call(s32[1]{0:T(128)} %bitcast.core_ref, bf16[96,1024]{1,0:T(8,128)(2,1)S(1)} %shard_map.104.refs_0_.refs_3_, bf16[1024,1024]{1,0:T(8,128)(2,1)S(1)} %get-tuple-element.70.refs_1_, bf16[1024,1024]{1,0:T(8,128)(2,1)S(1)} %get-tuple-element.71.refs_2_, ...), custom_call_target="tpu_custom_call" | custom-call | flops 1 | bytes 1 | tf_op jit(solution)/shard_map/pallas_call | solution.py:64
  31.7 1.5 %collective-permute-start.13 = (bf16[96,1024]{1,0:T(8,128)(2,1)S(1)}, bf16[96,1024]{1,0:T(8,128)(2,1)S(1)}, u32[]{:S(2)}, u32[]{:S(2)}) collective-permute-start(bf16[96,1024]{1,0:T(8,128)(2,1)S(1)} %get-tuple-element.79.refs_5_.refs_0_), channel_id=1, source_target_pairs={{0,2},{1,3},{2,0},{3,1},{4,6},{5,7},{6,4},{7,5},{8,10},{9,11},{10,... | collective-permute-start | bytes 589832 | tf_op jit(solution)/shard_map/ppermute | solution.py:465
  33.2 2.4 %shard_map.114.refs_3_.refs_5_ = f32[96,1024]{1,0:T(8,128)S(1)} custom-call(s32[1]{0:T(128)} %bitcast.core_ref, bf16[4096,1024]{1,0:T(8,128)(2,1)} %refs_0_.16, bf16[48,1024]{1,0:T(8,128)(2,1)S(1)} %get-tuple-element.77.refs_1_.refs_0_, bf16[48,1024]{1,0:T(8,128)(2,1)S(1)} %get-tuple-element.78.refs_2_.refs_1_, ...), custom_call_target="tpu_custom_call" | custom-call | flops 1 | bytes 1 | tf_op jit(solution)/shard_map/pallas_call | solution.py:64
  37.1 1.5 %collective-permute-start.12 = (bf16[96,1024]{1,0:T(8,128)(2,1)S(1)}, bf16[96,1024]{1,0:T(8,128)(2,1)S(1)}, u32[]{:S(2)}, u32[]{:S(2)}) collective-permute-start(bf16[96,1024]{1,0:T(8,128)(2,1)S(1)} %get-tuple-element.80.refs_6_.refs_0_), channel_id=1, source_target_pairs={{0,2},{1,3},{2,0},{3,1},{4,6},{5,7},{6,4},{7,5},{8,10},{9,11},{10,... | collective-permute-start | bytes 589832 | tf_op jit(solution)/shard_map/ppermute | solution.py:465
  38.6 2.4 %shard_map.116.refs_2_.refs_5_ = f32[96,1024]{1,0:T(8,128)S(1)} custom-call(s32[1]{0:T(128)} %bitcast.core_ref, bf16[4096,1024]{1,0:T(8,128)(2,1)} %refs_0_.16, bf16[48,1024]{1,0:T(8,128)(2,1)S(1)} %get-tuple-element.81.refs_1_.refs_2_, bf16[48,1024]{1,0:T(8,128)(2,1)S(1)} %get-tuple-element.82.refs_2_.refs_3_, ...), custom_call_target="tpu_custom_call" | custom-call | flops 1 | bytes 1 | tf_op jit(solution)/shard_map/pallas_call | solution.py:64
  42.7 2.4 %shard_map.118.refs_2_ = f32[96,1024]{1,0:T(8,128)S(1)} custom-call(s32[1]{0:T(128)} %bitcast.core_ref, bf16[4096,1024]{1,0:T(8,128)(2,1)} %refs_1_.11, bf16[48,1024]{1,0:T(8,128)(2,1)S(1)} %get-tuple-element.83.refs_1_.refs_6_, bf16[48,1024]{1,0:T(8,128)(2,1)S(1)} %get-tuple-element.84.refs_2_, bf16[48,1024]{1,0:T(8,128)(2,1)S(1)} %collective-permute-done.16.refs_3_, ...), custom_call_target="tpu_custom_call" | custom-call | flops 1 | bytes 1 | tf_op jit(solution)/shard_map/pallas_call | solution.py:64
  45.6 1.8 %shard_map.120.refs_2_.refs_3_ = f32[96,1024]{1,0:T(8,128)S(1)} custom-call(s32[1]{0:T(128)} %bitcast.core_ref, bf16[4096,1024]{1,0:T(8,128)(2,1)} %refs_1_.11, bf16[96,1024]{1,0:T(8,128)(2,1)S(1)} %shard_map.119.refs_1_.refs_3_, f32[96,1024]{1,0:T(8,128)S(1)} %shard_map.118.refs_2_, bf16[96,1024]{1,0:T(8,128)(2,1)S(1)} %shard_map.119.refs_1_.refs_3_), custom_call_target="tpu_custom_call" | custom-call | flops 1 | bytes 1 | tf_op jit(solution)/shard_map/pallas_call | solution.py:64
  47.4 1.8 %shard_map.121 = (f32[24,1024]{1,0:T(8,128)S(1)}, bf16[24,1024]{1,0:T(8,128)(2,1)S(1)}, bf16[24,1024]{1,0:T(8,128)(2,1)S(1)}, bf16[24,1024]{1,0:T(8,128)(2,1)S(1)}) custom-call(s32[1]{0:T(128)} %bitcast.core_ref, bf16[4096,1024]{1,0:T(8,128)(2,1)} %refs_1_.11, bf16[96,1024]{1,0:T(8,128)(2,1)S(1)} %collective-permute-done.18.refs_1_, ...), custom_call_target="tpu_custom_call" | custom-call | flops 1 | bytes 1 | tf_op jit(solution)/shard_map/pallas_call | solution.py:64
  49.3 3.2 %collective-permute-start.20 = (bf16[24,1024]{1,0:T(8,128)(2,1)S(1)}, bf16[24,1024]{1,0:T(8,128)(2,1)S(1)}, u32[]{:S(2)}, u32[]{:S(2)}) collective-permute-start(bf16[24,1024]{1,0:T(8,128)(2,1)S(1)} %get-tuple-element.87), channel_id=1, source_target_pairs={{0,8},{4,12},{8,0},{12,4},{1,9},{5,13},{9,1},{13,5},{2,10},{6,14},... | collective-permute-start | bytes 147464 | tf_op jit(solution)/shard_map/ppermute | solution.py:458
  52.4 1.2 %collective-permute-start.21 = (bf16[24,1024]{1,0:T(8,128)(2,1)S(1)}, bf16[24,1024]{1,0:T(8,128)(2,1)S(1)}, u32[]{:S(2)}, u32[]{:S(2)}) collective-permute-start(bf16[24,1024]{1,0:T(8,128)(2,1)S(1)} %get-tuple-element.88), channel_id=1, source_target_pairs={{0,12},{4,8},{8,4},{12,0},{1,13},{5,9},{9,5},{13,1},{2,14},{6,10},... | collective-permute-start | bytes 147464 | tf_op jit(solution)/shard_map/ppermute | solution.py:458
  53.8 2.2 %shard_map.122 = (f32[8,128]{1,0:T(8,128)S(1)}, bf16[1024,1024]{1,0:T(8,128)(2,1)S(1)}, bf16[1024,1024]{1,0:T(8,128)(2,1)S(1)}) custom-call(s32[1]{0:T(128)} %bitcast.core_ref, bf16[4096,1024]{1,0:T(8,128)(2,1)} %refs_1_.11, bf16[4096,1024]{1,0:T(8,128)(2,1)} %refs_1_.11, f32[24,1024]{1,0:T(8,128)S(1)} %get-tuple-element.85.refs_2_.refs_0_), custom_call_target="tpu_custom_call" | custom-call | flops 1 | bytes 1 | tf_op jit(solution)/shard_map/pallas_call | solution.py:64
  56.1 2.3 %collective-permute-done.21.refs_3_ = bf16[24,1024]{1,0:T(8,128)(2,1)S(1)} collective-permute-done((bf16[24,1024]{1,0:T(8,128)(2,1)S(1)}, bf16[24,1024]{1,0:T(8,128)(2,1)S(1)}, u32[]{:S(2)}, u32[]{:S(2)}) %collective-permute-start.21) | collective-permute-done | bytes 49184 | tf_op jit(solution)/shard_map/ppermute | solution.py:458
  58.4 1.3 %collective-permute-start.24 = (bf16[24,1024]{1,0:T(8,128)(2,1)S(1)}, bf16[24,1024]{1,0:T(8,128)(2,1)S(1)}, u32[]{:S(2)}, u32[]{:S(2)}) collective-permute-start(bf16[24,1024]{1,0:T(8,128)(2,1)S(1)} %shard_map.123.refs_2_.refs_0_), channel_id=1, source_target_pairs={{0,12},{4,8},{8,4},{12,0},{1,13},{5,9},{9,5},{13,1},{2,14},{6,10},... | collective-permute-start | bytes 147464 | tf_op jit(solution)/shard_map/ppermute | solution.py:455
  59.7 3.1 %collective-permute-start.22 = (bf16[24,1024]{1,0:T(8,128)(2,1)S(1)}, bf16[24,1024]{1,0:T(8,128)(2,1)S(1)}, u32[]{:S(2)}, u32[]{:S(2)}) collective-permute-start(bf16[24,1024]{1,0:T(8,128)(2,1)S(1)} %shard_map.123.refs_2_.refs_0_), channel_id=1, source_target_pairs={{0,4},{4,0},{8,12},{12,8},{1,5},{5,1},{9,13},{13,9},{2,6},{6,2},{1... | collective-permute-start | bytes 147464 | tf_op jit(solution)/shard_map/ppermute | solution.py:455
  62.8 2.2 %shard_map.124 = (f32[8,128]{1,0:T(8,128)S(1)}, bf16[1024,1024]{1,0:T(8,128)(2,1)S(1)}, bf16[1024,1024]{1,0:T(8,128)(2,1)S(1)}) custom-call(s32[1]{0:T(128)} %bitcast.core_ref, bf16[4096,1024]{1,0:T(8,128)(2,1)} %refs_1_.11, bf16[4096,1024]{1,0:T(8,128)(2,1)} %refs_1_.11, bf16[24,1024]{1,0:T(8,128)(2,1)S(1)} %shard_map.123.refs_2_.refs_0_), custom_call_target="tpu_custom_call" | custom-call | flops 1 | bytes 1 | tf_op jit(solution)/shard_map/pallas_call | solution.py:64
  68.5 1.2 %collective-permute-start.28 = (bf16[96,1024]{1,0:T(8,128)(2,1)S(1)}, bf16[96,1024]{1,0:T(8,128)(2,1)S(1)}, u32[]{:S(2)}, u32[]{:S(2)}) collective-permute-start(bf16[96,1024]{1,0:T(8,128)(2,1)S(1)} %shard_map.128.refs_3_.refs_0_), channel_id=1, source_target_pairs={{0,2},{1,3},{2,0},{3,1},{4,6},{5,7},{6,4},{7,5},{8,10},{9,11},{10,... | collective-permute-start | bytes 589832 | tf_op jit(solution)/shard_map/ppermute | solution.py:465
  70.4 1.1 %collective-permute-start.27 = (bf16[96,1024]{1,0:T(8,128)(2,1)S(1)}, bf16[96,1024]{1,0:T(8,128)(2,1)S(1)}, u32[]{:S(2)}, u32[]{:S(2)}) collective-permute-start(bf16[96,1024]{1,0:T(8,128)(2,1)S(1)} %shard_map.129.refs_9_.refs_0_), channel_id=1, source_target_pairs={{0,2},{1,3},{2,0},{3,1},{4,6},{5,7},{6,4},{7,5},{8,10},{9,11},{10,... | collective-permute-start | bytes 589832 | tf_op jit(solution)/shard_map/ppermute | solution.py:465
  71.6 3.7 %shard_map.130 = (f32[8,128]{1,0:T(8,128)S(1)}, bf16[4096,1024]{1,0:T(8,128)(2,1)}) custom-call(s32[1]{0:T(128)} %bitcast.core_ref, bf16[48,1024]{1,0:T(8,128)(2,1)S(1)} %get-tuple-element.77.refs_1_.refs_0_, bf16[48,1024]{1,0:T(8,128)(2,1)S(1)} %get-tuple-element.78.refs_2_.refs_1_, bf16[48,1024]{1,0:T(8,128)(2,1)S(1)} %get-tuple-element.81.refs_1_.refs_2_, ...), custom_call_target="tpu_custom_call" | custom-call | flops 1 | bytes 1 | tf_op jit(solution)/shard_map/pallas_call | solution.py:64
  75.3 1.1 %collective-permute-done.28.refs_1_ = bf16[96,1024]{1,0:T(8,128)(2,1)S(1)} collective-permute-done((bf16[96,1024]{1,0:T(8,128)(2,1)S(1)}, bf16[96,1024]{1,0:T(8,128)(2,1)S(1)}, u32[]{:S(2)}, u32[]{:S(2)}) %collective-permute-start.28) | collective-permute-done | bytes 196640 | tf_op jit(solution)/shard_map/ppermute | solution.py:465
  77.2 2.4 %shard_map.132 = (f32[8,128]{1,0:T(8,128)S(1)}, bf16[1024,4096]{1,0:T(8,128)(2,1)}, bf16[1024,4096]{1,0:T(8,128)(2,1)}) custom-call(s32[1]{0:T(128)} %bitcast.core_ref, bf16[96,1024]{1,0:T(8,128)(2,1)S(1)} %shard_map.104.refs_0_.refs_3_, bf16[2,32,1024]{2,1,0:T(8,128)(2,1)S(1)} %get-tuple-element.100.refs_1_.refs_4_, ...), custom_call_target="tpu_custom_call" | custom-call | flops 1 | bytes 1 | tf_op jit(solution)/shard_map/pallas_call | solution.py:64
  80.7 3.7 %shard_map.134 = (f32[8,128]{1,0:T(8,128)S(1)}, bf16[1024,4096]{1,0:T(8,128)(2,1)}, bf16[1024,4096]{1,0:T(8,128)(2,1)}) custom-call(s32[1]{0:T(128)} %bitcast.core_ref, bf16[96,1024]{1,0:T(8,128)(2,1)S(1)} %shard_map.104.refs_0_.refs_3_, bf16[2,32,1024]{2,1,0:T(8,128)(2,1)S(1)} %collective-permute-done.32.refs_1_, ...), custom_call_target="tpu_custom_call", output_to_operand_aliasing={{1}: (9, {}), {2}: (10, {})} | custom-call | flops 1 | bytes 1 | tf_op jit(solution)/shard_map/pallas_call | solution.py:64
  84.5 2.4 %shard_map.135 = (bf16[1024,4096]{1,0:T(8,128)(2,1)}, bf16[1024,4096]{1,0:T(8,128)(2,1)}) custom-call(s32[1]{0:T(128)} %bitcast.core_ref, bf16[96,1024]{1,0:T(8,128)(2,1)S(1)} %shard_map.104.refs_0_.refs_3_, bf16[2,32,1024]{2,1,0:T(8,128)(2,1)S(1)} %collective-permute-done.29.refs_1_, ...), custom_call_target="tpu_custom_call", output_to_operand_aliasing={{0}: (6, {}), {1}: (7, {})} | custom-call | flops 1 | bytes 1 | tf_op jit(solution)/shard_map/pallas_call | solution.py:64
  (77 shorter events, 14.6 us)
Async XLA Ops:
  0.6 10.5 %collective-permute-start.1 = (bf16[24,1024]{1,0:T(8,128)(2,1)}, bf16[24,1024]{1,0:T(8,128)(2,1)S(1)}, u32[]{:S(2)}, u32[]{:S(2)}) collective-permute-start(bf16[24,1024]{1,0:T(8,128)(2,1)} %refs_0_.12), channel_id=1, source_target_pairs={{0,8},{4,12},{8,0},{12,4},{1,9},{5,13},{9,1},{13,5},{2,10},{6,14},... | collective-permute-start | bytes 147464 | tf_op jit(solution)/shard_map/ppermute | solution.py:455
  4.7 6.4 %collective-permute-start = (bf16[24,1024]{1,0:T(8,128)(2,1)}, bf16[24,1024]{1,0:T(8,128)(2,1)S(1)}, u32[]{:S(2)}, u32[]{:S(2)}) collective-permute-start(bf16[24,1024]{1,0:T(8,128)(2,1)} %refs_0_.12), channel_id=1, source_target_pairs={{0,4},{4,0},{8,12},{12,8},{1,5},{5,1},{9,13},{13,9},{2,6},{6,2},{1... | collective-permute-start | bytes 147464 | tf_op jit(solution)/shard_map/ppermute | solution.py:455
  6.3 6.1 %collective-permute-start.2 = (bf16[24,1024]{1,0:T(8,128)(2,1)}, bf16[24,1024]{1,0:T(8,128)(2,1)S(1)}, u32[]{:S(2)}, u32[]{:S(2)}) collective-permute-start(bf16[24,1024]{1,0:T(8,128)(2,1)} %refs_0_.12), channel_id=1, source_target_pairs={{0,12},{4,8},{8,4},{12,0},{1,13},{5,9},{9,5},{13,1},{2,14},{6,10},... | collective-permute-start | bytes 147464 | tf_op jit(solution)/shard_map/ppermute | solution.py:455
  13.3 1.8 %collective-permute-start.3 = (bf16[2,96,1024]{2,1,0:T(8,128)(2,1)S(1)}, bf16[2,96,1024]{2,1,0:T(8,128)(2,1)S(1)}, u32[]{:S(2)}, u32[]{:S(2)}) collective-permute-start(bf16[2,96,1024]{2,1,0:T(8,128)(2,1)S(1)} %shard_map.105.refs_3_), channel_id=1, source_target_pairs={{0,1},{1,0},{2,3},{3,2},{4,5},{5,4},{6,7},{7,6},{8,9},{9,8},{10,11... | collective-permute-start | bytes 1179656 | tf_op jit(solution)/shard_map/ppermute | solution.py:461
  14.1 5.5 %collective-permute-start.4 = (bf16[2,96,1024]{2,1,0:T(8,128)(2,1)S(1)}, bf16[2,96,1024]{2,1,0:T(8,128)(2,1)S(1)}, u32[]{:S(2)}, u32[]{:S(2)}) collective-permute-start(bf16[2,96,1024]{2,1,0:T(8,128)(2,1)S(1)} %shard_map.106.refs_4_), channel_id=1, source_target_pairs={{0,1},{1,0},{2,3},{3,2},{4,5},{5,4},{6,7},{7,6},{8,9},{9,8},{10,11... | collective-permute-start | bytes 1179656 | tf_op jit(solution)/shard_map/ppermute | solution.py:461
  15.9 15.0 %collective-permute-start.9 = (bf16[2,96,1024]{2,1,0:T(8,128)(2,1)S(1)}, bf16[2,96,1024]{2,1,0:T(8,128)(2,1)S(1)}, u32[]{:S(2)}, u32[]{:S(2)}) collective-permute-start(bf16[2,96,1024]{2,1,0:T(8,128)(2,1)S(1)} %shard_map.107.refs_2_.refs_0_), channel_id=1, source_target_pairs={{0,2},{1,3},{2,0},{3,1},{4,6},{5,7},{6,4},{7,5},{8,10},{9,11},{10,... | collective-permute-start | bytes 1179656 | tf_op jit(solution)/shard_map/ppermute | solution.py:465
  20.5 15.7 %collective-permute-start.5 = (bf16[2,96,1024]{2,1,0:T(8,128)(2,1)S(1)}, bf16[2,96,1024]{2,1,0:T(8,128)(2,1)S(1)}, u32[]{:S(2)}, u32[]{:S(2)}) collective-permute-start(bf16[2,96,1024]{2,1,0:T(8,128)(2,1)S(1)} %shard_map.109.refs_3_.refs_0_), channel_id=1, source_target_pairs={{0,2},{1,3},{2,0},{3,1},{4,6},{5,7},{6,4},{7,5},{8,10},{9,11},{10,... | collective-permute-start | bytes 1179656 | tf_op jit(solution)/shard_map/ppermute | solution.py:465
  25.1 4.2 %collective-permute-start.7 = (bf16[2,32,2048]{2,1,0:T(8,128)(2,1)S(1)}, bf16[2,32,2048]{2,1,0:T(8,128)(2,1)S(1)}, u32[]{:S(2)}, u32[]{:S(2)}) collective-permute-start(bf16[2,32,2048]{2,1,0:T(8,128)(2,1)S(1)} %get-tuple-element.74), channel_id=1, source_target_pairs={{0,1},{1,0},{2,3},{3,2},{4,5},{5,4},{6,7},{7,6},{8,9},{9,8},{10,11... | collective-permute-start | bytes 786440 | tf_op jit(solution)/shard_map/ppermute | solution.py:461
  25.2 4.1 %collective-permute-start.8 = (bf16[2,32,2048]{2,1,0:T(8,128)(2,1)S(1)}, bf16[2,32,2048]{2,1,0:T(8,128)(2,1)S(1)}, u32[]{:S(2)}, u32[]{:S(2)}) collective-permute-start(bf16[2,32,2048]{2,1,0:T(8,128)(2,1)S(1)} %get-tuple-element.75), channel_id=1, source_target_pairs={{0,1},{1,0},{2,3},{3,2},{4,5},{5,4},{6,7},{7,6},{8,9},{9,8},{10,11... | collective-permute-start | bytes 786440 | tf_op jit(solution)/shard_map/ppermute | solution.py:461
  25.7 3.7 %collective-permute-start.6 = (bf16[2,32,2048]{2,1,0:T(8,128)(2,1)S(1)}, bf16[2,32,2048]{2,1,0:T(8,128)(2,1)S(1)}, u32[]{:S(2)}, u32[]{:S(2)}) collective-permute-start(bf16[2,32,2048]{2,1,0:T(8,128)(2,1)S(1)} %get-tuple-element.69.refs_4_), channel_id=1, source_target_pairs={{0,1},{1,0},{2,3},{3,2},{4,5},{5,4},{6,7},{7,6},{8,9},{9,8},{10,11... | collective-permute-start | bytes 786440 | tf_op jit(solution)/shard_map/ppermute | solution.py:461
  31.2 2.1 %collective-permute-start.10 = (bf16[48,1024]{1,0:T(8,128)(2,1)S(1)}, bf16[48,1024]{1,0:T(8,128)(2,1)S(1)}, u32[]{:S(2)}, u32[]{:S(2)}) collective-permute-start(bf16[48,1024]{1,0:T(8,128)(2,1)S(1)} %get-tuple-element.77.refs_1_.refs_0_), channel_id=1, source_target_pairs={{0,1},{1,0},{2,3},{3,2},{4,5},{5,4},{6,7},{7,6},{8,9},{9,8},{10,11... | collective-permute-start | bytes 294920 | tf_op jit(solution)/shard_map/ppermute | solution.py:461
  31.7 1.6 %collective-permute-start.11 = (bf16[48,1024]{1,0:T(8,128)(2,1)S(1)}, bf16[48,1024]{1,0:T(8,128)(2,1)S(1)}, u32[]{:S(2)}, u32[]{:S(2)}) collective-permute-start(bf16[48,1024]{1,0:T(8,128)(2,1)S(1)} %get-tuple-element.78.refs_2_.refs_1_), channel_id=1, source_target_pairs={{0,1},{1,0},{2,3},{3,2},{4,5},{5,4},{6,7},{7,6},{8,9},{9,8},{10,11... | collective-permute-start | bytes 294920 | tf_op jit(solution)/shard_map/ppermute | solution.py:461
  31.7 9.3 %collective-permute-start.13 = (bf16[96,1024]{1,0:T(8,128)(2,1)S(1)}, bf16[96,1024]{1,0:T(8,128)(2,1)S(1)}, u32[]{:S(2)}, u32[]{:S(2)}) collective-permute-start(bf16[96,1024]{1,0:T(8,128)(2,1)S(1)} %get-tuple-element.79.refs_5_.refs_0_), channel_id=1, source_target_pairs={{0,2},{1,3},{2,0},{3,1},{4,6},{5,7},{6,4},{7,5},{8,10},{9,11},{10,... | collective-permute-start | bytes 589832 | tf_op jit(solution)/shard_map/ppermute | solution.py:465
  36.5 2.1 %collective-permute-start.14 = (bf16[48,1024]{1,0:T(8,128)(2,1)S(1)}, bf16[48,1024]{1,0:T(8,128)(2,1)S(1)}, u32[]{:S(2)}, u32[]{:S(2)}) collective-permute-start(bf16[48,1024]{1,0:T(8,128)(2,1)S(1)} %get-tuple-element.81.refs_1_.refs_2_), channel_id=1, source_target_pairs={{0,1},{1,0},{2,3},{3,2},{4,5},{5,4},{6,7},{7,6},{8,9},{9,8},{10,11... | collective-permute-start | bytes 294920 | tf_op jit(solution)/shard_map/ppermute | solution.py:461
  36.6 2.0 %collective-permute-start.15 = (bf16[48,1024]{1,0:T(8,128)(2,1)S(1)}, bf16[48,1024]{1,0:T(8,128)(2,1)S(1)}, u32[]{:S(2)}, u32[]{:S(2)}) collective-permute-start(bf16[48,1024]{1,0:T(8,128)(2,1)S(1)} %get-tuple-element.82.refs_2_.refs_3_), channel_id=1, source_target_pairs={{0,1},{1,0},{2,3},{3,2},{4,5},{5,4},{6,7},{7,6},{8,9},{9,8},{10,11... | collective-permute-start | bytes 294920 | tf_op jit(solution)/shard_map/ppermute | solution.py:461
  37.1 8.0 %collective-permute-start.12 = (bf16[96,1024]{1,0:T(8,128)(2,1)S(1)}, bf16[96,1024]{1,0:T(8,128)(2,1)S(1)}, u32[]{:S(2)}, u32[]{:S(2)}) collective-permute-start(bf16[96,1024]{1,0:T(8,128)(2,1)S(1)} %get-tuple-element.80.refs_6_.refs_0_), channel_id=1, source_target_pairs={{0,2},{1,3},{2,0},{3,1},{4,6},{5,7},{6,4},{7,5},{8,10},{9,11},{10,... | collective-permute-start | bytes 589832 | tf_op jit(solution)/shard_map/ppermute | solution.py:465
  45.2 2.2 %collective-permute-start.18 = (bf16[96,1024]{1,0:T(8,128)(2,1)S(1)}, bf16[96,1024]{1,0:T(8,128)(2,1)S(1)}, u32[]{:S(2)}, u32[]{:S(2)}) collective-permute-start(bf16[96,1024]{1,0:T(8,128)(2,1)S(1)} %shard_map.119.refs_1_.refs_3_), channel_id=1, source_target_pairs={{0,1},{1,0},{2,3},{3,2},{4,5},{5,4},{6,7},{7,6},{8,9},{9,8},{10,11... | collective-permute-start | bytes 589832 | tf_op jit(solution)/shard_map/ppermute | solution.py:461
  49.2 6.8 %collective-permute-start.19 = (bf16[24,1024]{1,0:T(8,128)(2,1)S(1)}, bf16[24,1024]{1,0:T(8,128)(2,1)S(1)}, u32[]{:S(2)}, u32[]{:S(2)}) collective-permute-start(bf16[24,1024]{1,0:T(8,128)(2,1)S(1)} %get-tuple-element.86), channel_id=1, source_target_pairs={{0,4},{4,0},{8,12},{12,8},{1,5},{5,1},{9,13},{13,9},{2,6},{6,2},{1... | collective-permute-start | bytes 147464 | tf_op jit(solution)/shard_map/ppermute | solution.py:458
  49.3 6.8 %collective-permute-start.20 = (bf16[24,1024]{1,0:T(8,128)(2,1)S(1)}, bf16[24,1024]{1,0:T(8,128)(2,1)S(1)}, u32[]{:S(2)}, u32[]{:S(2)}) collective-permute-start(bf16[24,1024]{1,0:T(8,128)(2,1)S(1)} %get-tuple-element.87), channel_id=1, source_target_pairs={{0,8},{4,12},{8,0},{12,4},{1,9},{5,13},{9,1},{13,5},{2,10},{6,14},... | collective-permute-start | bytes 147464 | tf_op jit(solution)/shard_map/ppermute | solution.py:458
  52.4 5.9 %collective-permute-start.21 = (bf16[24,1024]{1,0:T(8,128)(2,1)S(1)}, bf16[24,1024]{1,0:T(8,128)(2,1)S(1)}, u32[]{:S(2)}, u32[]{:S(2)}) collective-permute-start(bf16[24,1024]{1,0:T(8,128)(2,1)S(1)} %get-tuple-element.88), channel_id=1, source_target_pairs={{0,12},{4,8},{8,4},{12,0},{1,13},{5,9},{9,5},{13,1},{2,14},{6,10},... | collective-permute-start | bytes 147464 | tf_op jit(solution)/shard_map/ppermute | solution.py:458
  58.4 6.6 %collective-permute-start.24 = (bf16[24,1024]{1,0:T(8,128)(2,1)S(1)}, bf16[24,1024]{1,0:T(8,128)(2,1)S(1)}, u32[]{:S(2)}, u32[]{:S(2)}) collective-permute-start(bf16[24,1024]{1,0:T(8,128)(2,1)S(1)} %shard_map.123.refs_2_.refs_0_), channel_id=1, source_target_pairs={{0,12},{4,8},{8,4},{12,0},{1,13},{5,9},{9,5},{13,1},{2,14},{6,10},... | collective-permute-start | bytes 147464 | tf_op jit(solution)/shard_map/ppermute | solution.py:455
  59.7 5.7 %collective-permute-start.23 = (bf16[24,1024]{1,0:T(8,128)(2,1)S(1)}, bf16[24,1024]{1,0:T(8,128)(2,1)S(1)}, u32[]{:S(2)}, u32[]{:S(2)}) collective-permute-start(bf16[24,1024]{1,0:T(8,128)(2,1)S(1)} %shard_map.123.refs_2_.refs_0_), channel_id=1, source_target_pairs={{0,8},{4,12},{8,0},{12,4},{1,9},{5,13},{9,1},{13,5},{2,10},{6,14},... | collective-permute-start | bytes 147464 | tf_op jit(solution)/shard_map/ppermute | solution.py:455
  59.7 5.7 %collective-permute-start.22 = (bf16[24,1024]{1,0:T(8,128)(2,1)S(1)}, bf16[24,1024]{1,0:T(8,128)(2,1)S(1)}, u32[]{:S(2)}, u32[]{:S(2)}) collective-permute-start(bf16[24,1024]{1,0:T(8,128)(2,1)S(1)} %shard_map.123.refs_2_.refs_0_), channel_id=1, source_target_pairs={{0,4},{4,0},{8,12},{12,8},{1,5},{5,1},{9,13},{13,9},{2,6},{6,2},{1... | collective-permute-start | bytes 147464 | tf_op jit(solution)/shard_map/ppermute | solution.py:455
  67.0 2.6 %collective-permute-start.25 = (bf16[96,1024]{1,0:T(8,128)(2,1)S(1)}, bf16[96,1024]{1,0:T(8,128)(2,1)S(1)}, u32[]{:S(2)}, u32[]{:S(2)}) collective-permute-start(bf16[96,1024]{1,0:T(8,128)(2,1)S(1)} %shard_map.127.refs_3_), channel_id=1, source_target_pairs={{0,1},{1,0},{2,3},{3,2},{4,5},{5,4},{6,7},{7,6},{8,9},{9,8},{10,11... | collective-permute-start | bytes 589832 | tf_op jit(solution)/shard_map/ppermute | solution.py:461
  68.5 8.0 %collective-permute-start.28 = (bf16[96,1024]{1,0:T(8,128)(2,1)S(1)}, bf16[96,1024]{1,0:T(8,128)(2,1)S(1)}, u32[]{:S(2)}, u32[]{:S(2)}) collective-permute-start(bf16[96,1024]{1,0:T(8,128)(2,1)S(1)} %shard_map.128.refs_3_.refs_0_), channel_id=1, source_target_pairs={{0,2},{1,3},{2,0},{3,1},{4,6},{5,7},{6,4},{7,5},{8,10},{9,11},{10,... | collective-permute-start | bytes 589832 | tf_op jit(solution)/shard_map/ppermute | solution.py:465
  70.4 9.4 %collective-permute-start.27 = (bf16[96,1024]{1,0:T(8,128)(2,1)S(1)}, bf16[96,1024]{1,0:T(8,128)(2,1)S(1)}, u32[]{:S(2)}, u32[]{:S(2)}) collective-permute-start(bf16[96,1024]{1,0:T(8,128)(2,1)S(1)} %shard_map.129.refs_9_.refs_0_), channel_id=1, source_target_pairs={{0,2},{1,3},{2,0},{3,1},{4,6},{5,7},{6,4},{7,5},{8,10},{9,11},{10,... | collective-permute-start | bytes 589832 | tf_op jit(solution)/shard_map/ppermute | solution.py:465
  76.6 4.0 %collective-permute-start.32 = (bf16[2,32,1024]{2,1,0:T(8,128)(2,1)S(1)}, bf16[2,32,1024]{2,1,0:T(8,128)(2,1)S(1)}, u32[]{:S(2)}, u32[]{:S(2)}) collective-permute-start(bf16[2,32,1024]{2,1,0:T(8,128)(2,1)S(1)} %get-tuple-element.100.refs_1_.refs_4_), channel_id=1, source_target_pairs={{0,1},{1,0},{2,3},{3,2},{4,5},{5,4},{6,7},{7,6},{8,9},{9,8},{10,11... | collective-permute-start | bytes 393224 | tf_op jit(solution)/shard_map/ppermute | solution.py:461
  76.6 4.1 %collective-permute-start.33 = (bf16[2,32,1024]{2,1,0:T(8,128)(2,1)S(1)}, bf16[2,32,1024]{2,1,0:T(8,128)(2,1)S(1)}, u32[]{:S(2)}, u32[]{:S(2)}) collective-permute-start(bf16[2,32,1024]{2,1,0:T(8,128)(2,1)S(1)} %get-tuple-element.101.refs_2_), channel_id=1, source_target_pairs={{0,1},{1,0},{2,3},{3,2},{4,5},{5,4},{6,7},{7,6},{8,9},{9,8},{10,11... | collective-permute-start | bytes 393224 | tf_op jit(solution)/shard_map/ppermute | solution.py:461
  77.1 3.6 %collective-permute-start.34 = (bf16[2,32,1024]{2,1,0:T(8,128)(2,1)S(1)}, bf16[2,32,1024]{2,1,0:T(8,128)(2,1)S(1)}, u32[]{:S(2)}, u32[]{:S(2)}) collective-permute-start(bf16[2,32,1024]{2,1,0:T(8,128)(2,1)S(1)} %get-tuple-element.102.refs_3_), channel_id=1, source_target_pairs={{0,1},{1,0},{2,3},{3,2},{4,5},{5,4},{6,7},{7,6},{8,9},{9,8},{10,11... | collective-permute-start | bytes 393224 | tf_op jit(solution)/shard_map/ppermute | solution.py:461
  80.0 4.5 %collective-permute-start.29 = (bf16[2,32,1024]{2,1,0:T(8,128)(2,1)S(1)}, bf16[2,32,1024]{2,1,0:T(8,128)(2,1)S(1)}, u32[]{:S(2)}, u32[]{:S(2)}) collective-permute-start(bf16[2,32,1024]{2,1,0:T(8,128)(2,1)S(1)} %get-tuple-element.104.refs_4_.refs_7_), channel_id=1, source_target_pairs={{0,1},{1,0},{2,3},{3,2},{4,5},{5,4},{6,7},{7,6},{8,9},{9,8},{10,11... | collective-permute-start | bytes 393224 | tf_op jit(solution)/shard_map/ppermute | solution.py:461
  80.2 4.3 %collective-permute-start.30 = (bf16[2,32,1024]{2,1,0:T(8,128)(2,1)S(1)}, bf16[2,32,1024]{2,1,0:T(8,128)(2,1)S(1)}, u32[]{:S(2)}, u32[]{:S(2)}) collective-permute-start(bf16[2,32,1024]{2,1,0:T(8,128)(2,1)S(1)} %get-tuple-element.105.refs_5_), channel_id=1, source_target_pairs={{0,1},{1,0},{2,3},{3,2},{4,5},{5,4},{6,7},{7,6},{8,9},{9,8},{10,11... | collective-permute-start | bytes 393224 | tf_op jit(solution)/shard_map/ppermute | solution.py:461
  80.5 4.0 %collective-permute-start.31 = (bf16[2,32,1024]{2,1,0:T(8,128)(2,1)S(1)}, bf16[2,32,1024]{2,1,0:T(8,128)(2,1)S(1)}, u32[]{:S(2)}, u32[]{:S(2)}) collective-permute-start(bf16[2,32,1024]{2,1,0:T(8,128)(2,1)S(1)} %get-tuple-element.106.refs_6_), channel_id=1, source_target_pairs={{0,1},{1,0},{2,3},{3,2},{4,5},{5,4},{6,7},{7,6},{8,9},{9,8},{10,11... | collective-permute-start | bytes 393224 | tf_op jit(solution)/shard_map/ppermute | solution.py:461
  (5 other events, 63.4 us)

commit v5 on v4

--- a/solution.py
+++ b/solution.py
@@ -243,7 +243,7 @@
     return call(body, order, [own, *others], pieces_of(*own.shape, pieces))
 
 
-def contract(order, terms, weight, carried, groups=0):
+def contract(order, terms, weight, carried, groups=0, brought=(), ahead=()):
     pieces = len(terms[0][0])
     tokens, chunk = terms[0][0][0].shape[0] * pieces, terms[0][0][0].shape[1]
     width = weight.shape[1]
@@ -251,46 +251,61 @@
     count = len(terms) * pieces
     high = min(256, chunk)
     parts = chunk // high
+    wanted = ([] if brought else [t[1:] for t in terms]) + [a[1:] for a in ahead]
+    streamed = len(wanted) - len(ahead)
+    given = len(brought) or 1
+    results = max(groups, 1)
 
     def body(core_ref, *refs):
-        w_ref, *refs, held, sems = refs
+        w_refs, next_refs, refs = refs[:given], refs[given:][: len(ahead)], refs[given + len(ahead) :]
         copies = []
-        for n, (_, side, index) in enumerate(terms):
-            start = place(core_ref, side, index, chunk)
-            for r in range(parts):
-                m = n * parts + r
-                here = pl.ds(pl.multiple_of(start + r * high, high), high)
-                copies.append(pltpu.make_async_copy(w_ref.at[here, :], held.at[m], sems.at[m]))
-                copies[-1].start()
+        if wanted:
+            *refs, sems = refs
+            if streamed:
+                *refs, held = refs
+            for n, (side, index) in enumerate(wanted):
+                start = place(core_ref, side, index, chunk)
+                for r in range(parts):
+                    m = n * parts + r
+                    here = pl.ds(pl.multiple_of(start + r * high, high), high)
+                    if n < streamed:
+                        source, target = w_refs[0], held.at[m]
+                    else:
+                        source = next_refs[n - streamed]
+                        target = refs[n - len(wanted)].at[r * high : (r + 1) * high, :]
+                    copies.append(pltpu.make_async_copy(source.at[here, :], target, sems.at[m]))
+                    copies[-1].start()
         total = refs[count][...] if carried is not None else None
         for n in range(len(terms)):
             left = joined(refs[n * pieces : (n + 1) * pieces])
             for r in range(parts):
-                m = n * parts + r
-                copies[m].wait()
-                term = jnp.dot(
-                    left[:, r * high : (r + 1) * high], held[m], preferred_element_type=F32
-                )
+                here = slice(r * high, (r + 1) * high)
+                if brought:
+                    right = w_refs[n][here, :]
+                else:
+                    copies[n * parts + r].wait()
+                    right = held[n * parts + r]
+                term = jnp.dot(left[:, here], right, preferred_element_type=F32)
                 total = term if total is None else total + term
-        outs = refs[count + (carried is not None) :]
+        outs = refs[count + (carried is not None) :][:results]
         for p, out in enumerate(outs):
             out[...] = total[p * rows : (p + 1) * rows, :].astype(out.dtype)
-
-    out_shape = [shape_of((rows, width), BF16 if p else F32) for p in range(max(groups, 1))]
+        for copy in copies[streamed * parts :]:
+            copy.wait()
+
+    out_shape = [shape_of((rows, width), BF16 if p else F32) for p in range(results)]
     outs = call(
         body,
         order,
-        [InHbm(weight)]
+        (list(brought) or [InHbm(weight)])
+        + [InHbm(a[0]) for a in ahead]
         + [piece for t in terms for piece in t[0]]
         + ([carried] if carried is not None else []),
-        out_shape,
-        scratch=[
-            pltpu.VMEM((len(terms) * parts, high, width), BF16),
-            pltpu.SemaphoreType.DMA((len(terms) * parts,)),
-        ],
-        mib=4 + 2 * len(terms),
-    )
-    return outs if groups else outs[0]
+        out_shape + [pltpu.VMEM((chunk, width), weight.dtype) for _ in ahead],
+        scratch=([pltpu.VMEM((streamed * parts, high, width), BF16)] if streamed else [])
+        + ([pltpu.SemaphoreType.DMA((len(wanted) * parts,))] if wanted else []),
+    )
+    return outs[:results] if groups else outs[0], outs[results:]
 
 
 def weigh(order, own, others, curvature):
@@ -490,13 +505,19 @@
     held = bring(order, [(w, 1, 0, i) for w in probe for i in each])
     (tangents,) = project(order, rows, [held[:CHUNKS], held[CHUNKS:]], sent, F32)
 
-    acted, carried, tan_others = [], None, []
+    acted, carried, tan_others, brought = [], None, [], ()
     for i in each:
         acted.append(activate(order, sums[i], others[i], tangents, i))
         tan_others.append(over_chips(acted[i][0]))
         hidden = (acted[i][3:], 0, i)
         hidden_other = ([to_core(piece) for piece in hidden[0]], 1, i)
-        carried = contract(order, [hidden, hidden_other], down_vector, carried)
+        if i < CHUNKS - 1:
+            ahead = [(down_vector, side, i + 1) for side in (0, 1)]
+        else:
+            ahead = [(down_weight, side, 0) for side in (0, 1)]
+        carried, brought = contract(
+            order, [hidden, hidden_other], down_vector, carried, 0, brought, ahead
+        )
         acted[i] = (*acted[i][:3], hidden, hidden_other)
     for i in each:
         last = i == CHUNKS - 1
@@ -504,10 +525,13 @@
         tan_other = [to_core(piece) for piece in hidden_tan]
         terms = [(hidden_tan, 0, i), (tan_other, 1, i)]
         if not last:
-            carried = contract(order, terms, down_weight, carried)
+            ahead = [(down_weight, 0, i + 1)] if False else []
+            carried, brought = contract(order, terms, down_weight, carried, 0, brought, ahead)
         else:
-            carried = contract(order, terms[:1], down_weight, carried)
-            carried = contract(order, terms[1:], down_weight, carried, groups)
+            carried, brought = contract(
+                order, terms[:1], down_weight, carried, 0, brought, [(down_weight, 1, i)]
+            )
+            carried, _ = contract(order, terms[1:], down_weight, carried, groups, brought)
     held = bring(order, [(down_weight, 0, 1, i) for i in each])
     weighted_mine = weigh(
         order, carried[0], [back_over_dp(carried[p], p) for p in range(1, groups)], mine

time: 87.3 us -> 85.4 us (0.978)
  transfers between devices with their start and end apart: 35 -> 35, of which waited for: 10 -> 10; matrix products, arithmetic and copies ran while one was open for 0% -> 0% of each run, Pallas kernels for 52% -> 54%
where the time goes in v5:
time: 85.4 us; the launch traced here: 85.2 us
  Pallas kernels  50.2 us (59%)
  starting transfers between devices  26.6 us (31%)
  waiting for transfers between devices  7.02 us (8%)
  between operations  1.17 us (1%)
    pallas_call x33, Pallas kernels, call(): pl.pallas_call(kernel, in_specs=[SMEM] + [HBM if isinstance(o, InHbm) els...  50.2 us
    ppermute x6, starting transfers between devices, over_dp(): lax.ppermute(value, 'dp', [(i, partner(i, step, groups)) for i in range(g...  10.1 us
    ppermute x6, starting transfers between devices, over_chips(): lax.ppermute(value, 'mp', [(2 * i + c, 2 * partner(i, k, chips) + c) for...  7 us
    ppermute x20, starting transfers between devices, to_core(): return lax.ppermute(value, 'mp', [(i, i ^ 1) for i in range(2 * chips)])  5.1 us
    ppermute x3, starting transfers between devices, back_over_dp(): lax.ppermute(value, 'dp', [(i, giver(i, step, groups)) for i in range(gro...  4.44 us
    ppermute x3, waiting for transfers between devices, back_over_dp(): lax.ppermute(value, 'dp', [(i, giver(i, step, groups)) for i in range(gro...  2.28 us
    ppermute x6, waiting for transfers between devices, over_chips(): lax.ppermute(value, 'mp', [(2 * i + c, 2 * partner(i, k, chips) + c) for...  1.74 us
  transfers between devices with their start and end apart: 35, of which 10 were waited for; matrix products, arithmetic and copies ran while one was open for 0% of the time, Pallas kernels for 54%

profile of v5, /device:TPU:0, one launch (start us, length us, event | category | flops | bytes accessed | tf_op | source)
XLA Modules:
  0.0 85.2 jit_solution(1208280816300234505)
XLA Ops:
  0.6 4.1 %collective-permute-start.1 = (bf16[24,1024]{1,0:T(8,128)(2,1)}, bf16[24,1024]{1,0:T(8,128)(2,1)S(1)}, u32[]{:S(2)}, u32[]{:S(2)}) collective-permute-start(bf16[24,1024]{1,0:T(8,128)(2,1)} %refs_0_.9), channel_id=1, source_target_pairs={{0,8},{4,12},{8,0},{12,4},{1,9},{5,13},{9,1},{13,5},{2,10},{6,14},... | collective-permute-start | bytes 147464 | tf_op jit(solution)/shard_map/ppermute | solution.py:470
  4.7 1.6 %collective-permute-start = (bf16[24,1024]{1,0:T(8,128)(2,1)}, bf16[24,1024]{1,0:T(8,128)(2,1)S(1)}, u32[]{:S(2)}, u32[]{:S(2)}) collective-permute-start(bf16[24,1024]{1,0:T(8,128)(2,1)} %refs_0_.9), channel_id=1, source_target_pairs={{0,4},{4,0},{8,12},{12,8},{1,5},{5,1},{9,13},{13,9},{2,6},{6,2},{1... | collective-permute-start | bytes 147464 | tf_op jit(solution)/shard_map/ppermute | solution.py:470
  6.3 4.8 %shard_map.103 = (f32[8,128]{1,0:T(8,128)S(1)}, bf16[1024,1024]{1,0:T(8,128)(2,1)S(1)}, bf16[1024,1024]{1,0:T(8,128)(2,1)S(1)}, bf16[1024,1024]{1,0:T(8,128)(2,1...) custom-call(s32[1]{0:T(128)} %bitcast.core_ref, ...), custom_call_target="tpu_custom_call" | custom-call | flops 1 | bytes 1 | tf_op jit(solution)/shard_map/pallas_call | solution.py:64
  11.2 1.2 %collective-permute-done.2.refs_3_ = bf16[24,1024]{1,0:T(8,128)(2,1)S(1)} collective-permute-done((bf16[24,1024]{1,0:T(8,128)(2,1)}, bf16[24,1024]{1,0:T(8,128)(2,1)S(1)}, u32[]{:S(2)}, u32[]{:S(2)}) %collective-permute-start.2) | collective-permute-done | bytes 49184 | tf_op jit(solution)/shard_map/ppermute | solution.py:470
  12.4 0.8 shard_map.105.refs_3_
  15.0 0.8 shard_map.107.refs_2_.refs_0_
  15.9 1.6 %collective-permute-start.9 = (bf16[2,96,1024]{2,1,0:T(8,128)(2,1)S(1)}, bf16[2,96,1024]{2,1,0:T(8,128)(2,1)S(1)}, u32[]{:S(2)}, u32[]{:S(2)}) collective-permute-start(bf16[2,96,1024]{2,1,0:T(8,128)(2,1)S(1)} %shard_map.107.refs_2_.refs_0_), channel_id=1, source_target_pairs={{0,2},{1,3},{2,0},{3,1},{4,6},{5,7},{6,4},{7,5},{8,10},{9,11},{10,... | collective-permute-start | bytes 1179656 | tf_op jit(solution)/shard_map/ppermute | solution.py:480
  17.4 2.2 %shard_map.108 = (f32[8,128]{1,0:T(8,128)S(1)}, bf16[1024,1024]{1,0:T(8,128)(2,1)S(1)}, bf16[1024,1024]{1,0:T(8,128)(2,1)S(1)}) custom-call(s32[1]{0:T(128)} %bitcast.core_ref, bf16[1024,4096]{1,0:T(8,128)(2,1)} %refs_0_.10, bf16[1024,4096]{1,0:T(8,128)(2,1)} %refs_1_.9, bf16[2,96,1024]{2,1,0:T(8,128)(2,1)S(1)} %shard_map.107.refs_2_.refs_0_), custom_call_target="tpu_custom_call" | custom-call | flops 1 | bytes 1 | tf_op jit(solution)/shard_map/pallas_call | solution.py:64
  19.7 0.8 shard_map.109.refs_3_.refs_0_
  21.1 4.0 %shard_map.110 = (bf16[2,32,2048]{2,1,0:T(8,128)(2,1)S(1)}, bf16[2,32,2048]{2,1,0:T(8,128)(2,1)S(1)}, bf16[2,32,2048]{2,1,0:T(8,128)(2,1)S(1)}) custom-call(s32[1]{0:T(128)} %bitcast.core_ref, bf16[96,1024]{1,0:T(8,128)(2,1)S(1)} %shard_map.104.refs_0_.refs_3_, bf16[1024,4096]{1,0:T(8,128)(2,1)} %refs_1_.11, bf16[1024,4096]{1,0:T(8,128)(2,1)} %refs_3_.4, ...), custom_call_target="tpu_custom_call" | custom-call | flops 1 | bytes 1 | tf_op jit(solution)/shard_map/pallas_call | solution.py:64
  25.7 3.5 %shard_map.111 = (f32[8,128]{1,0:T(8,128)S(1)}, bf16[1024,1024]{1,0:T(8,128)(2,1)S(1)}, bf16[1024,1024]{1,0:T(8,128)(2,1)S(1)}, bf16[1024,1024]{1,0:T(8,128)(2,1)S(1)}, bf16[1024,1024]{1,0:T(8,128)(2,1)S(1)}) custom-call(s32[1]{0:T(128)} %bitcast.core_ref, bf16[1024,4096]{1,0:T(8,128)(2,1)} %refs_1_.11, bf16[1024,4096]{1,0:T(8,128)(2,1)} %refs_1_.11, ...), custom_call_target="tpu_custom_call" | custom-call | flops 1 | bytes 1 | tf_op jit(solution)/shard_map/pallas_call | solution.py:64
  29.3 1.5 %shard_map.112.refs_2_.refs_3_ = f32[2,96,2048]{2,1,0:T(8,128)S(1)} custom-call(s32[1]{0:T(128)} %bitcast.core_ref, bf16[96,1024]{1,0:T(8,128)(2,1)S(1)} %shard_map.104.refs_0_.refs_3_, bf16[1024,1024]{1,0:T(8,128)(2,1)S(1)} %get-tuple-element.78.refs_1_, bf16[1024,1024]{1,0:T(8,128)(2,1)S(1)} %get-tuple-element.79.refs_2_, ...), custom_call_target="tpu_custom_call" | custom-call | flops 1 | bytes 1 | tf_op jit(solution)/shard_map/pallas_call | solution.py:64
  31.7 1.5 %collective-permute-start.15 = (bf16[96,1024]{1,0:T(8,128)(2,1)S(1)}, bf16[96,1024]{1,0:T(8,128)(2,1)S(1)}, u32[]{:S(2)}, u32[]{:S(2)}) collective-permute-start(bf16[96,1024]{1,0:T(8,128)(2,1)S(1)} %get-tuple-element.87.refs_7_.refs_0_), channel_id=1, source_target_pairs={{0,2},{1,3},{2,0},{3,1},{4,6},{5,7},{6,4},{7,5},{8,10},{9,11},{10,... | collective-permute-start | bytes 589832 | tf_op jit(solution)/shard_map/ppermute | solution.py:480
  33.2 3.5 %shard_map.114 = (f32[96,1024]{1,0:T(8,128)S(1)}, bf16[1024,1024]{1,0:T(8,128)(2,1)S(1)}, bf16[1024,1024]{1,0:T(8,128)(2,1)S(1)}) custom-call(s32[1]{0:T(128)} %bitcast.core_ref, bf16[4096,1024]{1,0:T(8,128)(2,1)} %refs_2_.8, bf16[4096,1024]{1,0:T(8,128)(2,1)} %refs_2_.8, bf16[4096,1024]{1,0:T(8,128)(2,1)} %refs_2_.8, ...), custom_call_target="tpu_custom_call" | custom-call | flops 1 | bytes 1 | tf_op jit(solution)/shard_map/pallas_call | solution.py:64
  37.7 1.2 %collective-permute-start.12 = (bf16[96,1024]{1,0:T(8,128)(2,1)S(1)}, bf16[96,1024]{1,0:T(8,128)(2,1)S(1)}, u32[]{:S(2)}, u32[]{:S(2)}) collective-permute-start(bf16[96,1024]{1,0:T(8,128)(2,1)S(1)} %get-tuple-element.89.refs_9_.refs_0_), channel_id=1, source_target_pairs={{0,2},{1,3},{2,0},{3,1},{4,6},{5,7},{6,4},{7,5},{8,10},{9,11},{10,... | collective-permute-start | bytes 589832 | tf_op jit(solution)/shard_map/ppermute | solution.py:480
  38.9 2.9 %shard_map.116 = (f32[96,1024]{1,0:T(8,128)S(1)}, bf16[1024,1024]{1,0:T(8,128)(2,1)S(1)}, bf16[1024,1024]{1,0:T(8,128)(2,1)S(1)}) custom-call(s32[1]{0:T(128)} %bitcast.core_ref, bf16[1024,1024]{1,0:T(8,128)(2,1)S(1)} %get-tuple-element.90.refs_0_, bf16[1024,1024]{1,0:T(8,128)(2,1)S(1)} %get-tuple-element.91.refs_1_, bf16[4096,1024]{1,0:T(8,128)(2,1)} %refs_1_.15, ...), custom_call_target="tpu_custom_call" | custom-call | flops 1 | bytes 1 | tf_op jit(solution)/shard_map/pallas_call | solution.py:64
  44.8 2.2 %shard_map.120 = (f32[96,1024]{1,0:T(8,128)S(1)}, bf16[1024,1024]{1,0:T(8,128)(2,1)S(1)}) custom-call(s32[1]{0:T(128)} %bitcast.core_ref, bf16[4096,1024]{1,0:T(8,128)(2,1)} %refs_1_.15, bf16[4096,1024]{1,0:T(8,128)(2,1)} %refs_1_.15, bf16[96,1024]{1,0:T(8,128)(2,1)S(1)} %shard_map.119.refs_2_.refs_4_, f32[96,1024]{1,0:T(8,128)S(1)} %shard_map.118.refs_2_.refs_3_, ...), custom_call_target="tpu_custom_call" | custom-call | flops 1 | bytes 1 | tf_op jit(solution)/shard_map/pallas_call | solution.py:64
  47.6 3.2 %collective-permute-start.20 = (bf16[24,1024]{1,0:T(8,128)(2,1)S(1)}, bf16[24,1024]{1,0:T(8,128)(2,1)S(1)}, u32[]{:S(2)}, u32[]{:S(2)}) collective-permute-start(bf16[24,1024]{1,0:T(8,128)(2,1)S(1)} %get-tuple-element.103), channel_id=1, source_target_pairs={{0,8},{4,12},{8,0},{12,4},{1,9},{5,13},{9,1},{13,5},{2,10},{6,14},... | collective-permute-start | bytes 147464 | tf_op jit(solution)/shard_map/ppermute | solution.py:473
  50.7 1.2 %collective-permute-start.21 = (bf16[24,1024]{1,0:T(8,128)(2,1)S(1)}, bf16[24,1024]{1,0:T(8,128)(2,1)S(1)}, u32[]{:S(2)}, u32[]{:S(2)}) collective-permute-start(bf16[24,1024]{1,0:T(8,128)(2,1)S(1)} %get-tuple-element.104), channel_id=1, source_target_pairs={{0,12},{4,8},{8,4},{12,0},{1,13},{5,9},{9,5},{13,1},{2,14},{6,10},... | collective-permute-start | bytes 147464 | tf_op jit(solution)/shard_map/ppermute | solution.py:473
  52.1 2.2 %shard_map.122 = (f32[8,128]{1,0:T(8,128)S(1)}, bf16[1024,1024]{1,0:T(8,128)(2,1)S(1)}, bf16[1024,1024]{1,0:T(8,128)(2,1)S(1)}) custom-call(s32[1]{0:T(128)} %bitcast.core_ref, bf16[4096,1024]{1,0:T(8,128)(2,1)} %refs_1_.15, bf16[4096,1024]{1,0:T(8,128)(2,1)} %refs_1_.15, f32[24,1024]{1,0:T(8,128)S(1)} %get-tuple-element.101.refs_2_.refs_0_), custom_call_target="tpu_custom_call" | custom-call | flops 1 | bytes 1 | tf_op jit(solution)/shard_map/pallas_call | solution.py:64
  54.4 2.3 %collective-permute-done.21.refs_3_ = bf16[24,1024]{1,0:T(8,128)(2,1)S(1)} collective-permute-done((bf16[24,1024]{1,0:T(8,128)(2,1)S(1)}, bf16[24,1024]{1,0:T(8,128)(2,1)S(1)}, u32[]{:S(2)}, u32[]{:S(2)}) %collective-permute-start.21) | collective-permute-done | bytes 49184 | tf_op jit(solution)/shard_map/ppermute | solution.py:473
  56.7 1.3 %collective-permute-start.24 = (bf16[24,1024]{1,0:T(8,128)(2,1)S(1)}, bf16[24,1024]{1,0:T(8,128)(2,1)S(1)}, u32[]{:S(2)}, u32[]{:S(2)}) collective-permute-start(bf16[24,1024]{1,0:T(8,128)(2,1)S(1)} %shard_map.123.refs_2_.refs_0_), channel_id=1, source_target_pairs={{0,12},{4,8},{8,4},{12,0},{1,13},{5,9},{9,5},{13,1},{2,14},{6,10},... | collective-permute-start | bytes 147464 | tf_op jit(solution)/shard_map/ppermute | solution.py:470
  58.0 3.1 %collective-permute-start.22 = (bf16[24,1024]{1,0:T(8,128)(2,1)S(1)}, bf16[24,1024]{1,0:T(8,128)(2,1)S(1)}, u32[]{:S(2)}, u32[]{:S(2)}) collective-permute-start(bf16[24,1024]{1,0:T(8,128)(2,1)S(1)} %shard_map.123.refs_2_.refs_0_), channel_id=1, source_target_pairs={{0,4},{4,0},{8,12},{12,8},{1,5},{5,1},{9,13},{13,9},{2,6},{6,2},{1... | collective-permute-start | bytes 147464 | tf_op jit(solution)/shard_map/ppermute | solution.py:470
  61.1 2.2 %shard_map.124 = (f32[8,128]{1,0:T(8,128)S(1)}, bf16[1024,1024]{1,0:T(8,128)(2,1)S(1)}, bf16[1024,1024]{1,0:T(8,128)(2,1)S(1)}) custom-call(s32[1]{0:T(128)} %bitcast.core_ref, bf16[4096,1024]{1,0:T(8,128)(2,1)} %refs_1_.15, bf16[4096,1024]{1,0:T(8,128)(2,1)} %refs_1_.15, bf16[24,1024]{1,0:T(8,128)(2,1)S(1)} %shard_map.123.refs_2_.refs_0_), custom_call_target="tpu_custom_call" | custom-call | flops 1 | bytes 1 | tf_op jit(solution)/shard_map/pallas_call | solution.py:64
  66.8 1.3 %collective-permute-start.28 = (bf16[96,1024]{1,0:T(8,128)(2,1)S(1)}, bf16[96,1024]{1,0:T(8,128)(2,1)S(1)}, u32[]{:S(2)}, u32[]{:S(2)}) collective-permute-start(bf16[96,1024]{1,0:T(8,128)(2,1)S(1)} %shard_map.128.refs_3_.refs_0_), channel_id=1, source_target_pairs={{0,2},{1,3},{2,0},{3,1},{4,6},{5,7},{6,4},{7,5},{8,10},{9,11},{10,... | collective-permute-start | bytes 589832 | tf_op jit(solution)/shard_map/ppermute | solution.py:480
  68.0 0.9 %shard_map.129.refs_9_.refs_0_ = bf16[96,1024]{1,0:T(8,128)(2,1)S(1)} custom-call(s32[1]{0:T(128)} %bitcast.core_ref, bf16[96,1024]{1,0:T(8,128)(2,1)S(1)} %shard_map.125.refs_0_.refs_2_.refs_8_, bf16[1024,1024]{1,0:T(8,128)(2,1)S(1)} %get-tuple-element.107.refs_1_, bf16[96,1024]{1,0:T(8,128)(2,1)S(1)} %collective-permute-done.25.refs_2_, ...), custom_call_target="tpu_custom_call" | custom-call | flops 1 | bytes 1 | tf_op jit(solution)/shard_map/pallas_call | solution.py:64
  69.0 0.9 %collective-permute-start.27 = (bf16[96,1024]{1,0:T(8,128)(2,1)S(1)}, bf16[96,1024]{1,0:T(8,128)(2,1)S(1)}, u32[]{:S(2)}, u32[]{:S(2)}) collective-permute-start(bf16[96,1024]{1,0:T(8,128)(2,1)S(1)} %shard_map.129.refs_9_.refs_0_), channel_id=1, source_target_pairs={{0,2},{1,3},{2,0},{3,1},{4,6},{5,7},{6,4},{7,5},{8,10},{9,11},{10,... | collective-permute-start | bytes 589832 | tf_op jit(solution)/shard_map/ppermute | solution.py:480
  69.9 3.7 %shard_map.130 = (f32[8,128]{1,0:T(8,128)S(1)}, bf16[4096,1024]{1,0:T(8,128)(2,1)}) custom-call(s32[1]{0:T(128)} %bitcast.core_ref, bf16[48,1024]{1,0:T(8,128)(2,1)S(1)} %get-tuple-element.85.refs_3_.refs_0_, bf16[48,1024]{1,0:T(8,128)(2,1)S(1)} %get-tuple-element.86.refs_4_.refs_1_, bf16[48,1024]{1,0:T(8,128)(2,1)S(1)} %get-tuple-element.92.refs_4_.refs_2_, ...), custom_call_target="tpu_custom_call" | custom-call | flops 1 | bytes 1 | tf_op jit(solution)/shard_map/pallas_call | solution.py:64
  73.6 1.0 %collective-permute-done.28.refs_1_ = bf16[96,1024]{1,0:T(8,128)(2,1)S(1)} collective-permute-done((bf16[96,1024]{1,0:T(8,128)(2,1)S(1)}, bf16[96,1024]{1,0:T(8,128)(2,1)S(1)}, u32[]{:S(2)}, u32[]{:S(2)}) %collective-permute-start.28) | collective-permute-done | bytes 196640 | tf_op jit(solution)/shard_map/ppermute | solution.py:480
  75.3 2.4 %shard_map.132 = (f32[8,128]{1,0:T(8,128)S(1)}, bf16[1024,4096]{1,0:T(8,128)(2,1)}, bf16[1024,4096]{1,0:T(8,128)(2,1)}) custom-call(s32[1]{0:T(128)} %bitcast.core_ref, bf16[96,1024]{1,0:T(8,128)(2,1)S(1)} %shard_map.104.refs_0_.refs_3_, bf16[2,32,1024]{2,1,0:T(8,128)(2,1)S(1)} %get-tuple-element.116.refs_1_.refs_4_, ...), custom_call_target="tpu_custom_call" | custom-call | flops 1 | bytes 1 | tf_op jit(solution)/shard_map/pallas_call | solution.py:64
  78.9 3.7 %shard_map.134 = (f32[8,128]{1,0:T(8,128)S(1)}, bf16[1024,4096]{1,0:T(8,128)(2,1)}, bf16[1024,4096]{1,0:T(8,128)(2,1)}) custom-call(s32[1]{0:T(128)} %bitcast.core_ref, bf16[96,1024]{1,0:T(8,128)(2,1)S(1)} %shard_map.104.refs_0_.refs_3_, bf16[2,32,1024]{2,1,0:T(8,128)(2,1)S(1)} %collective-permute-done.32.refs_1_, ...), custom_call_target="tpu_custom_call", output_to_operand_aliasing={{1}: (9, {}), {2}: (10, {})} | custom-call | flops 1 | bytes 1 | tf_op jit(solution)/shard_map/pallas_call | solution.py:64
  82.6 2.4 %shard_map.135 = (bf16[1024,4096]{1,0:T(8,128)(2,1)}, bf16[1024,4096]{1,0:T(8,128)(2,1)}) custom-call(s32[1]{0:T(128)} %bitcast.core_ref, bf16[96,1024]{1,0:T(8,128)(2,1)S(1)} %shard_map.104.refs_0_.refs_3_, bf16[2,32,1024]{2,1,0:T(8,128)(2,1)S(1)} %collective-permute-done.29.refs_1_, ...), custom_call_target="tpu_custom_call", output_to_operand_aliasing={{0}: (6, {}), {1}: (7, {})} | custom-call | flops 1 | bytes 1 | tf_op jit(solution)/shard_map/pallas_call | solution.py:64
  (77 shorter events, 13.9 us)
Async XLA Ops:
  0.6 10.5 %collective-permute-start.1 = (bf16[24,1024]{1,0:T(8,128)(2,1)}, bf16[24,1024]{1,0:T(8,128)(2,1)S(1)}, u32[]{:S(2)}, u32[]{:S(2)}) collective-permute-start(bf16[24,1024]{1,0:T(8,128)(2,1)} %refs_0_.9), channel_id=1, source_target_pairs={{0,8},{4,12},{8,0},{12,4},{1,9},{5,13},{9,1},{13,5},{2,10},{6,14},... | collective-permute-start | bytes 147464 | tf_op jit(solution)/shard_map/ppermute | solution.py:470
  4.7 6.4 %collective-permute-start = (bf16[24,1024]{1,0:T(8,128)(2,1)}, bf16[24,1024]{1,0:T(8,128)(2,1)S(1)}, u32[]{:S(2)}, u32[]{:S(2)}) collective-permute-start(bf16[24,1024]{1,0:T(8,128)(2,1)} %refs_0_.9), channel_id=1, source_target_pairs={{0,4},{4,0},{8,12},{12,8},{1,5},{5,1},{9,13},{13,9},{2,6},{6,2},{1... | collective-permute-start | bytes 147464 | tf_op jit(solution)/shard_map/ppermute | solution.py:470
  6.3 6.1 %collective-permute-start.2 = (bf16[24,1024]{1,0:T(8,128)(2,1)}, bf16[24,1024]{1,0:T(8,128)(2,1)S(1)}, u32[]{:S(2)}, u32[]{:S(2)}) collective-permute-start(bf16[24,1024]{1,0:T(8,128)(2,1)} %refs_0_.9), channel_id=1, source_target_pairs={{0,12},{4,8},{8,4},{12,0},{1,13},{5,9},{9,5},{13,1},{2,14},{6,10},... | collective-permute-start | bytes 147464 | tf_op jit(solution)/shard_map/ppermute | solution.py:470
  13.3 1.8 %collective-permute-start.3 = (bf16[2,96,1024]{2,1,0:T(8,128)(2,1)S(1)}, bf16[2,96,1024]{2,1,0:T(8,128)(2,1)S(1)}, u32[]{:S(2)}, u32[]{:S(2)}) collective-permute-start(bf16[2,96,1024]{2,1,0:T(8,128)(2,1)S(1)} %shard_map.105.refs_3_), channel_id=1, source_target_pairs={{0,1},{1,0},{2,3},{3,2},{4,5},{5,4},{6,7},{7,6},{8,9},{9,8},{10,11... | collective-permute-start | bytes 1179656 | tf_op jit(solution)/shard_map/ppermute | solution.py:476
  14.1 5.5 %collective-permute-start.4 = (bf16[2,96,1024]{2,1,0:T(8,128)(2,1)S(1)}, bf16[2,96,1024]{2,1,0:T(8,128)(2,1)S(1)}, u32[]{:S(2)}, u32[]{:S(2)}) collective-permute-start(bf16[2,96,1024]{2,1,0:T(8,128)(2,1)S(1)} %shard_map.106.refs_4_), channel_id=1, source_target_pairs={{0,1},{1,0},{2,3},{3,2},{4,5},{5,4},{6,7},{7,6},{8,9},{9,8},{10,11... | collective-permute-start | bytes 1179656 | tf_op jit(solution)/shard_map/ppermute | solution.py:476
  15.9 15.0 %collective-permute-start.9 = (bf16[2,96,1024]{2,1,0:T(8,128)(2,1)S(1)}, bf16[2,96,1024]{2,1,0:T(8,128)(2,1)S(1)}, u32[]{:S(2)}, u32[]{:S(2)}) collective-permute-start(bf16[2,96,1024]{2,1,0:T(8,128)(2,1)S(1)} %shard_map.107.refs_2_.refs_0_), channel_id=1, source_target_pairs={{0,2},{1,3},{2,0},{3,1},{4,6},{5,7},{6,4},{7,5},{8,10},{9,11},{10,... | collective-permute-start | bytes 1179656 | tf_op jit(solution)/shard_map/ppermute | solution.py:480
  20.5 16.3 %collective-permute-start.5 = (bf16[2,96,1024]{2,1,0:T(8,128)(2,1)S(1)}, bf16[2,96,1024]{2,1,0:T(8,128)(2,1)S(1)}, u32[]{:S(2)}, u32[]{:S(2)}) collective-permute-start(bf16[2,96,1024]{2,1,0:T(8,128)(2,1)S(1)} %shard_map.109.refs_3_.refs_0_), channel_id=1, source_target_pairs={{0,2},{1,3},{2,0},{3,1},{4,6},{5,7},{6,4},{7,5},{8,10},{9,11},{10,... | collective-permute-start | bytes 1179656 | tf_op jit(solution)/shard_map/ppermute | solution.py:480
  25.1 4.2 %collective-permute-start.7 = (bf16[2,32,2048]{2,1,0:T(8,128)(2,1)S(1)}, bf16[2,32,2048]{2,1,0:T(8,128)(2,1)S(1)}, u32[]{:S(2)}, u32[]{:S(2)}) collective-permute-start(bf16[2,32,2048]{2,1,0:T(8,128)(2,1)S(1)} %get-tuple-element.82), channel_id=1, source_target_pairs={{0,1},{1,0},{2,3},{3,2},{4,5},{5,4},{6,7},{7,6},{8,9},{9,8},{10,11... | collective-permute-start | bytes 786440 | tf_op jit(solution)/shard_map/ppermute | solution.py:476
  25.2 4.1 %collective-permute-start.8 = (bf16[2,32,2048]{2,1,0:T(8,128)(2,1)S(1)}, bf16[2,32,2048]{2,1,0:T(8,128)(2,1)S(1)}, u32[]{:S(2)}, u32[]{:S(2)}) collective-permute-start(bf16[2,32,2048]{2,1,0:T(8,128)(2,1)S(1)} %get-tuple-element.83), channel_id=1, source_target_pairs={{0,1},{1,0},{2,3},{3,2},{4,5},{5,4},{6,7},{7,6},{8,9},{9,8},{10,11... | collective-permute-start | bytes 786440 | tf_op jit(solution)/shard_map/ppermute | solution.py:476
  25.7 3.7 %collective-permute-start.6 = (bf16[2,32,2048]{2,1,0:T(8,128)(2,1)S(1)}, bf16[2,32,2048]{2,1,0:T(8,128)(2,1)S(1)}, u32[]{:S(2)}, u32[]{:S(2)}) collective-permute-start(bf16[2,32,2048]{2,1,0:T(8,128)(2,1)S(1)} %get-tuple-element.77.refs_4_), channel_id=1, source_target_pairs={{0,1},{1,0},{2,3},{3,2},{4,5},{5,4},{6,7},{7,6},{8,9},{9,8},{10,11... | collective-permute-start | bytes 786440 | tf_op jit(solution)/shard_map/ppermute | solution.py:476
  31.2 2.1 %collective-permute-start.10 = (bf16[48,1024]{1,0:T(8,128)(2,1)S(1)}, bf16[48,1024]{1,0:T(8,128)(2,1)S(1)}, u32[]{:S(2)}, u32[]{:S(2)}) collective-permute-start(bf16[48,1024]{1,0:T(8,128)(2,1)S(1)} %get-tuple-element.85.refs_3_.refs_0_), channel_id=1, source_target_pairs={{0,1},{1,0},{2,3},{3,2},{4,5},{5,4},{6,7},{7,6},{8,9},{9,8},{10,11... | collective-permute-start | bytes 294920 | tf_op jit(solution)/shard_map/ppermute | solution.py:476
  31.7 1.6 %collective-permute-start.11 = (bf16[48,1024]{1,0:T(8,128)(2,1)S(1)}, bf16[48,1024]{1,0:T(8,128)(2,1)S(1)}, u32[]{:S(2)}, u32[]{:S(2)}) collective-permute-start(bf16[48,1024]{1,0:T(8,128)(2,1)S(1)} %get-tuple-element.86.refs_4_.refs_1_), channel_id=1, source_target_pairs={{0,1},{1,0},{2,3},{3,2},{4,5},{5,4},{6,7},{7,6},{8,9},{9,8},{10,11... | collective-permute-start | bytes 294920 | tf_op jit(solution)/shard_map/ppermute | solution.py:476
  31.7 10.0 %collective-permute-start.15 = (bf16[96,1024]{1,0:T(8,128)(2,1)S(1)}, bf16[96,1024]{1,0:T(8,128)(2,1)S(1)}, u32[]{:S(2)}, u32[]{:S(2)}) collective-permute-start(bf16[96,1024]{1,0:T(8,128)(2,1)S(1)} %get-tuple-element.87.refs_7_.refs_0_), channel_id=1, source_target_pairs={{0,2},{1,3},{2,0},{3,1},{4,6},{5,7},{6,4},{7,5},{8,10},{9,11},{10,... | collective-permute-start | bytes 589832 | tf_op jit(solution)/shard_map/ppermute | solution.py:480
  37.1 1.8 %collective-permute-start.13 = (bf16[48,1024]{1,0:T(8,128)(2,1)S(1)}, bf16[48,1024]{1,0:T(8,128)(2,1)S(1)}, u32[]{:S(2)}, u32[]{:S(2)}) collective-permute-start(bf16[48,1024]{1,0:T(8,128)(2,1)S(1)} %get-tuple-element.92.refs_4_.refs_2_), channel_id=1, source_target_pairs={{0,1},{1,0},{2,3},{3,2},{4,5},{5,4},{6,7},{7,6},{8,9},{9,8},{10,11... | collective-permute-start | bytes 294920 | tf_op jit(solution)/shard_map/ppermute | solution.py:476
  37.3 1.6 %collective-permute-start.14 = (bf16[48,1024]{1,0:T(8,128)(2,1)S(1)}, bf16[48,1024]{1,0:T(8,128)(2,1)S(1)}, u32[]{:S(2)}, u32[]{:S(2)}) collective-permute-start(bf16[48,1024]{1,0:T(8,128)(2,1)S(1)} %get-tuple-element.93.refs_5_.refs_3_), channel_id=1, source_target_pairs={{0,1},{1,0},{2,3},{3,2},{4,5},{5,4},{6,7},{7,6},{8,9},{9,8},{10,11... | collective-permute-start | bytes 294920 | tf_op jit(solution)/shard_map/ppermute | solution.py:476
  37.7 7.0 %collective-permute-start.12 = (bf16[96,1024]{1,0:T(8,128)(2,1)S(1)}, bf16[96,1024]{1,0:T(8,128)(2,1)S(1)}, u32[]{:S(2)}, u32[]{:S(2)}) collective-permute-start(bf16[96,1024]{1,0:T(8,128)(2,1)S(1)} %get-tuple-element.89.refs_9_.refs_0_), channel_id=1, source_target_pairs={{0,2},{1,3},{2,0},{3,1},{4,6},{5,7},{6,4},{7,5},{8,10},{9,11},{10,... | collective-permute-start | bytes 589832 | tf_op jit(solution)/shard_map/ppermute | solution.py:480
  44.7 2.3 %collective-permute-start.18 = (bf16[96,1024]{1,0:T(8,128)(2,1)S(1)}, bf16[96,1024]{1,0:T(8,128)(2,1)S(1)}, u32[]{:S(2)}, u32[]{:S(2)}) collective-permute-start(bf16[96,1024]{1,0:T(8,128)(2,1)S(1)} %shard_map.119.refs_2_.refs_4_), channel_id=1, source_target_pairs={{0,1},{1,0},{2,3},{3,2},{4,5},{5,4},{6,7},{7,6},{8,9},{9,8},{10,11... | collective-permute-start | bytes 589832 | tf_op jit(solution)/shard_map/ppermute | solution.py:476
  47.5 6.8 %collective-permute-start.19 = (bf16[24,1024]{1,0:T(8,128)(2,1)S(1)}, bf16[24,1024]{1,0:T(8,128)(2,1)S(1)}, u32[]{:S(2)}, u32[]{:S(2)}) collective-permute-start(bf16[24,1024]{1,0:T(8,128)(2,1)S(1)} %get-tuple-element.102), channel_id=1, source_target_pairs={{0,4},{4,0},{8,12},{12,8},{1,5},{5,1},{9,13},{13,9},{2,6},{6,2},{1... | collective-permute-start | bytes 147464 | tf_op jit(solution)/shard_map/ppermute | solution.py:473
  47.6 6.8 %collective-permute-start.20 = (bf16[24,1024]{1,0:T(8,128)(2,1)S(1)}, bf16[24,1024]{1,0:T(8,128)(2,1)S(1)}, u32[]{:S(2)}, u32[]{:S(2)}) collective-permute-start(bf16[24,1024]{1,0:T(8,128)(2,1)S(1)} %get-tuple-element.103), channel_id=1, source_target_pairs={{0,8},{4,12},{8,0},{12,4},{1,9},{5,13},{9,1},{13,5},{2,10},{6,14},... | collective-permute-start | bytes 147464 | tf_op jit(solution)/shard_map/ppermute | solution.py:473
  50.7 5.9 %collective-permute-start.21 = (bf16[24,1024]{1,0:T(8,128)(2,1)S(1)}, bf16[24,1024]{1,0:T(8,128)(2,1)S(1)}, u32[]{:S(2)}, u32[]{:S(2)}) collective-permute-start(bf16[24,1024]{1,0:T(8,128)(2,1)S(1)} %get-tuple-element.104), channel_id=1, source_target_pairs={{0,12},{4,8},{8,4},{12,0},{1,13},{5,9},{9,5},{13,1},{2,14},{6,10},... | collective-permute-start | bytes 147464 | tf_op jit(solution)/shard_map/ppermute | solution.py:473
  56.7 6.6 %collective-permute-start.24 = (bf16[24,1024]{1,0:T(8,128)(2,1)S(1)}, bf16[24,1024]{1,0:T(8,128)(2,1)S(1)}, u32[]{:S(2)}, u32[]{:S(2)}) collective-permute-start(bf16[24,1024]{1,0:T(8,128)(2,1)S(1)} %shard_map.123.refs_2_.refs_0_), channel_id=1, source_target_pairs={{0,12},{4,8},{8,4},{12,0},{1,13},{5,9},{9,5},{13,1},{2,14},{6,10},... | collective-permute-start | bytes 147464 | tf_op jit(solution)/shard_map/ppermute | solution.py:470
  58.0 5.7 %collective-permute-start.23 = (bf16[24,1024]{1,0:T(8,128)(2,1)S(1)}, bf16[24,1024]{1,0:T(8,128)(2,1)S(1)}, u32[]{:S(2)}, u32[]{:S(2)}) collective-permute-start(bf16[24,1024]{1,0:T(8,128)(2,1)S(1)} %shard_map.123.refs_2_.refs_0_), channel_id=1, source_target_pairs={{0,8},{4,12},{8,0},{12,4},{1,9},{5,13},{9,1},{13,5},{2,10},{6,14},... | collective-permute-start | bytes 147464 | tf_op jit(solution)/shard_map/ppermute | solution.py:470
  58.0 5.7 %collective-permute-start.22 = (bf16[24,1024]{1,0:T(8,128)(2,1)S(1)}, bf16[24,1024]{1,0:T(8,128)(2,1)S(1)}, u32[]{:S(2)}, u32[]{:S(2)}) collective-permute-start(bf16[24,1024]{1,0:T(8,128)(2,1)S(1)} %shard_map.123.refs_2_.refs_0_), channel_id=1, source_target_pairs={{0,4},{4,0},{8,12},{12,8},{1,5},{5,1},{9,13},{13,9},{2,6},{6,2},{1... | collective-permute-start | bytes 147464 | tf_op jit(solution)/shard_map/ppermute | solution.py:470
  65.3 2.7 %collective-permute-start.25 = (bf16[96,1024]{1,0:T(8,128)(2,1)S(1)}, bf16[96,1024]{1,0:T(8,128)(2,1)S(1)}, u32[]{:S(2)}, u32[]{:S(2)}) collective-permute-start(bf16[96,1024]{1,0:T(8,128)(2,1)S(1)} %shard_map.127.refs_3_), channel_id=1, source_target_pairs={{0,1},{1,0},{2,3},{3,2},{4,5},{5,4},{6,7},{7,6},{8,9},{9,8},{10,11... | collective-permute-start | bytes 589832 | tf_op jit(solution)/shard_map/ppermute | solution.py:476
  66.8 7.8 %collective-permute-start.28 = (bf16[96,1024]{1,0:T(8,128)(2,1)S(1)}, bf16[96,1024]{1,0:T(8,128)(2,1)S(1)}, u32[]{:S(2)}, u32[]{:S(2)}) collective-permute-start(bf16[96,1024]{1,0:T(8,128)(2,1)S(1)} %shard_map.128.refs_3_.refs_0_), channel_id=1, source_target_pairs={{0,2},{1,3},{2,0},{3,1},{4,6},{5,7},{6,4},{7,5},{8,10},{9,11},{10,... | collective-permute-start | bytes 589832 | tf_op jit(solution)/shard_map/ppermute | solution.py:480
  69.0 9.0 %collective-permute-start.27 = (bf16[96,1024]{1,0:T(8,128)(2,1)S(1)}, bf16[96,1024]{1,0:T(8,128)(2,1)S(1)}, u32[]{:S(2)}, u32[]{:S(2)}) collective-permute-start(bf16[96,1024]{1,0:T(8,128)(2,1)S(1)} %shard_map.129.refs_9_.refs_0_), channel_id=1, source_target_pairs={{0,2},{1,3},{2,0},{3,1},{4,6},{5,7},{6,4},{7,5},{8,10},{9,11},{10,... | collective-permute-start | bytes 589832 | tf_op jit(solution)/shard_map/ppermute | solution.py:480
  74.7 4.0 %collective-permute-start.32 = (bf16[2,32,1024]{2,1,0:T(8,128)(2,1)S(1)}, bf16[2,32,1024]{2,1,0:T(8,128)(2,1)S(1)}, u32[]{:S(2)}, u32[]{:S(2)}) collective-permute-start(bf16[2,32,1024]{2,1,0:T(8,128)(2,1)S(1)} %get-tuple-element.116.refs_1_.refs_4_), channel_id=1, source_target_pairs={{0,1},{1,0},{2,3},{3,2},{4,5},{5,4},{6,7},{7,6},{8,9},{9,8},{10,11... | collective-permute-start | bytes 393224 | tf_op jit(solution)/shard_map/ppermute | solution.py:476
  74.8 4.1 %collective-permute-start.33 = (bf16[2,32,1024]{2,1,0:T(8,128)(2,1)S(1)}, bf16[2,32,1024]{2,1,0:T(8,128)(2,1)S(1)}, u32[]{:S(2)}, u32[]{:S(2)}) collective-permute-start(bf16[2,32,1024]{2,1,0:T(8,128)(2,1)S(1)} %get-tuple-element.117.refs_2_), channel_id=1, source_target_pairs={{0,1},{1,0},{2,3},{3,2},{4,5},{5,4},{6,7},{7,6},{8,9},{9,8},{10,11... | collective-permute-start | bytes 393224 | tf_op jit(solution)/shard_map/ppermute | solution.py:476
  75.3 3.6 %collective-permute-start.34 = (bf16[2,32,1024]{2,1,0:T(8,128)(2,1)S(1)}, bf16[2,32,1024]{2,1,0:T(8,128)(2,1)S(1)}, u32[]{:S(2)}, u32[]{:S(2)}) collective-permute-start(bf16[2,32,1024]{2,1,0:T(8,128)(2,1)S(1)} %get-tuple-element.118.refs_3_), channel_id=1, source_target_pairs={{0,1},{1,0},{2,3},{3,2},{4,5},{5,4},{6,7},{7,6},{8,9},{9,8},{10,11... | collective-permute-start | bytes 393224 | tf_op jit(solution)/shard_map/ppermute | solution.py:476
  78.1 4.5 %collective-permute-start.29 = (bf16[2,32,1024]{2,1,0:T(8,128)(2,1)S(1)}, bf16[2,32,1024]{2,1,0:T(8,128)(2,1)S(1)}, u32[]{:S(2)}, u32[]{:S(2)}) collective-permute-start(bf16[2,32,1024]{2,1,0:T(8,128)(2,1)S(1)} %get-tuple-element.120.refs_4_.refs_7_), channel_id=1, source_target_pairs={{0,1},{1,0},{2,3},{3,2},{4,5},{5,4},{6,7},{7,6},{8,9},{9,8},{10,11... | collective-permute-start | bytes 393224 | tf_op jit(solution)/shard_map/ppermute | solution.py:476
  78.3 4.3 %collective-permute-start.30 = (bf16[2,32,1024]{2,1,0:T(8,128)(2,1)S(1)}, bf16[2,32,1024]{2,1,0:T(8,128)(2,1)S(1)}, u32[]{:S(2)}, u32[]{:S(2)}) collective-permute-start(bf16[2,32,1024]{2,1,0:T(8,128)(2,1)S(1)} %get-tuple-element.121.refs_5_), channel_id=1, source_target_pairs={{0,1},{1,0},{2,3},{3,2},{4,5},{5,4},{6,7},{7,6},{8,9},{9,8},{10,11... | collective-permute-start | bytes 393224 | tf_op jit(solution)/shard_map/ppermute | solution.py:476
  78.7 4.0 %collective-permute-start.31 = (bf16[2,32,1024]{2,1,0:T(8,128)(2,1)S(1)}, bf16[2,32,1024]{2,1,0:T(8,128)(2,1)S(1)}, u32[]{:S(2)}, u32[]{:S(2)}) collective-permute-start(bf16[2,32,1024]{2,1,0:T(8,128)(2,1)S(1)} %get-tuple-element.122.refs_6_), channel_id=1, source_target_pairs={{0,1},{1,0},{2,3},{3,2},{4,5},{5,4},{6,7},{7,6},{8,9},{9,8},{10,11... | collective-permute-start | bytes 393224 | tf_op jit(solution)/shard_map/ppermute | solution.py:476
  (5 other events, 61.7 us)

commit v6 on v5

--- a/solution.py
+++ b/solution.py
@@ -105,7 +105,7 @@
 
 
 def bring(order, wanted):
-    parts = 4
+    parts = 1
     shapes = []
     for weight, dim, _, _ in wanted:
         shape = list(weight.shape)
@@ -157,7 +157,7 @@
     chunk = weights[0].shape[1] // 2 // CHUNKS if chunks else weights[0][0].shape[1]
     high = tokens // pieces
     given = kinds if chunks else kinds * count
-    parts = 2
+    parts = 4
     deep = depth // parts
 
     def body(core_ref, x_ref, *refs):
@@ -241,6 +241,13 @@
         put(refs[len(others) :], total)
 
     return call(body, order, [own, *others], pieces_of(*own.shape, pieces))
+
+
+def settle(order, kept, arrived):
+    def body(core_ref, kept_ref, arrived_ref, out):
+        out[...] = (kept_ref[...] + arrived_ref[...].astype(F32)).astype(BF16)
+
+    return call(body, order, [kept, arrived], shape_of(kept.shape, BF16))
 
 
 def contract(order, terms, weight, carried, groups=0, brought=(), ahead=()):
@@ -318,20 +325,20 @@
     return call(body, order, [own, *others, curvature], shape_of(own.shape, BF16))
 
 
-def pull_back(order, weighted, weight, added):
+def pull_back(order, weighted, weight, added, dtype=BF16):
     def body(core_ref, x_ref, w_ref, *refs):
         total = lax.dot_general(
             x_ref[...], w_ref[...], COLUMNS_BY_COLUMNS, preferred_element_type=F32
         )
         if added is not None:
             total += refs[0][...].astype(F32)
-        refs[-1][...] = total.astype(BF16)
+        refs[-1][...] = total.astype(dtype)
 
     return call(
         body,
         order,
         [weighted, weight] + ([added] if added is not None else []),
-        shape_of((weighted.shape[0], weight.shape[0]), BF16),
+        shape_of((weighted.shape[0], weight.shape[0]), dtype),
     )
 
 
@@ -498,7 +505,12 @@
         if n < 2 * CHUNKS:
             sent.append(to_core(project(order, rows, weights, [], BF16)[0]))
         else:
-            sums.append(project(order, rows, weights, [sent[len(sums)]], BF16)[0])
+            i = len(sums)
+            if i == 0:
+                (kept,) = project(order, rows, weights, [], F32)
+                sums.append(settle(order, kept, sent[i]))
+            else:
+                sums.append(project(order, rows, weights, [sent[i]], BF16)[0])
     others = [over_chips(s) for s in sums]
     sent = project(order, rows, probe, [], BF16, 3, 1, tuple(each))
     sent = [to_core(piece) for piece in sent]
@@ -542,7 +554,9 @@
     )
 
     sent = [to_core(pull_back(order, weighted, held[i], None)) for i in each]
-    sums = [pull_back(order, weighted, held[CHUNKS + i], sent[i]) for i in each]
+    kept = pull_back(order, weighted, held[CHUNKS], None, F32)
+    sums = [settle(order, kept, sent[0])]
+    sums += [pull_back(order, weighted, held[CHUNKS + i], sent[i]) for i in each[1:]]
     others = [over_chips(s) for s in sums]
     (fisher_down,) = outer_down(
         order, [a[3] for a in acted] + [a[4] for a in acted], weighted, ()

time: 85.4 us -> 85 us (level)
    pallas_call x33 -> x35, Pallas kernels: 50.2 us -> 50.3 us  [call(): pl.pallas_call(kernel, in_specs=[SMEM] + [HBM if isinstance(o, InHbm) els...]
  transfers between devices with their start and end apart: 35 -> 35, of which waited for: 10 -> 8; matrix products, arithmetic and copies ran while one was open for 0% -> 0% of each run, Pallas kernels for 54% -> 54%
where the time goes in v6:
time: 85 us; the launch traced here: 84.9 us
  Pallas kernels  50.3 us (59%)
  starting transfers between devices  26.8 us (32%)
  waiting for transfers between devices  6.43 us (8%)
  between operations  1.2 us (1%)
    pallas_call x35, Pallas kernels, call(): pl.pallas_call(kernel, in_specs=[SMEM] + [HBM if isinstance(o, InHbm) els...  50.3 us
    ppermute x6, starting transfers between devices, over_dp(): lax.ppermute(value, 'dp', [(i, partner(i, step, groups)) for i in range(g...  10.1 us
    ppermute x6, starting transfers between devices, over_chips(): lax.ppermute(value, 'mp', [(2 * i + c, 2 * partner(i, k, chips) + c) for...  7.01 us
    ppermute x20, starting transfers between devices, to_core(): return lax.ppermute(value, 'mp', [(i, i ^ 1) for i in range(2 * chips)])  5.24 us
    ppermute x3, starting transfers between devices, back_over_dp(): lax.ppermute(value, 'dp', [(i, giver(i, step, groups)) for i in range(gro...  4.44 us
    ppermute x3, waiting for transfers between devices, back_over_dp(): lax.ppermute(value, 'dp', [(i, giver(i, step, groups)) for i in range(gro...  2.18 us
  transfers between devices with their start and end apart: 35, of which 8 were waited for; matrix products, arithmetic and copies ran while one was open for 0% of the time, Pallas kernels for 54%

profile of v6, /device:TPU:0, one launch (start us, length us, event | category | flops | bytes accessed | tf_op | source)
XLA Modules:
  0.0 84.9 jit_solution(640275376882946562)
XLA Ops:
  0.6 4.1 %collective-permute-start.1 = (bf16[24,1024]{1,0:T(8,128)(2,1)}, bf16[24,1024]{1,0:T(8,128)(2,1)S(1)}, u32[]{:S(2)}, u32[]{:S(2)}) collective-permute-start(bf16[24,1024]{1,0:T(8,128)(2,1)} %refs_0_.9), channel_id=1, source_target_pairs={{0,8},{4,12},{8,0},{12,4},{1,9},{5,13},{9,1},{13,5},{2,10},{6,14},... | collective-permute-start | bytes 147464 | tf_op jit(solution)/shard_map/ppermute | solution.py:477
  4.7 1.6 %collective-permute-start = (bf16[24,1024]{1,0:T(8,128)(2,1)}, bf16[24,1024]{1,0:T(8,128)(2,1)S(1)}, u32[]{:S(2)}, u32[]{:S(2)}) collective-permute-start(bf16[24,1024]{1,0:T(8,128)(2,1)} %refs_0_.9), channel_id=1, source_target_pairs={{0,4},{4,0},{8,12},{12,8},{1,5},{5,1},{9,13},{13,9},{2,6},{6,2},{1... | collective-permute-start | bytes 147464 | tf_op jit(solution)/shard_map/ppermute | solution.py:477
  6.3 4.8 %shard_map.103 = (f32[8,128]{1,0:T(8,128)S(1)}, bf16[1024,1024]{1,0:T(8,128)(2,1)S(1)}, bf16[1024,1024]{1,0:T(8,128)(2,1)S(1)}, bf16[1024,1024]{1,0:T(8,128)(2,1...) custom-call(s32[1]{0:T(128)} %bitcast.core_ref, ...), custom_call_target="tpu_custom_call" | custom-call | flops 1 | bytes 1 | tf_op jit(solution)/shard_map/pallas_call | solution.py:64
  11.1 1.3 %collective-permute-done.2.refs_3_ = bf16[24,1024]{1,0:T(8,128)(2,1)S(1)} collective-permute-done((bf16[24,1024]{1,0:T(8,128)(2,1)}, bf16[24,1024]{1,0:T(8,128)(2,1)S(1)}, u32[]{:S(2)}, u32[]{:S(2)}) %collective-permute-start.2) | collective-permute-done | bytes 49184 | tf_op jit(solution)/shard_map/ppermute | solution.py:477
  12.4 0.8 shard_map.105.refs_3_
  14.7 0.8 shard_map.107.refs_0_.refs_2_
  15.6 1.6 %collective-permute-start.9 = (bf16[2,96,1024]{2,1,0:T(8,128)(2,1)S(1)}, bf16[2,96,1024]{2,1,0:T(8,128)(2,1)S(1)}, u32[]{:S(2)}, u32[]{:S(2)}) collective-permute-start(bf16[2,96,1024]{2,1,0:T(8,128)(2,1)S(1)} %shard_map.108.refs_2_.refs_0_), channel_id=1, source_target_pairs={{0,2},{1,3},{2,0},{3,1},{4,6},{5,7},{6,4},{7,5},{8,10},{9,11},{10,... | collective-permute-start | bytes 1179656 | tf_op jit(solution)/shard_map/ppermute | solution.py:487
  17.1 2.2 %shard_map.109 = (f32[8,128]{1,0:T(8,128)S(1)}, bf16[1024,1024]{1,0:T(8,128)(2,1)S(1)}, bf16[1024,1024]{1,0:T(8,128)(2,1)S(1)}) custom-call(s32[1]{0:T(128)} %bitcast.core_ref, bf16[1024,4096]{1,0:T(8,128)(2,1)} %refs_0_.10, bf16[1024,4096]{1,0:T(8,128)(2,1)} %refs_1_.9, bf16[2,96,1024]{2,1,0:T(8,128)(2,1)S(1)} %shard_map.108.refs_2_.refs_0_), custom_call_target="tpu_custom_call" | custom-call | flops 1 | bytes 1 | tf_op jit(solution)/shard_map/pallas_call | solution.py:64
  19.4 0.8 shard_map.110.refs_3_.refs_0_
  20.8 4.0 %shard_map.111 = (bf16[2,32,2048]{2,1,0:T(8,128)(2,1)S(1)}, bf16[2,32,2048]{2,1,0:T(8,128)(2,1)S(1)}, bf16[2,32,2048]{2,1,0:T(8,128)(2,1)S(1)}) custom-call(s32[1]{0:T(128)} %bitcast.core_ref, bf16[96,1024]{1,0:T(8,128)(2,1)S(1)} %shard_map.104.refs_0_.refs_3_, bf16[1024,4096]{1,0:T(8,128)(2,1)} %refs_1_.11, bf16[1024,4096]{1,0:T(8,128)(2,1)} %refs_3_.4, ...), custom_call_target="tpu_custom_call" | custom-call | flops 1 | bytes 1 | tf_op jit(solution)/shard_map/pallas_call | solution.py:64
  25.5 3.5 %shard_map.112 = (f32[8,128]{1,0:T(8,128)S(1)}, bf16[1024,1024]{1,0:T(8,128)(2,1)S(1)}, bf16[1024,1024]{1,0:T(8,128)(2,1)S(1)}, bf16[1024,1024]{1,0:T(8,128)(2,1)S(1)}, bf16[1024,1024]{1,0:T(8,128)(2,1)S(1)}) custom-call(s32[1]{0:T(128)} %bitcast.core_ref, bf16[1024,4096]{1,0:T(8,128)(2,1)} %refs_1_.11, bf16[1024,4096]{1,0:T(8,128)(2,1)} %refs_1_.11, ...), custom_call_target="tpu_custom_call" | custom-call | flops 1 | bytes 1 | tf_op jit(solution)/shard_map/pallas_call | solution.py:64
  29.1 1.5 %shard_map.113.refs_2_.refs_3_ = f32[2,96,2048]{2,1,0:T(8,128)S(1)} custom-call(s32[1]{0:T(128)} %bitcast.core_ref, bf16[96,1024]{1,0:T(8,128)(2,1)S(1)} %shard_map.104.refs_0_.refs_3_, bf16[1024,1024]{1,0:T(8,128)(2,1)S(1)} %get-tuple-element.78.refs_1_, bf16[1024,1024]{1,0:T(8,128)(2,1)S(1)} %get-tuple-element.79.refs_2_, ...), custom_call_target="tpu_custom_call" | custom-call | flops 1 | bytes 1 | tf_op jit(solution)/shard_map/pallas_call | solution.py:64
  31.5 1.5 %collective-permute-start.15 = (bf16[96,1024]{1,0:T(8,128)(2,1)S(1)}, bf16[96,1024]{1,0:T(8,128)(2,1)S(1)}, u32[]{:S(2)}, u32[]{:S(2)}) collective-permute-start(bf16[96,1024]{1,0:T(8,128)(2,1)S(1)} %get-tuple-element.87.refs_7_.refs_0_), channel_id=1, source_target_pairs={{0,2},{1,3},{2,0},{3,1},{4,6},{5,7},{6,4},{7,5},{8,10},{9,11},{10,... | collective-permute-start | bytes 589832 | tf_op jit(solution)/shard_map/ppermute | solution.py:487
  33.0 3.5 %shard_map.115 = (f32[96,1024]{1,0:T(8,128)S(1)}, bf16[1024,1024]{1,0:T(8,128)(2,1)S(1)}, bf16[1024,1024]{1,0:T(8,128)(2,1)S(1)}) custom-call(s32[1]{0:T(128)} %bitcast.core_ref, bf16[4096,1024]{1,0:T(8,128)(2,1)} %refs_2_.8, bf16[4096,1024]{1,0:T(8,128)(2,1)} %refs_2_.8, bf16[4096,1024]{1,0:T(8,128)(2,1)} %refs_2_.8, ...), custom_call_target="tpu_custom_call" | custom-call | flops 1 | bytes 1 | tf_op jit(solution)/shard_map/pallas_call | solution.py:64
  37.4 1.2 %collective-permute-start.12 = (bf16[96,1024]{1,0:T(8,128)(2,1)S(1)}, bf16[96,1024]{1,0:T(8,128)(2,1)S(1)}, u32[]{:S(2)}, u32[]{:S(2)}) collective-permute-start(bf16[96,1024]{1,0:T(8,128)(2,1)S(1)} %get-tuple-element.89.refs_9_.refs_0_), channel_id=1, source_target_pairs={{0,2},{1,3},{2,0},{3,1},{4,6},{5,7},{6,4},{7,5},{8,10},{9,11},{10,... | collective-permute-start | bytes 589832 | tf_op jit(solution)/shard_map/ppermute | solution.py:487
  38.7 2.9 %shard_map.117 = (f32[96,1024]{1,0:T(8,128)S(1)}, bf16[1024,1024]{1,0:T(8,128)(2,1)S(1)}, bf16[1024,1024]{1,0:T(8,128)(2,1)S(1)}) custom-call(s32[1]{0:T(128)} %bitcast.core_ref, bf16[1024,1024]{1,0:T(8,128)(2,1)S(1)} %get-tuple-element.90.refs_0_, bf16[1024,1024]{1,0:T(8,128)(2,1)S(1)} %get-tuple-element.91.refs_1_, bf16[4096,1024]{1,0:T(8,128)(2,1)} %refs_1_.15, ...), custom_call_target="tpu_custom_call" | custom-call | flops 1 | bytes 1 | tf_op jit(solution)/shard_map/pallas_call | solution.py:64
  44.5 2.2 %shard_map.121 = (f32[96,1024]{1,0:T(8,128)S(1)}, bf16[1024,1024]{1,0:T(8,128)(2,1)S(1)}) custom-call(s32[1]{0:T(128)} %bitcast.core_ref, bf16[4096,1024]{1,0:T(8,128)(2,1)} %refs_1_.15, bf16[4096,1024]{1,0:T(8,128)(2,1)} %refs_1_.15, bf16[96,1024]{1,0:T(8,128)(2,1)S(1)} %shard_map.120.refs_2_.refs_4_, f32[96,1024]{1,0:T(8,128)S(1)} %shard_map.119.refs_2_.refs_3_, ...), custom_call_target="tpu_custom_call" | custom-call | flops 1 | bytes 1 | tf_op jit(solution)/shard_map/pallas_call | solution.py:64
  47.3 3.1 %collective-permute-start.20 = (bf16[24,1024]{1,0:T(8,128)(2,1)S(1)}, bf16[24,1024]{1,0:T(8,128)(2,1)S(1)}, u32[]{:S(2)}, u32[]{:S(2)}) collective-permute-start(bf16[24,1024]{1,0:T(8,128)(2,1)S(1)} %get-tuple-element.103), channel_id=1, source_target_pairs={{0,8},{4,12},{8,0},{12,4},{1,9},{5,13},{9,1},{13,5},{2,10},{6,14},... | collective-permute-start | bytes 147464 | tf_op jit(solution)/shard_map/ppermute | solution.py:480
  50.4 1.3 %collective-permute-start.21 = (bf16[24,1024]{1,0:T(8,128)(2,1)S(1)}, bf16[24,1024]{1,0:T(8,128)(2,1)S(1)}, u32[]{:S(2)}, u32[]{:S(2)}) collective-permute-start(bf16[24,1024]{1,0:T(8,128)(2,1)S(1)} %get-tuple-element.104), channel_id=1, source_target_pairs={{0,12},{4,8},{8,4},{12,0},{1,13},{5,9},{9,5},{13,1},{2,14},{6,10},... | collective-permute-start | bytes 147464 | tf_op jit(solution)/shard_map/ppermute | solution.py:480
  51.9 2.2 %shard_map.123 = (f32[8,128]{1,0:T(8,128)S(1)}, bf16[1024,1024]{1,0:T(8,128)(2,1)S(1)}, bf16[1024,1024]{1,0:T(8,128)(2,1)S(1)}) custom-call(s32[1]{0:T(128)} %bitcast.core_ref, bf16[4096,1024]{1,0:T(8,128)(2,1)} %refs_1_.15, bf16[4096,1024]{1,0:T(8,128)(2,1)} %refs_1_.15, f32[24,1024]{1,0:T(8,128)S(1)} %get-tuple-element.101.refs_2_.refs_0_), custom_call_target="tpu_custom_call" | custom-call | flops 1 | bytes 1 | tf_op jit(solution)/shard_map/pallas_call | solution.py:64
  54.2 2.2 %collective-permute-done.21.refs_3_ = bf16[24,1024]{1,0:T(8,128)(2,1)S(1)} collective-permute-done((bf16[24,1024]{1,0:T(8,128)(2,1)S(1)}, bf16[24,1024]{1,0:T(8,128)(2,1)S(1)}, u32[]{:S(2)}, u32[]{:S(2)}) %collective-permute-start.21) | collective-permute-done | bytes 49184 | tf_op jit(solution)/shard_map/ppermute | solution.py:480
  56.4 1.4 %collective-permute-start.24 = (bf16[24,1024]{1,0:T(8,128)(2,1)S(1)}, bf16[24,1024]{1,0:T(8,128)(2,1)S(1)}, u32[]{:S(2)}, u32[]{:S(2)}) collective-permute-start(bf16[24,1024]{1,0:T(8,128)(2,1)S(1)} %shard_map.124.refs_2_.refs_0_), channel_id=1, source_target_pairs={{0,12},{4,8},{8,4},{12,0},{1,13},{5,9},{9,5},{13,1},{2,14},{6,10},... | collective-permute-start | bytes 147464 | tf_op jit(solution)/shard_map/ppermute | solution.py:477
  57.8 3.0 %collective-permute-start.22 = (bf16[24,1024]{1,0:T(8,128)(2,1)S(1)}, bf16[24,1024]{1,0:T(8,128)(2,1)S(1)}, u32[]{:S(2)}, u32[]{:S(2)}) collective-permute-start(bf16[24,1024]{1,0:T(8,128)(2,1)S(1)} %shard_map.124.refs_2_.refs_0_), channel_id=1, source_target_pairs={{0,4},{4,0},{8,12},{12,8},{1,5},{5,1},{9,13},{13,9},{2,6},{6,2},{1... | collective-permute-start | bytes 147464 | tf_op jit(solution)/shard_map/ppermute | solution.py:477
  60.8 2.2 %shard_map.125 = (f32[8,128]{1,0:T(8,128)S(1)}, bf16[1024,1024]{1,0:T(8,128)(2,1)S(1)}, bf16[1024,1024]{1,0:T(8,128)(2,1)S(1)}) custom-call(s32[1]{0:T(128)} %bitcast.core_ref, bf16[4096,1024]{1,0:T(8,128)(2,1)} %refs_1_.15, bf16[4096,1024]{1,0:T(8,128)(2,1)} %refs_1_.15, bf16[24,1024]{1,0:T(8,128)(2,1)S(1)} %shard_map.124.refs_2_.refs_0_), custom_call_target="tpu_custom_call" | custom-call | flops 1 | bytes 1 | tf_op jit(solution)/shard_map/pallas_call | solution.py:64
  66.4 1.3 %collective-permute-start.28 = (bf16[96,1024]{1,0:T(8,128)(2,1)S(1)}, bf16[96,1024]{1,0:T(8,128)(2,1)S(1)}, u32[]{:S(2)}, u32[]{:S(2)}) collective-permute-start(bf16[96,1024]{1,0:T(8,128)(2,1)S(1)} %shard_map.130.refs_3_.refs_0_), channel_id=1, source_target_pairs={{0,2},{1,3},{2,0},{3,1},{4,6},{5,7},{6,4},{7,5},{8,10},{9,11},{10,... | collective-permute-start | bytes 589832 | tf_op jit(solution)/shard_map/ppermute | solution.py:487
  67.7 0.9 %shard_map.131.refs_9_.refs_0_ = bf16[96,1024]{1,0:T(8,128)(2,1)S(1)} custom-call(s32[1]{0:T(128)} %bitcast.core_ref, bf16[96,1024]{1,0:T(8,128)(2,1)S(1)} %shard_map.126.refs_0_.refs_2_.refs_8_, bf16[1024,1024]{1,0:T(8,128)(2,1)S(1)} %get-tuple-element.107.refs_1_, bf16[96,1024]{1,0:T(8,128)(2,1)S(1)} %collective-permute-done.25.refs_2_, ...), custom_call_target="tpu_custom_call" | custom-call | flops 1 | bytes 1 | tf_op jit(solution)/shard_map/pallas_call | solution.py:64
  68.7 0.9 %collective-permute-start.27 = (bf16[96,1024]{1,0:T(8,128)(2,1)S(1)}, bf16[96,1024]{1,0:T(8,128)(2,1)S(1)}, u32[]{:S(2)}, u32[]{:S(2)}) collective-permute-start(bf16[96,1024]{1,0:T(8,128)(2,1)S(1)} %shard_map.131.refs_9_.refs_0_), channel_id=1, source_target_pairs={{0,2},{1,3},{2,0},{3,1},{4,6},{5,7},{6,4},{7,5},{8,10},{9,11},{10,... | collective-permute-start | bytes 589832 | tf_op jit(solution)/shard_map/ppermute | solution.py:487
  69.5 3.7 %shard_map.132 = (f32[8,128]{1,0:T(8,128)S(1)}, bf16[4096,1024]{1,0:T(8,128)(2,1)}) custom-call(s32[1]{0:T(128)} %bitcast.core_ref, bf16[48,1024]{1,0:T(8,128)(2,1)S(1)} %get-tuple-element.85.refs_3_.refs_0_, bf16[48,1024]{1,0:T(8,128)(2,1)S(1)} %get-tuple-element.86.refs_4_.refs_1_, bf16[48,1024]{1,0:T(8,128)(2,1)S(1)} %get-tuple-element.92.refs_4_.refs_2_, ...), custom_call_target="tpu_custom_call" | custom-call | flops 1 | bytes 1 | tf_op jit(solution)/shard_map/pallas_call | solution.py:64
  73.3 1.0 %collective-permute-done.28.refs_1_ = bf16[96,1024]{1,0:T(8,128)(2,1)S(1)} collective-permute-done((bf16[96,1024]{1,0:T(8,128)(2,1)S(1)}, bf16[96,1024]{1,0:T(8,128)(2,1)S(1)}, u32[]{:S(2)}, u32[]{:S(2)}) %collective-permute-start.28) | collective-permute-done | bytes 196640 | tf_op jit(solution)/shard_map/ppermute | solution.py:487
  75.0 2.4 %shard_map.134 = (f32[8,128]{1,0:T(8,128)S(1)}, bf16[1024,4096]{1,0:T(8,128)(2,1)}, bf16[1024,4096]{1,0:T(8,128)(2,1)}) custom-call(s32[1]{0:T(128)} %bitcast.core_ref, bf16[96,1024]{1,0:T(8,128)(2,1)S(1)} %shard_map.104.refs_0_.refs_3_, bf16[2,32,1024]{2,1,0:T(8,128)(2,1)S(1)} %get-tuple-element.116.refs_1_.refs_4_, ...), custom_call_target="tpu_custom_call" | custom-call | flops 1 | bytes 1 | tf_op jit(solution)/shard_map/pallas_call | solution.py:64
  78.5 3.7 %shard_map.136 = (f32[8,128]{1,0:T(8,128)S(1)}, bf16[1024,4096]{1,0:T(8,128)(2,1)}, bf16[1024,4096]{1,0:T(8,128)(2,1)}) custom-call(s32[1]{0:T(128)} %bitcast.core_ref, bf16[96,1024]{1,0:T(8,128)(2,1)S(1)} %shard_map.104.refs_0_.refs_3_, bf16[2,32,1024]{2,1,0:T(8,128)(2,1)S(1)} %collective-permute-done.32.refs_1_, ...), custom_call_target="tpu_custom_call", output_to_operand_aliasing={{1}: (9, {}), {2}: (10, {})} | custom-call | flops 1 | bytes 1 | tf_op jit(solution)/shard_map/pallas_call | solution.py:64
  82.3 2.4 %shard_map.137 = (bf16[1024,4096]{1,0:T(8,128)(2,1)}, bf16[1024,4096]{1,0:T(8,128)(2,1)}) custom-call(s32[1]{0:T(128)} %bitcast.core_ref, bf16[96,1024]{1,0:T(8,128)(2,1)S(1)} %shard_map.104.refs_0_.refs_3_, bf16[2,32,1024]{2,1,0:T(8,128)(2,1)S(1)} %collective-permute-done.29.refs_1_, ...), custom_call_target="tpu_custom_call", output_to_operand_aliasing={{0}: (6, {}), {1}: (7, {})} | custom-call | flops 1 | bytes 1 | tf_op jit(solution)/shard_map/pallas_call | solution.py:64
  (79 shorter events, 13.6 us)
Async XLA Ops:
  0.6 10.5 %collective-permute-start.1 = (bf16[24,1024]{1,0:T(8,128)(2,1)}, bf16[24,1024]{1,0:T(8,128)(2,1)S(1)}, u32[]{:S(2)}, u32[]{:S(2)}) collective-permute-start(bf16[24,1024]{1,0:T(8,128)(2,1)} %refs_0_.9), channel_id=1, source_target_pairs={{0,8},{4,12},{8,0},{12,4},{1,9},{5,13},{9,1},{13,5},{2,10},{6,14},... | collective-permute-start | bytes 147464 | tf_op jit(solution)/shard_map/ppermute | solution.py:477
  4.7 6.4 %collective-permute-start = (bf16[24,1024]{1,0:T(8,128)(2,1)}, bf16[24,1024]{1,0:T(8,128)(2,1)S(1)}, u32[]{:S(2)}, u32[]{:S(2)}) collective-permute-start(bf16[24,1024]{1,0:T(8,128)(2,1)} %refs_0_.9), channel_id=1, source_target_pairs={{0,4},{4,0},{8,12},{12,8},{1,5},{5,1},{9,13},{13,9},{2,6},{6,2},{1... | collective-permute-start | bytes 147464 | tf_op jit(solution)/shard_map/ppermute | solution.py:477
  6.3 6.1 %collective-permute-start.2 = (bf16[24,1024]{1,0:T(8,128)(2,1)}, bf16[24,1024]{1,0:T(8,128)(2,1)S(1)}, u32[]{:S(2)}, u32[]{:S(2)}) collective-permute-start(bf16[24,1024]{1,0:T(8,128)(2,1)} %refs_0_.9), channel_id=1, source_target_pairs={{0,12},{4,8},{8,4},{12,0},{1,13},{5,9},{9,5},{13,1},{2,14},{6,10},... | collective-permute-start | bytes 147464 | tf_op jit(solution)/shard_map/ppermute | solution.py:477
  13.3 2.3 %collective-permute-start.3 = (bf16[2,96,1024]{2,1,0:T(8,128)(2,1)S(1)}, bf16[2,96,1024]{2,1,0:T(8,128)(2,1)S(1)}, u32[]{:S(2)}, u32[]{:S(2)}) collective-permute-start(bf16[2,96,1024]{2,1,0:T(8,128)(2,1)S(1)} %shard_map.105.refs_3_), channel_id=1, source_target_pairs={{0,1},{1,0},{2,3},{3,2},{4,5},{5,4},{6,7},{7,6},{8,9},{9,8},{10,11... | collective-permute-start | bytes 1179656 | tf_op jit(solution)/shard_map/ppermute | solution.py:483
  14.1 5.3 %collective-permute-start.4 = (bf16[2,96,1024]{2,1,0:T(8,128)(2,1)S(1)}, bf16[2,96,1024]{2,1,0:T(8,128)(2,1)S(1)}, u32[]{:S(2)}, u32[]{:S(2)}) collective-permute-start(bf16[2,96,1024]{2,1,0:T(8,128)(2,1)S(1)} %shard_map.106.refs_3_), channel_id=1, source_target_pairs={{0,1},{1,0},{2,3},{3,2},{4,5},{5,4},{6,7},{7,6},{8,9},{9,8},{10,11... | collective-permute-start | bytes 1179656 | tf_op jit(solution)/shard_map/ppermute | solution.py:483
  15.6 15.0 %collective-permute-start.9 = (bf16[2,96,1024]{2,1,0:T(8,128)(2,1)S(1)}, bf16[2,96,1024]{2,1,0:T(8,128)(2,1)S(1)}, u32[]{:S(2)}, u32[]{:S(2)}) collective-permute-start(bf16[2,96,1024]{2,1,0:T(8,128)(2,1)S(1)} %shard_map.108.refs_2_.refs_0_), channel_id=1, source_target_pairs={{0,2},{1,3},{2,0},{3,1},{4,6},{5,7},{6,4},{7,5},{8,10},{9,11},{10,... | collective-permute-start | bytes 1179656 | tf_op jit(solution)/shard_map/ppermute | solution.py:487
  20.2 16.3 %collective-permute-start.5 = (bf16[2,96,1024]{2,1,0:T(8,128)(2,1)S(1)}, bf16[2,96,1024]{2,1,0:T(8,128)(2,1)S(1)}, u32[]{:S(2)}, u32[]{:S(2)}) collective-permute-start(bf16[2,96,1024]{2,1,0:T(8,128)(2,1)S(1)} %shard_map.110.refs_3_.refs_0_), channel_id=1, source_target_pairs={{0,2},{1,3},{2,0},{3,1},{4,6},{5,7},{6,4},{7,5},{8,10},{9,11},{10,... | collective-permute-start | bytes 1179656 | tf_op jit(solution)/shard_map/ppermute | solution.py:487
  24.9 4.2 %collective-permute-start.7 = (bf16[2,32,2048]{2,1,0:T(8,128)(2,1)S(1)}, bf16[2,32,2048]{2,1,0:T(8,128)(2,1)S(1)}, u32[]{:S(2)}, u32[]{:S(2)}) collective-permute-start(bf16[2,32,2048]{2,1,0:T(8,128)(2,1)S(1)} %get-tuple-element.82), channel_id=1, source_target_pairs={{0,1},{1,0},{2,3},{3,2},{4,5},{5,4},{6,7},{7,6},{8,9},{9,8},{10,11... | collective-permute-start | bytes 786440 | tf_op jit(solution)/shard_map/ppermute | solution.py:483
  25.0 4.1 %collective-permute-start.8 = (bf16[2,32,2048]{2,1,0:T(8,128)(2,1)S(1)}, bf16[2,32,2048]{2,1,0:T(8,128)(2,1)S(1)}, u32[]{:S(2)}, u32[]{:S(2)}) collective-permute-start(bf16[2,32,2048]{2,1,0:T(8,128)(2,1)S(1)} %get-tuple-element.83), channel_id=1, source_target_pairs={{0,1},{1,0},{2,3},{3,2},{4,5},{5,4},{6,7},{7,6},{8,9},{9,8},{10,11... | collective-permute-start | bytes 786440 | tf_op jit(solution)/shard_map/ppermute | solution.py:483
  25.4 3.6 %collective-permute-start.6 = (bf16[2,32,2048]{2,1,0:T(8,128)(2,1)S(1)}, bf16[2,32,2048]{2,1,0:T(8,128)(2,1)S(1)}, u32[]{:S(2)}, u32[]{:S(2)}) collective-permute-start(bf16[2,32,2048]{2,1,0:T(8,128)(2,1)S(1)} %get-tuple-element.77.refs_4_), channel_id=1, source_target_pairs={{0,1},{1,0},{2,3},{3,2},{4,5},{5,4},{6,7},{7,6},{8,9},{9,8},{10,11... | collective-permute-start | bytes 786440 | tf_op jit(solution)/shard_map/ppermute | solution.py:483
  30.9 2.1 %collective-permute-start.10 = (bf16[48,1024]{1,0:T(8,128)(2,1)S(1)}, bf16[48,1024]{1,0:T(8,128)(2,1)S(1)}, u32[]{:S(2)}, u32[]{:S(2)}) collective-permute-start(bf16[48,1024]{1,0:T(8,128)(2,1)S(1)} %get-tuple-element.85.refs_3_.refs_0_), channel_id=1, source_target_pairs={{0,1},{1,0},{2,3},{3,2},{4,5},{5,4},{6,7},{7,6},{8,9},{9,8},{10,11... | collective-permute-start | bytes 294920 | tf_op jit(solution)/shard_map/ppermute | solution.py:483
  31.5 10.0 %collective-permute-start.15 = (bf16[96,1024]{1,0:T(8,128)(2,1)S(1)}, bf16[96,1024]{1,0:T(8,128)(2,1)S(1)}, u32[]{:S(2)}, u32[]{:S(2)}) collective-permute-start(bf16[96,1024]{1,0:T(8,128)(2,1)S(1)} %get-tuple-element.87.refs_7_.refs_0_), channel_id=1, source_target_pairs={{0,2},{1,3},{2,0},{3,1},{4,6},{5,7},{6,4},{7,5},{8,10},{9,11},{10,... | collective-permute-start | bytes 589832 | tf_op jit(solution)/shard_map/ppermute | solution.py:487
  36.9 1.8 %collective-permute-start.13 = (bf16[48,1024]{1,0:T(8,128)(2,1)S(1)}, bf16[48,1024]{1,0:T(8,128)(2,1)S(1)}, u32[]{:S(2)}, u32[]{:S(2)}) collective-permute-start(bf16[48,1024]{1,0:T(8,128)(2,1)S(1)} %get-tuple-element.92.refs_4_.refs_2_), channel_id=1, source_target_pairs={{0,1},{1,0},{2,3},{3,2},{4,5},{5,4},{6,7},{7,6},{8,9},{9,8},{10,11... | collective-permute-start | bytes 294920 | tf_op jit(solution)/shard_map/ppermute | solution.py:483
  37.1 1.6 %collective-permute-start.14 = (bf16[48,1024]{1,0:T(8,128)(2,1)S(1)}, bf16[48,1024]{1,0:T(8,128)(2,1)S(1)}, u32[]{:S(2)}, u32[]{:S(2)}) collective-permute-start(bf16[48,1024]{1,0:T(8,128)(2,1)S(1)} %get-tuple-element.93.refs_5_.refs_3_), channel_id=1, source_target_pairs={{0,1},{1,0},{2,3},{3,2},{4,5},{5,4},{6,7},{7,6},{8,9},{9,8},{10,11... | collective-permute-start | bytes 294920 | tf_op jit(solution)/shard_map/ppermute | solution.py:483
  37.4 7.0 %collective-permute-start.12 = (bf16[96,1024]{1,0:T(8,128)(2,1)S(1)}, bf16[96,1024]{1,0:T(8,128)(2,1)S(1)}, u32[]{:S(2)}, u32[]{:S(2)}) collective-permute-start(bf16[96,1024]{1,0:T(8,128)(2,1)S(1)} %get-tuple-element.89.refs_9_.refs_0_), channel_id=1, source_target_pairs={{0,2},{1,3},{2,0},{3,1},{4,6},{5,7},{6,4},{7,5},{8,10},{9,11},{10,... | collective-permute-start | bytes 589832 | tf_op jit(solution)/shard_map/ppermute | solution.py:487
  44.5 2.3 %collective-permute-start.18 = (bf16[96,1024]{1,0:T(8,128)(2,1)S(1)}, bf16[96,1024]{1,0:T(8,128)(2,1)S(1)}, u32[]{:S(2)}, u32[]{:S(2)}) collective-permute-start(bf16[96,1024]{1,0:T(8,128)(2,1)S(1)} %shard_map.120.refs_2_.refs_4_), channel_id=1, source_target_pairs={{0,1},{1,0},{2,3},{3,2},{4,5},{5,4},{6,7},{7,6},{8,9},{9,8},{10,11... | collective-permute-start | bytes 589832 | tf_op jit(solution)/shard_map/ppermute | solution.py:483
  47.3 6.9 %collective-permute-start.19 = (bf16[24,1024]{1,0:T(8,128)(2,1)S(1)}, bf16[24,1024]{1,0:T(8,128)(2,1)S(1)}, u32[]{:S(2)}, u32[]{:S(2)}) collective-permute-start(bf16[24,1024]{1,0:T(8,128)(2,1)S(1)} %get-tuple-element.102), channel_id=1, source_target_pairs={{0,4},{4,0},{8,12},{12,8},{1,5},{5,1},{9,13},{13,9},{2,6},{6,2},{1... | collective-permute-start | bytes 147464 | tf_op jit(solution)/shard_map/ppermute | solution.py:480
  47.3 6.8 %collective-permute-start.20 = (bf16[24,1024]{1,0:T(8,128)(2,1)S(1)}, bf16[24,1024]{1,0:T(8,128)(2,1)S(1)}, u32[]{:S(2)}, u32[]{:S(2)}) collective-permute-start(bf16[24,1024]{1,0:T(8,128)(2,1)S(1)} %get-tuple-element.103), channel_id=1, source_target_pairs={{0,8},{4,12},{8,0},{12,4},{1,9},{5,13},{9,1},{13,5},{2,10},{6,14},... | collective-permute-start | bytes 147464 | tf_op jit(solution)/shard_map/ppermute | solution.py:480
  50.4 5.9 %collective-permute-start.21 = (bf16[24,1024]{1,0:T(8,128)(2,1)S(1)}, bf16[24,1024]{1,0:T(8,128)(2,1)S(1)}, u32[]{:S(2)}, u32[]{:S(2)}) collective-permute-start(bf16[24,1024]{1,0:T(8,128)(2,1)S(1)} %get-tuple-element.104), channel_id=1, source_target_pairs={{0,12},{4,8},{8,4},{12,0},{1,13},{5,9},{9,5},{13,1},{2,14},{6,10},... | collective-permute-start | bytes 147464 | tf_op jit(solution)/shard_map/ppermute | solution.py:480
  56.4 6.7 %collective-permute-start.24 = (bf16[24,1024]{1,0:T(8,128)(2,1)S(1)}, bf16[24,1024]{1,0:T(8,128)(2,1)S(1)}, u32[]{:S(2)}, u32[]{:S(2)}) collective-permute-start(bf16[24,1024]{1,0:T(8,128)(2,1)S(1)} %shard_map.124.refs_2_.refs_0_), channel_id=1, source_target_pairs={{0,12},{4,8},{8,4},{12,0},{1,13},{5,9},{9,5},{13,1},{2,14},{6,10},... | collective-permute-start | bytes 147464 | tf_op jit(solution)/shard_map/ppermute | solution.py:477
  57.8 5.6 %collective-permute-start.23 = (bf16[24,1024]{1,0:T(8,128)(2,1)S(1)}, bf16[24,1024]{1,0:T(8,128)(2,1)S(1)}, u32[]{:S(2)}, u32[]{:S(2)}) collective-permute-start(bf16[24,1024]{1,0:T(8,128)(2,1)S(1)} %shard_map.124.refs_2_.refs_0_), channel_id=1, source_target_pairs={{0,8},{4,12},{8,0},{12,4},{1,9},{5,13},{9,1},{13,5},{2,10},{6,14},... | collective-permute-start | bytes 147464 | tf_op jit(solution)/shard_map/ppermute | solution.py:477
  57.8 5.6 %collective-permute-start.22 = (bf16[24,1024]{1,0:T(8,128)(2,1)S(1)}, bf16[24,1024]{1,0:T(8,128)(2,1)S(1)}, u32[]{:S(2)}, u32[]{:S(2)}) collective-permute-start(bf16[24,1024]{1,0:T(8,128)(2,1)S(1)} %shard_map.124.refs_2_.refs_0_), channel_id=1, source_target_pairs={{0,4},{4,0},{8,12},{12,8},{1,5},{5,1},{9,13},{13,9},{2,6},{6,2},{1... | collective-permute-start | bytes 147464 | tf_op jit(solution)/shard_map/ppermute | solution.py:477
  64.2 2.2 %collective-permute-start.26 = (bf16[96,1024]{1,0:T(8,128)(2,1)S(1)}, bf16[96,1024]{1,0:T(8,128)(2,1)S(1)}, u32[]{:S(2)}, u32[]{:S(2)}) collective-permute-start(bf16[96,1024]{1,0:T(8,128)(2,1)S(1)} %shard_map.127.refs_2_), channel_id=1, source_target_pairs={{0,1},{1,0},{2,3},{3,2},{4,5},{5,4},{6,7},{7,6},{8,9},{9,8},{10,11... | collective-permute-start | bytes 589832 | tf_op jit(solution)/shard_map/ppermute | solution.py:483
  65.1 2.7 %collective-permute-start.25 = (bf16[96,1024]{1,0:T(8,128)(2,1)S(1)}, bf16[96,1024]{1,0:T(8,128)(2,1)S(1)}, u32[]{:S(2)}, u32[]{:S(2)}) collective-permute-start(bf16[96,1024]{1,0:T(8,128)(2,1)S(1)} %shard_map.128.refs_2_), channel_id=1, source_target_pairs={{0,1},{1,0},{2,3},{3,2},{4,5},{5,4},{6,7},{7,6},{8,9},{9,8},{10,11... | collective-permute-start | bytes 589832 | tf_op jit(solution)/shard_map/ppermute | solution.py:483
  66.4 7.8 %collective-permute-start.28 = (bf16[96,1024]{1,0:T(8,128)(2,1)S(1)}, bf16[96,1024]{1,0:T(8,128)(2,1)S(1)}, u32[]{:S(2)}, u32[]{:S(2)}) collective-permute-start(bf16[96,1024]{1,0:T(8,128)(2,1)S(1)} %shard_map.130.refs_3_.refs_0_), channel_id=1, source_target_pairs={{0,2},{1,3},{2,0},{3,1},{4,6},{5,7},{6,4},{7,5},{8,10},{9,11},{10,... | collective-permute-start | bytes 589832 | tf_op jit(solution)/shard_map/ppermute | solution.py:487
  68.7 8.9 %collective-permute-start.27 = (bf16[96,1024]{1,0:T(8,128)(2,1)S(1)}, bf16[96,1024]{1,0:T(8,128)(2,1)S(1)}, u32[]{:S(2)}, u32[]{:S(2)}) collective-permute-start(bf16[96,1024]{1,0:T(8,128)(2,1)S(1)} %shard_map.131.refs_9_.refs_0_), channel_id=1, source_target_pairs={{0,2},{1,3},{2,0},{3,1},{4,6},{5,7},{6,4},{7,5},{8,10},{9,11},{10,... | collective-permute-start | bytes 589832 | tf_op jit(solution)/shard_map/ppermute | solution.py:487
  74.4 3.8 %collective-permute-start.32 = (bf16[2,32,1024]{2,1,0:T(8,128)(2,1)S(1)}, bf16[2,32,1024]{2,1,0:T(8,128)(2,1)S(1)}, u32[]{:S(2)}, u32[]{:S(2)}) collective-permute-start(bf16[2,32,1024]{2,1,0:T(8,128)(2,1)S(1)} %get-tuple-element.116.refs_1_.refs_4_), channel_id=1, source_target_pairs={{0,1},{1,0},{2,3},{3,2},{4,5},{5,4},{6,7},{7,6},{8,9},{9,8},{10,11... | collective-permute-start | bytes 393224 | tf_op jit(solution)/shard_map/ppermute | solution.py:483
  74.4 4.1 %collective-permute-start.33 = (bf16[2,32,1024]{2,1,0:T(8,128)(2,1)S(1)}, bf16[2,32,1024]{2,1,0:T(8,128)(2,1)S(1)}, u32[]{:S(2)}, u32[]{:S(2)}) collective-permute-start(bf16[2,32,1024]{2,1,0:T(8,128)(2,1)S(1)} %get-tuple-element.117.refs_2_), channel_id=1, source_target_pairs={{0,1},{1,0},{2,3},{3,2},{4,5},{5,4},{6,7},{7,6},{8,9},{9,8},{10,11... | collective-permute-start | bytes 393224 | tf_op jit(solution)/shard_map/ppermute | solution.py:483
  74.9 3.6 %collective-permute-start.34 = (bf16[2,32,1024]{2,1,0:T(8,128)(2,1)S(1)}, bf16[2,32,1024]{2,1,0:T(8,128)(2,1)S(1)}, u32[]{:S(2)}, u32[]{:S(2)}) collective-permute-start(bf16[2,32,1024]{2,1,0:T(8,128)(2,1)S(1)} %get-tuple-element.118.refs_3_), channel_id=1, source_target_pairs={{0,1},{1,0},{2,3},{3,2},{4,5},{5,4},{6,7},{7,6},{8,9},{9,8},{10,11... | collective-permute-start | bytes 393224 | tf_op jit(solution)/shard_map/ppermute | solution.py:483
  77.6 4.6 %collective-permute-start.29 = (bf16[2,32,1024]{2,1,0:T(8,128)(2,1)S(1)}, bf16[2,32,1024]{2,1,0:T(8,128)(2,1)S(1)}, u32[]{:S(2)}, u32[]{:S(2)}) collective-permute-start(bf16[2,32,1024]{2,1,0:T(8,128)(2,1)S(1)} %get-tuple-element.120.refs_4_.refs_7_), channel_id=1, source_target_pairs={{0,1},{1,0},{2,3},{3,2},{4,5},{5,4},{6,7},{7,6},{8,9},{9,8},{10,11... | collective-permute-start | bytes 393224 | tf_op jit(solution)/shard_map/ppermute | solution.py:483
  78.0 4.3 %collective-permute-start.30 = (bf16[2,32,1024]{2,1,0:T(8,128)(2,1)S(1)}, bf16[2,32,1024]{2,1,0:T(8,128)(2,1)S(1)}, u32[]{:S(2)}, u32[]{:S(2)}) collective-permute-start(bf16[2,32,1024]{2,1,0:T(8,128)(2,1)S(1)} %get-tuple-element.121.refs_5_), channel_id=1, source_target_pairs={{0,1},{1,0},{2,3},{3,2},{4,5},{5,4},{6,7},{7,6},{8,9},{9,8},{10,11... | collective-permute-start | bytes 393224 | tf_op jit(solution)/shard_map/ppermute | solution.py:483
  78.2 4.1 %collective-permute-start.31 = (bf16[2,32,1024]{2,1,0:T(8,128)(2,1)S(1)}, bf16[2,32,1024]{2,1,0:T(8,128)(2,1)S(1)}, u32[]{:S(2)}, u32[]{:S(2)}) collective-permute-start(bf16[2,32,1024]{2,1,0:T(8,128)(2,1)S(1)} %get-tuple-element.122.refs_6_), channel_id=1, source_target_pairs={{0,1},{1,0},{2,3},{3,2},{4,5},{5,4},{6,7},{7,6},{8,9},{9,8},{10,11... | collective-permute-start | bytes 393224 | tf_op jit(solution)/shard_map/ppermute | solution.py:483
  (5 other events, 61.5 us)

commit v7 on v6

--- a/solution.py
+++ b/solution.py
@@ -479,6 +479,9 @@
     def back_over_dp(value, step):
         return lax.ppermute(value, "dp", [(i, giver(i, step, groups)) for i in range(groups)])
 
+    def to_all_groups(value):
+        return [value] + [over_dp(value, p) for p in reversed(range(1, groups))][::-1]
+
     def to_core(value):
         return lax.ppermute(value, "mp", [(i, i ^ 1) for i in range(2 * chips)])
 
@@ -496,7 +499,7 @@
     primal, probe = (gate_weight, up_weight), (gate_vector, up_vector)
     wanted = [(w, 1, side, i) for side in (1, 0) for i in each for w in primal]
     held = bring(order, wanted[:-2])
-    rows = assemble(order, [tokens] + [over_dp(tokens, p) for p in range(1, groups)])
+    rows = assemble(order, to_all_groups(tokens))
     sent, sums = [], []
     for n in range(0, len(wanted), 2):
         if n == len(held):
@@ -546,11 +549,11 @@
             carried, _ = contract(order, terms[1:], down_weight, carried, groups, brought)
     held = bring(order, [(down_weight, 0, 1, i) for i in each])
     weighted_mine = weigh(
-        order, carried[0], [back_over_dp(carried[p], p) for p in range(1, groups)], mine
+        order, carried[0], [back_over_dp(carried[p], p) for p in reversed(range(1, groups))], mine
     )
     held += bring(order, [(down_weight, 0, 0, i) for i in each])
     weighted = assemble(
-        order, [weighted_mine] + [over_dp(weighted_mine, p) for p in range(1, groups)]
+        order, to_all_groups(weighted_mine)
     )
 
     sent = [to_core(pull_back(order, weighted, held[i], None)) for i in each]

time: 85 us -> 84.8 us (level)
    ppermute x3, waiting for transfers between devices: 2.18 us -> 1.23 us  [back_over_dp(): lax.ppermute(value, 'dp', [(i, giver(i, step, groups)) for i in range(gro...]
where the time goes in v7:
time: 84.8 us; the launch traced here: 84.6 us
  Pallas kernels  50.3 us (59%)
  starting transfers between devices  26.8 us (32%)
  waiting for transfers between devices  6.16 us (7%)
  between operations  1.19 us (1%)
    pallas_call x35, Pallas kernels, call(): pl.pallas_call(kernel, in_specs=[SMEM] + [HBM if isinstance(o, InHbm) els...  50.3 us
    ppermute x6, starting transfers between devices, over_dp(): lax.ppermute(value, 'dp', [(i, partner(i, step, groups)) for i in range(g...  10.1 us
    ppermute x6, starting transfers between devices, over_chips(): lax.ppermute(value, 'mp', [(2 * i + c, 2 * partner(i, k, chips) + c) for...  7.01 us
    ppermute x20, starting transfers between devices, to_core(): return lax.ppermute(value, 'mp', [(i, i ^ 1) for i in range(2 * chips)])  5.25 us
    ppermute x3, starting transfers between devices, back_over_dp(): lax.ppermute(value, 'dp', [(i, giver(i, step, groups)) for i in range(gro...  4.45 us
    ppermute x6, waiting for transfers between devices, over_dp(): lax.ppermute(value, 'dp', [(i, partner(i, step, groups)) for i in range(g...  2.33 us
  transfers between devices with their start and end apart: 35, of which 8 were waited for; matrix products, arithmetic and copies ran while one was open for 0% of the time, Pallas kernels for 54%

profile of v7, /device:TPU:0, one launch (start us, length us, event | category | flops | bytes accessed | tf_op | source)
XLA Modules:
  0.0 84.6 jit_solution(16241534600965573010)
XLA Ops:
  0.6 4.1 %collective-permute-start.1 = (bf16[24,1024]{1,0:T(8,128)(2,1)}, bf16[24,1024]{1,0:T(8,128)(2,1)S(1)}, u32[]{:S(2)}, u32[]{:S(2)}) collective-permute-start(bf16[24,1024]{1,0:T(8,128)(2,1)} %refs_0_.9), channel_id=1, source_target_pairs={{0,8},{4,12},{8,0},{12,4},{1,9},{5,13},{9,1},{13,5},{2,10},{6,14},... | collective-permute-start | bytes 147464 | tf_op jit(solution)/shard_map/ppermute | solution.py:477
  4.7 1.6 %collective-permute-start = (bf16[24,1024]{1,0:T(8,128)(2,1)}, bf16[24,1024]{1,0:T(8,128)(2,1)S(1)}, u32[]{:S(2)}, u32[]{:S(2)}) collective-permute-start(bf16[24,1024]{1,0:T(8,128)(2,1)} %refs_0_.9), channel_id=1, source_target_pairs={{0,4},{4,0},{8,12},{12,8},{1,5},{5,1},{9,13},{13,9},{2,6},{6,2},{1... | collective-permute-start | bytes 147464 | tf_op jit(solution)/shard_map/ppermute | solution.py:477
  6.3 4.8 %shard_map.103 = (f32[8,128]{1,0:T(8,128)S(1)}, bf16[1024,1024]{1,0:T(8,128)(2,1)S(1)}, bf16[1024,1024]{1,0:T(8,128)(2,1)S(1)}, bf16[1024,1024]{1,0:T(8,128)(2,1...) custom-call(s32[1]{0:T(128)} %bitcast.core_ref, ...), custom_call_target="tpu_custom_call" | custom-call | flops 1 | bytes 1 | tf_op jit(solution)/shard_map/pallas_call | solution.py:64
  11.1 1.3 %collective-permute-done.2.refs_3_ = bf16[24,1024]{1,0:T(8,128)(2,1)S(1)} collective-permute-done((bf16[24,1024]{1,0:T(8,128)(2,1)}, bf16[24,1024]{1,0:T(8,128)(2,1)S(1)}, u32[]{:S(2)}, u32[]{:S(2)}) %collective-permute-start.2) | collective-permute-done | bytes 49184 | tf_op jit(solution)/shard_map/ppermute | solution.py:477
  12.4 0.8 shard_map.105.refs_3_
  15.6 1.6 %collective-permute-start.9 = (bf16[2,96,1024]{2,1,0:T(8,128)(2,1)S(1)}, bf16[2,96,1024]{2,1,0:T(8,128)(2,1)S(1)}, u32[]{:S(2)}, u32[]{:S(2)}) collective-permute-start(bf16[2,96,1024]{2,1,0:T(8,128)(2,1)S(1)} %shard_map.108.refs_2_.refs_0_), channel_id=1, source_target_pairs={{0,2},{1,3},{2,0},{3,1},{4,6},{5,7},{6,4},{7,5},{8,10},{9,11},{10,... | collective-permute-start | bytes 1179656 | tf_op jit(solution)/shard_map/ppermute | solution.py:490
  17.1 2.2 %shard_map.109 = (f32[8,128]{1,0:T(8,128)S(1)}, bf16[1024,1024]{1,0:T(8,128)(2,1)S(1)}, bf16[1024,1024]{1,0:T(8,128)(2,1)S(1)}) custom-call(s32[1]{0:T(128)} %bitcast.core_ref, bf16[1024,4096]{1,0:T(8,128)(2,1)} %refs_0_.10, bf16[1024,4096]{1,0:T(8,128)(2,1)} %refs_1_.9, bf16[2,96,1024]{2,1,0:T(8,128)(2,1)S(1)} %shard_map.108.refs_2_.refs_0_), custom_call_target="tpu_custom_call" | custom-call | flops 1 | bytes 1 | tf_op jit(solution)/shard_map/pallas_call | solution.py:64
  19.4 0.8 shard_map.110.refs_3_.refs_0_
  20.8 4.0 %shard_map.111 = (bf16[2,32,2048]{2,1,0:T(8,128)(2,1)S(1)}, bf16[2,32,2048]{2,1,0:T(8,128)(2,1)S(1)}, bf16[2,32,2048]{2,1,0:T(8,128)(2,1)S(1)}) custom-call(s32[1]{0:T(128)} %bitcast.core_ref, bf16[96,1024]{1,0:T(8,128)(2,1)S(1)} %shard_map.104.refs_0_.refs_3_, bf16[1024,4096]{1,0:T(8,128)(2,1)} %refs_1_.11, bf16[1024,4096]{1,0:T(8,128)(2,1)} %refs_3_.4, ...), custom_call_target="tpu_custom_call" | custom-call | flops 1 | bytes 1 | tf_op jit(solution)/shard_map/pallas_call | solution.py:64
  25.5 3.5 %shard_map.112 = (f32[8,128]{1,0:T(8,128)S(1)}, bf16[1024,1024]{1,0:T(8,128)(2,1)S(1)}, bf16[1024,1024]{1,0:T(8,128)(2,1)S(1)}, bf16[1024,1024]{1,0:T(8,128)(2,1)S(1)}, bf16[1024,1024]{1,0:T(8,128)(2,1)S(1)}) custom-call(s32[1]{0:T(128)} %bitcast.core_ref, bf16[1024,4096]{1,0:T(8,128)(2,1)} %refs_1_.11, bf16[1024,4096]{1,0:T(8,128)(2,1)} %refs_1_.11, ...), custom_call_target="tpu_custom_call" | custom-call | flops 1 | bytes 1 | tf_op jit(solution)/shard_map/pallas_call | solution.py:64
  29.1 1.5 %shard_map.113.refs_2_.refs_3_ = f32[2,96,2048]{2,1,0:T(8,128)S(1)} custom-call(s32[1]{0:T(128)} %bitcast.core_ref, bf16[96,1024]{1,0:T(8,128)(2,1)S(1)} %shard_map.104.refs_0_.refs_3_, bf16[1024,1024]{1,0:T(8,128)(2,1)S(1)} %get-tuple-element.78.refs_1_, bf16[1024,1024]{1,0:T(8,128)(2,1)S(1)} %get-tuple-element.79.refs_2_, ...), custom_call_target="tpu_custom_call" | custom-call | flops 1 | bytes 1 | tf_op jit(solution)/shard_map/pallas_call | solution.py:64
  31.5 1.5 %collective-permute-start.15 = (bf16[96,1024]{1,0:T(8,128)(2,1)S(1)}, bf16[96,1024]{1,0:T(8,128)(2,1)S(1)}, u32[]{:S(2)}, u32[]{:S(2)}) collective-permute-start(bf16[96,1024]{1,0:T(8,128)(2,1)S(1)} %get-tuple-element.87.refs_7_.refs_0_), channel_id=1, source_target_pairs={{0,2},{1,3},{2,0},{3,1},{4,6},{5,7},{6,4},{7,5},{8,10},{9,11},{10,... | collective-permute-start | bytes 589832 | tf_op jit(solution)/shard_map/ppermute | solution.py:490
  33.0 3.5 %shard_map.115 = (f32[96,1024]{1,0:T(8,128)S(1)}, bf16[1024,1024]{1,0:T(8,128)(2,1)S(1)}, bf16[1024,1024]{1,0:T(8,128)(2,1)S(1)}) custom-call(s32[1]{0:T(128)} %bitcast.core_ref, bf16[4096,1024]{1,0:T(8,128)(2,1)} %refs_2_.8, bf16[4096,1024]{1,0:T(8,128)(2,1)} %refs_2_.8, bf16[4096,1024]{1,0:T(8,128)(2,1)} %refs_2_.8, ...), custom_call_target="tpu_custom_call" | custom-call | flops 1 | bytes 1 | tf_op jit(solution)/shard_map/pallas_call | solution.py:64
  37.4 1.2 %collective-permute-start.12 = (bf16[96,1024]{1,0:T(8,128)(2,1)S(1)}, bf16[96,1024]{1,0:T(8,128)(2,1)S(1)}, u32[]{:S(2)}, u32[]{:S(2)}) collective-permute-start(bf16[96,1024]{1,0:T(8,128)(2,1)S(1)} %get-tuple-element.89.refs_9_.refs_0_), channel_id=1, source_target_pairs={{0,2},{1,3},{2,0},{3,1},{4,6},{5,7},{6,4},{7,5},{8,10},{9,11},{10,... | collective-permute-start | bytes 589832 | tf_op jit(solution)/shard_map/ppermute | solution.py:490
  38.7 2.9 %shard_map.117 = (f32[96,1024]{1,0:T(8,128)S(1)}, bf16[1024,1024]{1,0:T(8,128)(2,1)S(1)}, bf16[1024,1024]{1,0:T(8,128)(2,1)S(1)}) custom-call(s32[1]{0:T(128)} %bitcast.core_ref, bf16[1024,1024]{1,0:T(8,128)(2,1)S(1)} %get-tuple-element.90.refs_0_, bf16[1024,1024]{1,0:T(8,128)(2,1)S(1)} %get-tuple-element.91.refs_1_, bf16[4096,1024]{1,0:T(8,128)(2,1)} %refs_1_.15, ...), custom_call_target="tpu_custom_call" | custom-call | flops 1 | bytes 1 | tf_op jit(solution)/shard_map/pallas_call | solution.py:64
  44.5 2.2 %shard_map.121 = (f32[96,1024]{1,0:T(8,128)S(1)}, bf16[1024,1024]{1,0:T(8,128)(2,1)S(1)}) custom-call(s32[1]{0:T(128)} %bitcast.core_ref, bf16[4096,1024]{1,0:T(8,128)(2,1)} %refs_1_.15, bf16[4096,1024]{1,0:T(8,128)(2,1)} %refs_1_.15, bf16[96,1024]{1,0:T(8,128)(2,1)S(1)} %shard_map.120.refs_2_.refs_4_, f32[96,1024]{1,0:T(8,128)S(1)} %shard_map.119.refs_2_.refs_3_, ...), custom_call_target="tpu_custom_call" | custom-call | flops 1 | bytes 1 | tf_op jit(solution)/shard_map/pallas_call | solution.py:64
  47.3 2.6 %collective-permute-start.19 = (bf16[24,1024]{1,0:T(8,128)(2,1)S(1)}, bf16[24,1024]{1,0:T(8,128)(2,1)S(1)}, u32[]{:S(2)}, u32[]{:S(2)}) collective-permute-start(bf16[24,1024]{1,0:T(8,128)(2,1)S(1)} %get-tuple-element.102), channel_id=1, source_target_pairs={{0,12},{4,8},{8,4},{12,0},{1,13},{5,9},{9,5},{13,1},{2,14},{6,10},... | collective-permute-start | bytes 147464 | tf_op jit(solution)/shard_map/ppermute | solution.py:480
  49.9 1.8 %collective-permute-start.21 = (bf16[24,1024]{1,0:T(8,128)(2,1)S(1)}, bf16[24,1024]{1,0:T(8,128)(2,1)S(1)}, u32[]{:S(2)}, u32[]{:S(2)}) collective-permute-start(bf16[24,1024]{1,0:T(8,128)(2,1)S(1)} %get-tuple-element.104), channel_id=1, source_target_pairs={{0,4},{4,0},{8,12},{12,8},{1,5},{5,1},{9,13},{13,9},{2,6},{6,2},{1... | collective-permute-start | bytes 147464 | tf_op jit(solution)/shard_map/ppermute | solution.py:480
  51.9 2.2 %shard_map.123 = (f32[8,128]{1,0:T(8,128)S(1)}, bf16[1024,1024]{1,0:T(8,128)(2,1)S(1)}, bf16[1024,1024]{1,0:T(8,128)(2,1)S(1)}) custom-call(s32[1]{0:T(128)} %bitcast.core_ref, bf16[4096,1024]{1,0:T(8,128)(2,1)} %refs_1_.15, bf16[4096,1024]{1,0:T(8,128)(2,1)} %refs_1_.15, f32[24,1024]{1,0:T(8,128)S(1)} %get-tuple-element.101.refs_2_.refs_0_), custom_call_target="tpu_custom_call" | custom-call | flops 1 | bytes 1 | tf_op jit(solution)/shard_map/pallas_call | solution.py:64
  54.1 1.2 %collective-permute-done.20.refs_2_ = bf16[24,1024]{1,0:T(8,128)(2,1)S(1)} collective-permute-done((bf16[24,1024]{1,0:T(8,128)(2,1)S(1)}, bf16[24,1024]{1,0:T(8,128)(2,1)S(1)}, u32[]{:S(2)}, u32[]{:S(2)}) %collective-permute-start.20) | collective-permute-done | bytes 49184 | tf_op jit(solution)/shard_map/ppermute | solution.py:480
  55.4 2.6 %collective-permute-start.24 = (bf16[24,1024]{1,0:T(8,128)(2,1)S(1)}, bf16[24,1024]{1,0:T(8,128)(2,1)S(1)}, u32[]{:S(2)}, u32[]{:S(2)}) collective-permute-start(bf16[24,1024]{1,0:T(8,128)(2,1)S(1)} %shard_map.124.refs_2_.refs_0_), channel_id=1, source_target_pairs={{0,12},{4,8},{8,4},{12,0},{1,13},{5,9},{9,5},{13,1},{2,14},{6,10},... | collective-permute-start | bytes 147464 | tf_op jit(solution)/shard_map/ppermute | solution.py:477
  58.0 1.8 %collective-permute-start.22 = (bf16[24,1024]{1,0:T(8,128)(2,1)S(1)}, bf16[24,1024]{1,0:T(8,128)(2,1)S(1)}, u32[]{:S(2)}, u32[]{:S(2)}) collective-permute-start(bf16[24,1024]{1,0:T(8,128)(2,1)S(1)} %shard_map.124.refs_2_.refs_0_), channel_id=1, source_target_pairs={{0,4},{4,0},{8,12},{12,8},{1,5},{5,1},{9,13},{13,9},{2,6},{6,2},{1... | collective-permute-start | bytes 147464 | tf_op jit(solution)/shard_map/ppermute | solution.py:477
  59.9 2.2 %shard_map.125 = (f32[8,128]{1,0:T(8,128)S(1)}, bf16[1024,1024]{1,0:T(8,128)(2,1)S(1)}, bf16[1024,1024]{1,0:T(8,128)(2,1)S(1)}) custom-call(s32[1]{0:T(128)} %bitcast.core_ref, bf16[4096,1024]{1,0:T(8,128)(2,1)} %refs_1_.15, bf16[4096,1024]{1,0:T(8,128)(2,1)} %refs_1_.15, bf16[24,1024]{1,0:T(8,128)(2,1)S(1)} %shard_map.124.refs_2_.refs_0_), custom_call_target="tpu_custom_call" | custom-call | flops 1 | bytes 1 | tf_op jit(solution)/shard_map/pallas_call | solution.py:64
  62.1 1.0 %collective-permute-done.23.refs_2_ = bf16[24,1024]{1,0:T(8,128)(2,1)S(1)} collective-permute-done((bf16[24,1024]{1,0:T(8,128)(2,1)S(1)}, bf16[24,1024]{1,0:T(8,128)(2,1)S(1)}, u32[]{:S(2)}, u32[]{:S(2)}) %collective-permute-start.23) | collective-permute-done | bytes 49184 | tf_op jit(solution)/shard_map/ppermute | solution.py:477
  66.2 1.3 %collective-permute-start.28 = (bf16[96,1024]{1,0:T(8,128)(2,1)S(1)}, bf16[96,1024]{1,0:T(8,128)(2,1)S(1)}, u32[]{:S(2)}, u32[]{:S(2)}) collective-permute-start(bf16[96,1024]{1,0:T(8,128)(2,1)S(1)} %shard_map.130.refs_3_.refs_0_), channel_id=1, source_target_pairs={{0,2},{1,3},{2,0},{3,1},{4,6},{5,7},{6,4},{7,5},{8,10},{9,11},{10,... | collective-permute-start | bytes 589832 | tf_op jit(solution)/shard_map/ppermute | solution.py:490
  67.4 0.9 %shard_map.131.refs_9_.refs_0_ = bf16[96,1024]{1,0:T(8,128)(2,1)S(1)} custom-call(s32[1]{0:T(128)} %bitcast.core_ref, bf16[96,1024]{1,0:T(8,128)(2,1)S(1)} %shard_map.126.refs_0_.refs_2_.refs_8_, bf16[1024,1024]{1,0:T(8,128)(2,1)S(1)} %get-tuple-element.107.refs_1_, bf16[96,1024]{1,0:T(8,128)(2,1)S(1)} %collective-permute-done.25.refs_2_, ...), custom_call_target="tpu_custom_call" | custom-call | flops 1 | bytes 1 | tf_op jit(solution)/shard_map/pallas_call | solution.py:64
  68.4 0.9 %collective-permute-start.27 = (bf16[96,1024]{1,0:T(8,128)(2,1)S(1)}, bf16[96,1024]{1,0:T(8,128)(2,1)S(1)}, u32[]{:S(2)}, u32[]{:S(2)}) collective-permute-start(bf16[96,1024]{1,0:T(8,128)(2,1)S(1)} %shard_map.131.refs_9_.refs_0_), channel_id=1, source_target_pairs={{0,2},{1,3},{2,0},{3,1},{4,6},{5,7},{6,4},{7,5},{8,10},{9,11},{10,... | collective-permute-start | bytes 589832 | tf_op jit(solution)/shard_map/ppermute | solution.py:490
  69.3 3.7 %shard_map.132 = (f32[8,128]{1,0:T(8,128)S(1)}, bf16[4096,1024]{1,0:T(8,128)(2,1)}) custom-call(s32[1]{0:T(128)} %bitcast.core_ref, bf16[48,1024]{1,0:T(8,128)(2,1)S(1)} %get-tuple-element.85.refs_3_.refs_0_, bf16[48,1024]{1,0:T(8,128)(2,1)S(1)} %get-tuple-element.86.refs_4_.refs_1_, bf16[48,1024]{1,0:T(8,128)(2,1)S(1)} %get-tuple-element.92.refs_4_.refs_2_, ...), custom_call_target="tpu_custom_call" | custom-call | flops 1 | bytes 1 | tf_op jit(solution)/shard_map/pallas_call | solution.py:64
  73.0 1.0 %collective-permute-done.28.refs_1_ = bf16[96,1024]{1,0:T(8,128)(2,1)S(1)} collective-permute-done((bf16[96,1024]{1,0:T(8,128)(2,1)S(1)}, bf16[96,1024]{1,0:T(8,128)(2,1)S(1)}, u32[]{:S(2)}, u32[]{:S(2)}) %collective-permute-start.28) | collective-permute-done | bytes 196640 | tf_op jit(solution)/shard_map/ppermute | solution.py:490
  74.8 2.4 %shard_map.134 = (f32[8,128]{1,0:T(8,128)S(1)}, bf16[1024,4096]{1,0:T(8,128)(2,1)}, bf16[1024,4096]{1,0:T(8,128)(2,1)}) custom-call(s32[1]{0:T(128)} %bitcast.core_ref, bf16[96,1024]{1,0:T(8,128)(2,1)S(1)} %shard_map.104.refs_0_.refs_3_, bf16[2,32,1024]{2,1,0:T(8,128)(2,1)S(1)} %get-tuple-element.116.refs_1_.refs_4_, ...), custom_call_target="tpu_custom_call" | custom-call | flops 1 | bytes 1 | tf_op jit(solution)/shard_map/pallas_call | solution.py:64
  78.3 3.7 %shard_map.136 = (f32[8,128]{1,0:T(8,128)S(1)}, bf16[1024,4096]{1,0:T(8,128)(2,1)}, bf16[1024,4096]{1,0:T(8,128)(2,1)}) custom-call(s32[1]{0:T(128)} %bitcast.core_ref, bf16[96,1024]{1,0:T(8,128)(2,1)S(1)} %shard_map.104.refs_0_.refs_3_, bf16[2,32,1024]{2,1,0:T(8,128)(2,1)S(1)} %collective-permute-done.32.refs_1_, ...), custom_call_target="tpu_custom_call", output_to_operand_aliasing={{1}: (9, {}), {2}: (10, {})} | custom-call | flops 1 | bytes 1 | tf_op jit(solution)/shard_map/pallas_call | solution.py:64
  82.0 2.4 %shard_map.137 = (bf16[1024,4096]{1,0:T(8,128)(2,1)}, bf16[1024,4096]{1,0:T(8,128)(2,1)}) custom-call(s32[1]{0:T(128)} %bitcast.core_ref, bf16[96,1024]{1,0:T(8,128)(2,1)S(1)} %shard_map.104.refs_0_.refs_3_, bf16[2,32,1024]{2,1,0:T(8,128)(2,1)S(1)} %collective-permute-done.29.refs_1_, ...), custom_call_target="tpu_custom_call", output_to_operand_aliasing={{0}: (6, {}), {1}: (7, {})} | custom-call | flops 1 | bytes 1 | tf_op jit(solution)/shard_map/pallas_call | solution.py:64
  (79 shorter events, 14.0 us)
Async XLA Ops:
  0.6 10.5 %collective-permute-start.1 = (bf16[24,1024]{1,0:T(8,128)(2,1)}, bf16[24,1024]{1,0:T(8,128)(2,1)S(1)}, u32[]{:S(2)}, u32[]{:S(2)}) collective-permute-start(bf16[24,1024]{1,0:T(8,128)(2,1)} %refs_0_.9), channel_id=1, source_target_pairs={{0,8},{4,12},{8,0},{12,4},{1,9},{5,13},{9,1},{13,5},{2,10},{6,14},... | collective-permute-start | bytes 147464 | tf_op jit(solution)/shard_map/ppermute | solution.py:477
  4.7 6.4 %collective-permute-start = (bf16[24,1024]{1,0:T(8,128)(2,1)}, bf16[24,1024]{1,0:T(8,128)(2,1)S(1)}, u32[]{:S(2)}, u32[]{:S(2)}) collective-permute-start(bf16[24,1024]{1,0:T(8,128)(2,1)} %refs_0_.9), channel_id=1, source_target_pairs={{0,4},{4,0},{8,12},{12,8},{1,5},{5,1},{9,13},{13,9},{2,6},{6,2},{1... | collective-permute-start | bytes 147464 | tf_op jit(solution)/shard_map/ppermute | solution.py:477
  6.3 6.1 %collective-permute-start.2 = (bf16[24,1024]{1,0:T(8,128)(2,1)}, bf16[24,1024]{1,0:T(8,128)(2,1)S(1)}, u32[]{:S(2)}, u32[]{:S(2)}) collective-permute-start(bf16[24,1024]{1,0:T(8,128)(2,1)} %refs_0_.9), channel_id=1, source_target_pairs={{0,12},{4,8},{8,4},{12,0},{1,13},{5,9},{9,5},{13,1},{2,14},{6,10},... | collective-permute-start | bytes 147464 | tf_op jit(solution)/shard_map/ppermute | solution.py:477
  13.3 2.3 %collective-permute-start.3 = (bf16[2,96,1024]{2,1,0:T(8,128)(2,1)S(1)}, bf16[2,96,1024]{2,1,0:T(8,128)(2,1)S(1)}, u32[]{:S(2)}, u32[]{:S(2)}) collective-permute-start(bf16[2,96,1024]{2,1,0:T(8,128)(2,1)S(1)} %shard_map.105.refs_3_), channel_id=1, source_target_pairs={{0,1},{1,0},{2,3},{3,2},{4,5},{5,4},{6,7},{7,6},{8,9},{9,8},{10,11... | collective-permute-start | bytes 1179656 | tf_op jit(solution)/shard_map/ppermute | solution.py:486
  14.1 5.3 %collective-permute-start.4 = (bf16[2,96,1024]{2,1,0:T(8,128)(2,1)S(1)}, bf16[2,96,1024]{2,1,0:T(8,128)(2,1)S(1)}, u32[]{:S(2)}, u32[]{:S(2)}) collective-permute-start(bf16[2,96,1024]{2,1,0:T(8,128)(2,1)S(1)} %shard_map.106.refs_3_), channel_id=1, source_target_pairs={{0,1},{1,0},{2,3},{3,2},{4,5},{5,4},{6,7},{7,6},{8,9},{9,8},{10,11... | collective-permute-start | bytes 1179656 | tf_op jit(solution)/shard_map/ppermute | solution.py:486
  15.6 15.0 %collective-permute-start.9 = (bf16[2,96,1024]{2,1,0:T(8,128)(2,1)S(1)}, bf16[2,96,1024]{2,1,0:T(8,128)(2,1)S(1)}, u32[]{:S(2)}, u32[]{:S(2)}) collective-permute-start(bf16[2,96,1024]{2,1,0:T(8,128)(2,1)S(1)} %shard_map.108.refs_2_.refs_0_), channel_id=1, source_target_pairs={{0,2},{1,3},{2,0},{3,1},{4,6},{5,7},{6,4},{7,5},{8,10},{9,11},{10,... | collective-permute-start | bytes 1179656 | tf_op jit(solution)/shard_map/ppermute | solution.py:490
  20.2 16.3 %collective-permute-start.5 = (bf16[2,96,1024]{2,1,0:T(8,128)(2,1)S(1)}, bf16[2,96,1024]{2,1,0:T(8,128)(2,1)S(1)}, u32[]{:S(2)}, u32[]{:S(2)}) collective-permute-start(bf16[2,96,1024]{2,1,0:T(8,128)(2,1)S(1)} %shard_map.110.refs_3_.refs_0_), channel_id=1, source_target_pairs={{0,2},{1,3},{2,0},{3,1},{4,6},{5,7},{6,4},{7,5},{8,10},{9,11},{10,... | collective-permute-start | bytes 1179656 | tf_op jit(solution)/shard_map/ppermute | solution.py:490
  24.9 4.2 %collective-permute-start.7 = (bf16[2,32,2048]{2,1,0:T(8,128)(2,1)S(1)}, bf16[2,32,2048]{2,1,0:T(8,128)(2,1)S(1)}, u32[]{:S(2)}, u32[]{:S(2)}) collective-permute-start(bf16[2,32,2048]{2,1,0:T(8,128)(2,1)S(1)} %get-tuple-element.82), channel_id=1, source_target_pairs={{0,1},{1,0},{2,3},{3,2},{4,5},{5,4},{6,7},{7,6},{8,9},{9,8},{10,11... | collective-permute-start | bytes 786440 | tf_op jit(solution)/shard_map/ppermute | solution.py:486
  25.0 4.1 %collective-permute-start.8 = (bf16[2,32,2048]{2,1,0:T(8,128)(2,1)S(1)}, bf16[2,32,2048]{2,1,0:T(8,128)(2,1)S(1)}, u32[]{:S(2)}, u32[]{:S(2)}) collective-permute-start(bf16[2,32,2048]{2,1,0:T(8,128)(2,1)S(1)} %get-tuple-element.83), channel_id=1, source_target_pairs={{0,1},{1,0},{2,3},{3,2},{4,5},{5,4},{6,7},{7,6},{8,9},{9,8},{10,11... | collective-permute-start | bytes 786440 | tf_op jit(solution)/shard_map/ppermute | solution.py:486
  25.4 3.6 %collective-permute-start.6 = (bf16[2,32,2048]{2,1,0:T(8,128)(2,1)S(1)}, bf16[2,32,2048]{2,1,0:T(8,128)(2,1)S(1)}, u32[]{:S(2)}, u32[]{:S(2)}) collective-permute-start(bf16[2,32,2048]{2,1,0:T(8,128)(2,1)S(1)} %get-tuple-element.77.refs_4_), channel_id=1, source_target_pairs={{0,1},{1,0},{2,3},{3,2},{4,5},{5,4},{6,7},{7,6},{8,9},{9,8},{10,11... | collective-permute-start | bytes 786440 | tf_op jit(solution)/shard_map/ppermute | solution.py:486
  30.9 2.1 %collective-permute-start.10 = (bf16[48,1024]{1,0:T(8,128)(2,1)S(1)}, bf16[48,1024]{1,0:T(8,128)(2,1)S(1)}, u32[]{:S(2)}, u32[]{:S(2)}) collective-permute-start(bf16[48,1024]{1,0:T(8,128)(2,1)S(1)} %get-tuple-element.85.refs_3_.refs_0_), channel_id=1, source_target_pairs={{0,1},{1,0},{2,3},{3,2},{4,5},{5,4},{6,7},{7,6},{8,9},{9,8},{10,11... | collective-permute-start | bytes 294920 | tf_op jit(solution)/shard_map/ppermute | solution.py:486
  31.4 1.6 %collective-permute-start.11 = (bf16[48,1024]{1,0:T(8,128)(2,1)S(1)}, bf16[48,1024]{1,0:T(8,128)(2,1)S(1)}, u32[]{:S(2)}, u32[]{:S(2)}) collective-permute-start(bf16[48,1024]{1,0:T(8,128)(2,1)S(1)} %get-tuple-element.86.refs_4_.refs_1_), channel_id=1, source_target_pairs={{0,1},{1,0},{2,3},{3,2},{4,5},{5,4},{6,7},{7,6},{8,9},{9,8},{10,11... | collective-permute-start | bytes 294920 | tf_op jit(solution)/shard_map/ppermute | solution.py:486
  31.5 10.0 %collective-permute-start.15 = (bf16[96,1024]{1,0:T(8,128)(2,1)S(1)}, bf16[96,1024]{1,0:T(8,128)(2,1)S(1)}, u32[]{:S(2)}, u32[]{:S(2)}) collective-permute-start(bf16[96,1024]{1,0:T(8,128)(2,1)S(1)} %get-tuple-element.87.refs_7_.refs_0_), channel_id=1, source_target_pairs={{0,2},{1,3},{2,0},{3,1},{4,6},{5,7},{6,4},{7,5},{8,10},{9,11},{10,... | collective-permute-start | bytes 589832 | tf_op jit(solution)/shard_map/ppermute | solution.py:490
  36.9 1.8 %collective-permute-start.13 = (bf16[48,1024]{1,0:T(8,128)(2,1)S(1)}, bf16[48,1024]{1,0:T(8,128)(2,1)S(1)}, u32[]{:S(2)}, u32[]{:S(2)}) collective-permute-start(bf16[48,1024]{1,0:T(8,128)(2,1)S(1)} %get-tuple-element.92.refs_4_.refs_2_), channel_id=1, source_target_pairs={{0,1},{1,0},{2,3},{3,2},{4,5},{5,4},{6,7},{7,6},{8,9},{9,8},{10,11... | collective-permute-start | bytes 294920 | tf_op jit(solution)/shard_map/ppermute | solution.py:486
  37.4 7.0 %collective-permute-start.12 = (bf16[96,1024]{1,0:T(8,128)(2,1)S(1)}, bf16[96,1024]{1,0:T(8,128)(2,1)S(1)}, u32[]{:S(2)}, u32[]{:S(2)}) collective-permute-start(bf16[96,1024]{1,0:T(8,128)(2,1)S(1)} %get-tuple-element.89.refs_9_.refs_0_), channel_id=1, source_target_pairs={{0,2},{1,3},{2,0},{3,1},{4,6},{5,7},{6,4},{7,5},{8,10},{9,11},{10,... | collective-permute-start | bytes 589832 | tf_op jit(solution)/shard_map/ppermute | solution.py:490
  44.5 2.3 %collective-permute-start.18 = (bf16[96,1024]{1,0:T(8,128)(2,1)S(1)}, bf16[96,1024]{1,0:T(8,128)(2,1)S(1)}, u32[]{:S(2)}, u32[]{:S(2)}) collective-permute-start(bf16[96,1024]{1,0:T(8,128)(2,1)S(1)} %shard_map.120.refs_2_.refs_4_), channel_id=1, source_target_pairs={{0,1},{1,0},{2,3},{3,2},{4,5},{5,4},{6,7},{7,6},{8,9},{9,8},{10,11... | collective-permute-start | bytes 589832 | tf_op jit(solution)/shard_map/ppermute | solution.py:486
  47.3 6.9 %collective-permute-start.19 = (bf16[24,1024]{1,0:T(8,128)(2,1)S(1)}, bf16[24,1024]{1,0:T(8,128)(2,1)S(1)}, u32[]{:S(2)}, u32[]{:S(2)}) collective-permute-start(bf16[24,1024]{1,0:T(8,128)(2,1)S(1)} %get-tuple-element.102), channel_id=1, source_target_pairs={{0,12},{4,8},{8,4},{12,0},{1,13},{5,9},{9,5},{13,1},{2,14},{6,10},... | collective-permute-start | bytes 147464 | tf_op jit(solution)/shard_map/ppermute | solution.py:480
  49.9 5.5 %collective-permute-start.20 = (bf16[24,1024]{1,0:T(8,128)(2,1)S(1)}, bf16[24,1024]{1,0:T(8,128)(2,1)S(1)}, u32[]{:S(2)}, u32[]{:S(2)}) collective-permute-start(bf16[24,1024]{1,0:T(8,128)(2,1)S(1)} %get-tuple-element.103), channel_id=1, source_target_pairs={{0,8},{4,12},{8,0},{12,4},{1,9},{5,13},{9,1},{13,5},{2,10},{6,14},... | collective-permute-start | bytes 147464 | tf_op jit(solution)/shard_map/ppermute | solution.py:480
  49.9 5.5 %collective-permute-start.21 = (bf16[24,1024]{1,0:T(8,128)(2,1)S(1)}, bf16[24,1024]{1,0:T(8,128)(2,1)S(1)}, u32[]{:S(2)}, u32[]{:S(2)}) collective-permute-start(bf16[24,1024]{1,0:T(8,128)(2,1)S(1)} %get-tuple-element.104), channel_id=1, source_target_pairs={{0,4},{4,0},{8,12},{12,8},{1,5},{5,1},{9,13},{13,9},{2,6},{6,2},{1... | collective-permute-start | bytes 147464 | tf_op jit(solution)/shard_map/ppermute | solution.py:480
  55.4 6.7 %collective-permute-start.24 = (bf16[24,1024]{1,0:T(8,128)(2,1)S(1)}, bf16[24,1024]{1,0:T(8,128)(2,1)S(1)}, u32[]{:S(2)}, u32[]{:S(2)}) collective-permute-start(bf16[24,1024]{1,0:T(8,128)(2,1)S(1)} %shard_map.124.refs_2_.refs_0_), channel_id=1, source_target_pairs={{0,12},{4,8},{8,4},{12,0},{1,13},{5,9},{9,5},{13,1},{2,14},{6,10},... | collective-permute-start | bytes 147464 | tf_op jit(solution)/shard_map/ppermute | solution.py:477
  58.0 5.1 %collective-permute-start.23 = (bf16[24,1024]{1,0:T(8,128)(2,1)S(1)}, bf16[24,1024]{1,0:T(8,128)(2,1)S(1)}, u32[]{:S(2)}, u32[]{:S(2)}) collective-permute-start(bf16[24,1024]{1,0:T(8,128)(2,1)S(1)} %shard_map.124.refs_2_.refs_0_), channel_id=1, source_target_pairs={{0,8},{4,12},{8,0},{12,4},{1,9},{5,13},{9,1},{13,5},{2,10},{6,14},... | collective-permute-start | bytes 147464 | tf_op jit(solution)/shard_map/ppermute | solution.py:477
  58.0 5.1 %collective-permute-start.22 = (bf16[24,1024]{1,0:T(8,128)(2,1)S(1)}, bf16[24,1024]{1,0:T(8,128)(2,1)S(1)}, u32[]{:S(2)}, u32[]{:S(2)}) collective-permute-start(bf16[24,1024]{1,0:T(8,128)(2,1)S(1)} %shard_map.124.refs_2_.refs_0_), channel_id=1, source_target_pairs={{0,4},{4,0},{8,12},{12,8},{1,5},{5,1},{9,13},{13,9},{2,6},{6,2},{1... | collective-permute-start | bytes 147464 | tf_op jit(solution)/shard_map/ppermute | solution.py:477
  63.9 2.2 %collective-permute-start.26 = (bf16[96,1024]{1,0:T(8,128)(2,1)S(1)}, bf16[96,1024]{1,0:T(8,128)(2,1)S(1)}, u32[]{:S(2)}, u32[]{:S(2)}) collective-permute-start(bf16[96,1024]{1,0:T(8,128)(2,1)S(1)} %shard_map.127.refs_2_), channel_id=1, source_target_pairs={{0,1},{1,0},{2,3},{3,2},{4,5},{5,4},{6,7},{7,6},{8,9},{9,8},{10,11... | collective-permute-start | bytes 589832 | tf_op jit(solution)/shard_map/ppermute | solution.py:486
  64.8 2.7 %collective-permute-start.25 = (bf16[96,1024]{1,0:T(8,128)(2,1)S(1)}, bf16[96,1024]{1,0:T(8,128)(2,1)S(1)}, u32[]{:S(2)}, u32[]{:S(2)}) collective-permute-start(bf16[96,1024]{1,0:T(8,128)(2,1)S(1)} %shard_map.128.refs_2_), channel_id=1, source_target_pairs={{0,1},{1,0},{2,3},{3,2},{4,5},{5,4},{6,7},{7,6},{8,9},{9,8},{10,11... | collective-permute-start | bytes 589832 | tf_op jit(solution)/shard_map/ppermute | solution.py:486
  66.2 7.8 %collective-permute-start.28 = (bf16[96,1024]{1,0:T(8,128)(2,1)S(1)}, bf16[96,1024]{1,0:T(8,128)(2,1)S(1)}, u32[]{:S(2)}, u32[]{:S(2)}) collective-permute-start(bf16[96,1024]{1,0:T(8,128)(2,1)S(1)} %shard_map.130.refs_3_.refs_0_), channel_id=1, source_target_pairs={{0,2},{1,3},{2,0},{3,1},{4,6},{5,7},{6,4},{7,5},{8,10},{9,11},{10,... | collective-permute-start | bytes 589832 | tf_op jit(solution)/shard_map/ppermute | solution.py:490
  68.4 8.9 %collective-permute-start.27 = (bf16[96,1024]{1,0:T(8,128)(2,1)S(1)}, bf16[96,1024]{1,0:T(8,128)(2,1)S(1)}, u32[]{:S(2)}, u32[]{:S(2)}) collective-permute-start(bf16[96,1024]{1,0:T(8,128)(2,1)S(1)} %shard_map.131.refs_9_.refs_0_), channel_id=1, source_target_pairs={{0,2},{1,3},{2,0},{3,1},{4,6},{5,7},{6,4},{7,5},{8,10},{9,11},{10,... | collective-permute-start | bytes 589832 | tf_op jit(solution)/shard_map/ppermute | solution.py:490
  74.1 3.8 %collective-permute-start.32 = (bf16[2,32,1024]{2,1,0:T(8,128)(2,1)S(1)}, bf16[2,32,1024]{2,1,0:T(8,128)(2,1)S(1)}, u32[]{:S(2)}, u32[]{:S(2)}) collective-permute-start(bf16[2,32,1024]{2,1,0:T(8,128)(2,1)S(1)} %get-tuple-element.116.refs_1_.refs_4_), channel_id=1, source_target_pairs={{0,1},{1,0},{2,3},{3,2},{4,5},{5,4},{6,7},{7,6},{8,9},{9,8},{10,11... | collective-permute-start | bytes 393224 | tf_op jit(solution)/shard_map/ppermute | solution.py:486
  74.2 4.1 %collective-permute-start.33 = (bf16[2,32,1024]{2,1,0:T(8,128)(2,1)S(1)}, bf16[2,32,1024]{2,1,0:T(8,128)(2,1)S(1)}, u32[]{:S(2)}, u32[]{:S(2)}) collective-permute-start(bf16[2,32,1024]{2,1,0:T(8,128)(2,1)S(1)} %get-tuple-element.117.refs_2_), channel_id=1, source_target_pairs={{0,1},{1,0},{2,3},{3,2},{4,5},{5,4},{6,7},{7,6},{8,9},{9,8},{10,11... | collective-permute-start | bytes 393224 | tf_op jit(solution)/shard_map/ppermute | solution.py:486
  74.7 3.6 %collective-permute-start.34 = (bf16[2,32,1024]{2,1,0:T(8,128)(2,1)S(1)}, bf16[2,32,1024]{2,1,0:T(8,128)(2,1)S(1)}, u32[]{:S(2)}, u32[]{:S(2)}) collective-permute-start(bf16[2,32,1024]{2,1,0:T(8,128)(2,1)S(1)} %get-tuple-element.118.refs_3_), channel_id=1, source_target_pairs={{0,1},{1,0},{2,3},{3,2},{4,5},{5,4},{6,7},{7,6},{8,9},{9,8},{10,11... | collective-permute-start | bytes 393224 | tf_op jit(solution)/shard_map/ppermute | solution.py:486
  77.4 4.7 %collective-permute-start.29 = (bf16[2,32,1024]{2,1,0:T(8,128)(2,1)S(1)}, bf16[2,32,1024]{2,1,0:T(8,128)(2,1)S(1)}, u32[]{:S(2)}, u32[]{:S(2)}) collective-permute-start(bf16[2,32,1024]{2,1,0:T(8,128)(2,1)S(1)} %get-tuple-element.120.refs_4_.refs_7_), channel_id=1, source_target_pairs={{0,1},{1,0},{2,3},{3,2},{4,5},{5,4},{6,7},{7,6},{8,9},{9,8},{10,11... | collective-permute-start | bytes 393224 | tf_op jit(solution)/shard_map/ppermute | solution.py:486
  77.8 4.3 %collective-permute-start.30 = (bf16[2,32,1024]{2,1,0:T(8,128)(2,1)S(1)}, bf16[2,32,1024]{2,1,0:T(8,128)(2,1)S(1)}, u32[]{:S(2)}, u32[]{:S(2)}) collective-permute-start(bf16[2,32,1024]{2,1,0:T(8,128)(2,1)S(1)} %get-tuple-element.121.refs_5_), channel_id=1, source_target_pairs={{0,1},{1,0},{2,3},{3,2},{4,5},{5,4},{6,7},{7,6},{8,9},{9,8},{10,11... | collective-permute-start | bytes 393224 | tf_op jit(solution)/shard_map/ppermute | solution.py:486
  77.9 4.1 %collective-permute-start.31 = (bf16[2,32,1024]{2,1,0:T(8,128)(2,1)S(1)}, bf16[2,32,1024]{2,1,0:T(8,128)(2,1)S(1)}, u32[]{:S(2)}, u32[]{:S(2)}) collective-permute-start(bf16[2,32,1024]{2,1,0:T(8,128)(2,1)S(1)} %get-tuple-element.122.refs_6_), channel_id=1, source_target_pairs={{0,1},{1,0},{2,3},{3,2},{4,5},{5,4},{6,7},{7,6},{8,9},{9,8},{10,11... | collective-permute-start | bytes 393224 | tf_op jit(solution)/shard_map/ppermute | solution.py:486
  (5 other events, 61.5 us)
